TPU v7x, 128 devices: a whole 4x4x4 slice. The times are simulated.
128 devices in a mesh: gx: 16 (over x, z), gy: 8 (over y, core).
Axes of the slice: x: 4, y: 4, z: 4, core: 2. Of those that a mesh axis runs over, the one named last changes fastest.
Arguments:
- state: float32 [144, 128, 1024], P(None, 'gx', 'gy'), may hold values from -6 to 6
- owner: int32 [128, 1024], P('gx', 'gy'), may hold values from 0 to 127, as said below
- counts: int32 [128, 1024], P('gx', 'gy'), may hold values from 1 to 4
- vert: float32 [72, 72], replicated, may hold values from -0.75 to 0.75
- down_map: float32 [50, 72], replicated, may hold values from -0.75 to 0.75
- up_map: float32 [72, 50], replicated, may hold values from -0.875 to 0.875
- courant: float32 [50], replicated, may hold values from 0.05 to 0.9
- crm_field: float32 [3200, 229376], P(None, ('gx', 'gy')), may hold values from -4 to 4
Outputs:
- new_state: float32 [144, 128, 1024], P(None, 'gx', 'gy')
Inputs may be any that keep to these rules, and one draw needn't show every extreme that they name: In each device's block of 8 x 128 columns no owner is named more than 14 times; one owner is named exactly 14 times in every block.
All inputs are finite; a program needn't handle non-finite values.
Results may differ from a plain program's by a relative error of at most 0.0003.
Values sent between devices are 32-bit elements; how exact they have to be, the bound alone decides.
No kernel may reach another device: no remote copies, remote signals or barrier semaphores. Data moves between devices by JAX's collectives and lax.ppermute only.
A program may use at most 128 MiB of HBM per device.

v0:
```python
import math

import jax
import jax.numpy as jnp
from jax import lax
from jax.sharding import PartitionSpec as P

S_MAX = 4


diffusion_rate = 0.1
condense_rate = 0.5
latent_heat = 1.0
moisture_slope = 0.3


def padded_2(cells, sides, width):
    for axis, dim in sides:
        count = lax.axis_size(axis)
        head = lax.slice_in_dim(cells, 0, width, axis=dim)
        tail = lax.slice_in_dim(cells, cells.shape[dim] - width, cells.shape[dim], axis=dim)
        cells = jnp.concatenate(
            [
                lax.ppermute(tail, axis, [(i, (i + 1) % count) for i in range(count)]),
                cells,
                lax.ppermute(head, axis, [((i + 1) % count, i) for i in range(count)]),
            ],
            axis=dim,
        )
    return cells


def profiles(columns, down_map):
    levels = columns.reshape(2, down_map.shape[1], -1)
    return jnp.einsum("zl,vlb->vzb", down_map, levels, precision=lax.Precision.HIGHEST)


def advance(fields, courant, active):
    shifted = jnp.roll(fields, 1, axis=2)
    moved = fields - courant[None, :, None, None] * (fields - shifted)
    temper = moved[0]
    vapour = moved[1]
    condensed = condense_rate * jnp.maximum(vapour - jnp.exp(moisture_slope * temper), 0.0)
    result = jnp.stack([temper + latent_heat * condensed, vapour - condensed])
    return jnp.where(active[None, None, None, :], result, fields)


def body(state, owner, counts, vert, down_map, up_map, courant, crm_field):
    nlev = vert.shape[0]
    rows = state.shape[0]
    width_x = state.shape[1]
    width_y = state.shape[2]
    col_dev = width_x * width_y
    padded = padded_2(state, (("gx", 1), ("gy", 2)), 1)
    lap = (
        padded[:, 2:, 1:-1]
        + padded[:, :-2, 1:-1]
        + padded[:, 1:-1, 2:]
        + padded[:, 1:-1, :-2]
        - 4.0 * state
    )
    levels = state.reshape(2, nlev, width_x, width_y)
    mixed = jnp.einsum("ij,vjxy->vixy", vert, levels, precision=lax.Precision.HIGHEST)
    dyn = state + diffusion_rate * lap + mixed.reshape(state.shape)
    columns = dyn.reshape(rows, col_dev)
    owners = owner.reshape(col_dev)
    steps_col = counts.reshape(col_dev).astype(jnp.float32)
    across = lax.axis_size("gx")
    along = lax.axis_size("gy")
    devices = across * along
    cap = max(2, 7 * col_dev // (4 * devices))
    slots = devices * cap
    onehot = (owners[:, None] == jnp.arange(devices, dtype=jnp.int32)[None, :]).astype(jnp.int32)
    ranks = jnp.sum(jnp.cumsum(onehot, axis=0) * onehot, axis=1) - 1
    slot_of = owners * cap + ranks
    outgoing = jnp.zeros((rows, slots), jnp.float32).at[:, slot_of].set(columns)
    out_steps = jnp.zeros((1, slots), jnp.float32).at[0, slot_of].set(steps_col)
    arrived, arrived_steps = (
        lax.all_to_all(outgoing, ("gx", "gy"), split_axis=1, concat_axis=1, tiled=True),
        lax.all_to_all(out_steps, ("gx", "gy"), split_axis=1, concat_axis=1, tiled=True),
    )
    crm_z = down_map.shape[0]
    field_rows = crm_field.shape[0]
    crm_x = field_rows // (2 * crm_z)
    block = math.gcd(slots, 128)
    blocks = slots // block

    def crm_block(index, tend_slots):
        start = index * block
        block_cols = lax.dynamic_slice_in_dim(arrived, start, block, 1)
        block_steps = lax.dynamic_slice_in_dim(arrived_steps, start, block, 1)[0]
        block_field = lax.dynamic_slice_in_dim(crm_field, start, block, 1)
        prof = profiles(block_cols, down_map)
        init = prof[:, :, None, :] + block_field.reshape(2, crm_z, crm_x, block)

        def turn(step, fields):
            return advance(fields, courant, step.astype(jnp.float32) < block_steps)

        final = lax.fori_loop(0, S_MAX, turn, init)
        change = jnp.mean(final - init, axis=2)
        out = jnp.einsum("lz,vzb->vlb", up_map, change, precision=lax.Precision.HIGHEST)
        return lax.dynamic_update_slice_in_dim(tend_slots, out.reshape(rows, block), start, 1)

    tend_slots = lax.fori_loop(0, blocks, crm_block, jnp.zeros((rows, slots), jnp.float32))
    returned = lax.all_to_all(tend_slots, ("gx", "gy"), split_axis=1, concat_axis=1, tiled=True)
    tend = returned[:, slot_of].reshape(rows, width_x, width_y)
    return dyn + tend


def solution(mesh):
    in_specs = (
        P(None, "gx", "gy"),
        P("gx", "gy"),
        P("gx", "gy"),
        P(),
        P(),
        P(),
        P(),
        P(None, ("gx", "gy")),
    )
    out_specs = P(None, "gx", "gy")
    return jax.shard_map(body, mesh=mesh, in_specs=in_specs, out_specs=out_specs, check_vma=False)
```

profile of v0, /device:TPU:1, one launch (start us, length us, event | category | flops | bytes accessed | tf_op | source)
XLA Modules:
  0.0 260.7 jit_solution(699279371907681527)
XLA Ops:
  0.0 1.4 fusion.30
  1.4 2.5 collective-permute-start.1
  3.9 4.4 %collective-permute-start = (f32[144,1,128]{2,1,0:T(1,128)S(1)}, f32[144,1,128]{2,1,0:T(1,128)S(1)}, u32[]{:S(2)}, u32[]{:S(2)}) collective-permute-start(f32[144,1,128]{2,1,0:T(1,128)S(1)} %get-tuple-element.289), channel_id=1, source_target_pairs={{8,0},{16,8},{24,16},{32,24},{40,32},{48,40},{56,48},{64,56},{72,6... | collective-permute-start | bytes 221192 | tf_op jit(solution)/shard_map/ppermute | solution.py:26
  10.9 4.3 %scatter_custom_fusion.1 = f32[1792]{0:T(1024)S(1)} fusion(s32[1024]{0:T(1024)S(1)} %broadcast_select_fusion, f32[1024]{0:T(1024)S(1)} %convert_bitcast_fusion, f32[]{:T(128)} %constant.87.clone.1), kind=kCustom, calls=%fused_computation.59 | custom fusion | bytes 7172
  16.0 6.7 %all-to-all-start.1 = ((f32[1,128,14]{2,0,1:T(1,128)}), f32[1,128,14]{2,0,1:T(1,128)S(1)}, u32[]{:S(2)}, u32[]{:S(2)}) async-start(f32[1,128,14]{2,0,1:T(1,128)} %bitcast.23), calls=%async_computation.1 | async-start | bytes 131072 | tf_op jit(solution)/shard_map/all_to_all | solution.py:80
  24.2 1.6 collective-permute-start.3
  26.7 2.5 collective-permute-done.2
  29.9 1.5 copy.28
  31.4 2.1 fusion.17
  34.4 6.1 %scatter_custom_fusion = f32[144,1792]{0,1:T(8,128)} fusion(s32[1024]{0:T(1024)S(1)} %bitcast.93, f32[1024,144]{1,0:T(8,128)S(1)} %bitcast.92, f32[]{:T(128)} %constant.87.clone.1), kind=kCustom, calls=%fused_computation.27 | custom fusion | bytes 1032196 | tf_op jit(solution)/shard_map/scatter | solution.py:76
  40.5 1.6 all_to_all.24
  42.0 3.8 %reshape.146 = f32[128,1,2016]{2,1,0:T(1,128)} reshape(f32[128,14,144]{2,1,0:T(8,128)S(1)} %bitcast.84) | data formatting | bytes 2064384
  45.9 8.9 %all-to-all-start = ((f32[128,1,2016]{2,1,0:T(1,128)}), f32[128,1,2016]{2,1,0:T(1,128)S(1)}, u32[]{:S(2)}, u32[]{:S(2)}) async-start(f32[128,1,2016]{2,1,0:T(1,128)} %reshape.146), calls=%async_computation | async-start | bytes 2097152 | tf_op jit(solution)/shard_map/all_to_all | solution.py:79
  56.4 17.5 %all-to-all-done = f32[128,1,2016]{2,1,0:T(1,128)S(1)} async-done(((f32[128,1,2016]{2,1,0:T(1,128)}), f32[128,1,2016]{2,1,0:T(1,128)S(1)}, u32[]{:S(2)}, u32[]{:S(2)}) %all-to-all-start) | async-done | bytes 1032224 | tf_op jit(solution)/shard_map/all_to_all | solution.py:79
  74.4 3.2 %reduce.8 = f32[128,2016]{1,0:T(8,128)S(1)} reduce(f32[128,1,2016]{2,1,0:T(1,128)S(1)} %all-to-all-done, f32[]{:T(128)} %broadcast.152), dimensions={1}, to_apply=%all_to_all.25.reduce_sub_computation | reduce | bytes 2064388 | tf_op jit(solution)/shard_map/all_to_all | solution.py:79
  77.7 1.4 reshape.147
  79.1 1.5 all_to_all.26
  80.6 3.0 %copy.36 = f32[144,1792]{1,0:T(8,128)} copy(f32[144,1792]{0,1:T(8,128)} %all_to_all.26) | data formatting | bytes 2064384 | tf_op jit(solution)/shard_map/while | solution.py:104
  83.6 1.0 broadcast.107.clone
  84.6 130.8 %while.39 = (s32[]{:T(128)}, f32[144,1792]{1,0:T(8,128)}, f32[144,1792]{1,0:T(8,128)}, f32[50,72]{1,0:T(8,128)S(1)}, f32[3200,1792]{1,0:T(8,128)}, /*index=5*/f3...) while((s32[]{:T(128)}, f32[144,1792]{1,0:T(8,128)}, ...), condition=%wide.region_9.10_spmd, body=%wide.region_5.0_spmd.sunk | while | flops 27443336 | bytes 23769476 | solution.py:104
  84.6 0.9 constant_dynamic-slice_fusion.6
  85.7 1.5 constant_dynamic-slice_fusion.5
  87.6 4.8 %while.40 = (s32[]{:T(128)}, f32[2,50,32,128]{3,2,1,0:T(8,128)S(1)}, f32[128]{0:T(128)S(1)}, f32[50]{0:T(128)S(1)}, s32[]{:T(128)}) while((s32[]{:T(128)}, f32[2,50,32,128]{3,2,1,0:T(8,128)S(1)}, f32[128]{0:T(128)S(1)}, f32[50]{0:T(128)S(1)}, s32[]{:T(128)}) %tuple.64), condition=%wide.region_7.7_spmd, body=%wide.region_6.6_spmd.sunk | while | flops 3686531 | bytes 13210641 | solution.py:99
  94.0 0.9 constant_dynamic-slice_fusion.6
  95.1 1.5 constant_dynamic-slice_fusion.5
  96.9 4.8 %while.40 = (s32[]{:T(128)}, f32[2,50,32,128]{3,2,1,0:T(8,128)S(1)}, f32[128]{0:T(128)S(1)}, f32[50]{0:T(128)S(1)}, s32[]{:T(128)}) while((s32[]{:T(128)}, f32[2,50,32,128]{3,2,1,0:T(8,128)S(1)}, f32[128]{0:T(128)S(1)}, f32[50]{0:T(128)S(1)}, s32[]{:T(128)}) %tuple.64), condition=%wide.region_7.7_spmd, body=%wide.region_6.6_spmd.sunk | while | flops 3686531 | bytes 13210641 | solution.py:99
  103.3 0.9 constant_dynamic-slice_fusion.6
  104.4 1.5 constant_dynamic-slice_fusion.5
  106.2 4.8 %while.40 = (s32[]{:T(128)}, f32[2,50,32,128]{3,2,1,0:T(8,128)S(1)}, f32[128]{0:T(128)S(1)}, f32[50]{0:T(128)S(1)}, s32[]{:T(128)}) while((s32[]{:T(128)}, f32[2,50,32,128]{3,2,1,0:T(8,128)S(1)}, f32[128]{0:T(128)S(1)}, f32[50]{0:T(128)S(1)}, s32[]{:T(128)}) %tuple.64), condition=%wide.region_7.7_spmd, body=%wide.region_6.6_spmd.sunk | while | flops 3686531 | bytes 13210641 | solution.py:99
  112.6 0.9 constant_dynamic-slice_fusion.6
  113.7 1.5 constant_dynamic-slice_fusion.5
  115.6 4.8 %while.40 = (s32[]{:T(128)}, f32[2,50,32,128]{3,2,1,0:T(8,128)S(1)}, f32[128]{0:T(128)S(1)}, f32[50]{0:T(128)S(1)}, s32[]{:T(128)}) while((s32[]{:T(128)}, f32[2,50,32,128]{3,2,1,0:T(8,128)S(1)}, f32[128]{0:T(128)S(1)}, f32[50]{0:T(128)S(1)}, s32[]{:T(128)}) %tuple.64), condition=%wide.region_7.7_spmd, body=%wide.region_6.6_spmd.sunk | while | flops 3686531 | bytes 13210641 | solution.py:99
  122.0 0.9 constant_dynamic-slice_fusion.6
  123.1 1.5 constant_dynamic-slice_fusion.5
  124.9 4.8 %while.40 = (s32[]{:T(128)}, f32[2,50,32,128]{3,2,1,0:T(8,128)S(1)}, f32[128]{0:T(128)S(1)}, f32[50]{0:T(128)S(1)}, s32[]{:T(128)}) while((s32[]{:T(128)}, f32[2,50,32,128]{3,2,1,0:T(8,128)S(1)}, f32[128]{0:T(128)S(1)}, f32[50]{0:T(128)S(1)}, s32[]{:T(128)}) %tuple.64), condition=%wide.region_7.7_spmd, body=%wide.region_6.6_spmd.sunk | while | flops 3686531 | bytes 13210641 | solution.py:99
  131.3 0.9 constant_dynamic-slice_fusion.6
  132.4 1.5 constant_dynamic-slice_fusion.5
  134.2 4.8 %while.40 = (s32[]{:T(128)}, f32[2,50,32,128]{3,2,1,0:T(8,128)S(1)}, f32[128]{0:T(128)S(1)}, f32[50]{0:T(128)S(1)}, s32[]{:T(128)}) while((s32[]{:T(128)}, f32[2,50,32,128]{3,2,1,0:T(8,128)S(1)}, f32[128]{0:T(128)S(1)}, f32[50]{0:T(128)S(1)}, s32[]{:T(128)}) %tuple.64), condition=%wide.region_7.7_spmd, body=%wide.region_6.6_spmd.sunk | while | flops 3686531 | bytes 13210641 | solution.py:99
  140.6 0.9 constant_dynamic-slice_fusion.6
  141.7 1.5 constant_dynamic-slice_fusion.5
  143.6 4.8 %while.40 = (s32[]{:T(128)}, f32[2,50,32,128]{3,2,1,0:T(8,128)S(1)}, f32[128]{0:T(128)S(1)}, f32[50]{0:T(128)S(1)}, s32[]{:T(128)}) while((s32[]{:T(128)}, f32[2,50,32,128]{3,2,1,0:T(8,128)S(1)}, f32[128]{0:T(128)S(1)}, f32[50]{0:T(128)S(1)}, s32[]{:T(128)}) %tuple.64), condition=%wide.region_7.7_spmd, body=%wide.region_6.6_spmd.sunk | while | flops 3686531 | bytes 13210641 | solution.py:99
  151.1 1.5 constant_dynamic-slice_fusion.5
  152.9 4.8 %while.40 = (s32[]{:T(128)}, f32[2,50,32,128]{3,2,1,0:T(8,128)S(1)}, f32[128]{0:T(128)S(1)}, f32[50]{0:T(128)S(1)}, s32[]{:T(128)}) while((s32[]{:T(128)}, f32[2,50,32,128]{3,2,1,0:T(8,128)S(1)}, f32[128]{0:T(128)S(1)}, f32[50]{0:T(128)S(1)}, s32[]{:T(128)}) %tuple.64), condition=%wide.region_7.7_spmd, body=%wide.region_6.6_spmd.sunk | while | flops 3686531 | bytes 13210641 | solution.py:99
  160.4 1.5 constant_dynamic-slice_fusion.5
  162.2 4.8 %while.40 = (s32[]{:T(128)}, f32[2,50,32,128]{3,2,1,0:T(8,128)S(1)}, f32[128]{0:T(128)S(1)}, f32[50]{0:T(128)S(1)}, s32[]{:T(128)}) while((s32[]{:T(128)}, f32[2,50,32,128]{3,2,1,0:T(8,128)S(1)}, f32[128]{0:T(128)S(1)}, f32[50]{0:T(128)S(1)}, s32[]{:T(128)}) %tuple.64), condition=%wide.region_7.7_spmd, body=%wide.region_6.6_spmd.sunk | while | flops 3686531 | bytes 13210641 | solution.py:99
  169.7 1.5 constant_dynamic-slice_fusion.5
  171.6 4.8 %while.40 = (s32[]{:T(128)}, f32[2,50,32,128]{3,2,1,0:T(8,128)S(1)}, f32[128]{0:T(128)S(1)}, f32[50]{0:T(128)S(1)}, s32[]{:T(128)}) while((s32[]{:T(128)}, f32[2,50,32,128]{3,2,1,0:T(8,128)S(1)}, f32[128]{0:T(128)S(1)}, f32[50]{0:T(128)S(1)}, s32[]{:T(128)}) %tuple.64), condition=%wide.region_7.7_spmd, body=%wide.region_6.6_spmd.sunk | while | flops 3686531 | bytes 13210641 | solution.py:99
  179.1 1.5 constant_dynamic-slice_fusion.5
  180.9 4.8 %while.40 = (s32[]{:T(128)}, f32[2,50,32,128]{3,2,1,0:T(8,128)S(1)}, f32[128]{0:T(128)S(1)}, f32[50]{0:T(128)S(1)}, s32[]{:T(128)}) while((s32[]{:T(128)}, f32[2,50,32,128]{3,2,1,0:T(8,128)S(1)}, f32[128]{0:T(128)S(1)}, f32[50]{0:T(128)S(1)}, s32[]{:T(128)}) %tuple.64), condition=%wide.region_7.7_spmd, body=%wide.region_6.6_spmd.sunk | while | flops 3686531 | bytes 13210641 | solution.py:99
  188.4 1.5 constant_dynamic-slice_fusion.5
  190.3 4.8 %while.40 = (s32[]{:T(128)}, f32[2,50,32,128]{3,2,1,0:T(8,128)S(1)}, f32[128]{0:T(128)S(1)}, f32[50]{0:T(128)S(1)}, s32[]{:T(128)}) while((s32[]{:T(128)}, f32[2,50,32,128]{3,2,1,0:T(8,128)S(1)}, f32[128]{0:T(128)S(1)}, f32[50]{0:T(128)S(1)}, s32[]{:T(128)}) %tuple.64), condition=%wide.region_7.7_spmd, body=%wide.region_6.6_spmd.sunk | while | flops 3686531 | bytes 13210641 | solution.py:99
  197.8 1.5 constant_dynamic-slice_fusion.5
  199.6 4.8 %while.40 = (s32[]{:T(128)}, f32[2,50,32,128]{3,2,1,0:T(8,128)S(1)}, f32[128]{0:T(128)S(1)}, f32[50]{0:T(128)S(1)}, s32[]{:T(128)}) while((s32[]{:T(128)}, f32[2,50,32,128]{3,2,1,0:T(8,128)S(1)}, f32[128]{0:T(128)S(1)}, f32[50]{0:T(128)S(1)}, s32[]{:T(128)}) %tuple.64), condition=%wide.region_7.7_spmd, body=%wide.region_6.6_spmd.sunk | while | flops 3686531 | bytes 13210641 | solution.py:99
  207.1 1.5 constant_dynamic-slice_fusion.5
  209.0 4.8 %while.40 = (s32[]{:T(128)}, f32[2,50,32,128]{3,2,1,0:T(8,128)S(1)}, f32[128]{0:T(128)S(1)}, f32[50]{0:T(128)S(1)}, s32[]{:T(128)}) while((s32[]{:T(128)}, f32[2,50,32,128]{3,2,1,0:T(8,128)S(1)}, f32[128]{0:T(128)S(1)}, f32[50]{0:T(128)S(1)}, s32[]{:T(128)}) %tuple.64), condition=%wide.region_7.7_spmd, body=%wide.region_6.6_spmd.sunk | while | flops 3686531 | bytes 13210641 | solution.py:99
  215.4 3.0 %copy.37 = f32[144,1792]{0,1:T(8,128)} copy(f32[144,1792]{1,0:T(8,128)} %get-tuple-element.436) | data formatting | bytes 2064384 | tf_op jit(solution)/shard_map/while | solution.py:104
  218.4 1.6 all_to_all.30
  220.0 3.8 %reshape.148 = f32[128,1,2016]{2,1,0:T(1,128)} reshape(f32[128,14,144]{2,1,0:T(8,128)S(1)} %bitcast.86) | data formatting | bytes 2064384
  223.8 4.7 %all-to-all-start.2 = ((f32[128,1,2016]{2,1,0:T(1,128)}), f32[128,1,2016]{2,1,0:T(1,128)S(1)}, u32[]{:S(2)}, u32[]{:S(2)}) async-start(f32[128,1,2016]{2,1,0:T(1,128)} %reshape.148), calls=%async_computation.2 | async-start | bytes 2097152 | tf_op jit(solution)/shard_map/all_to_all | solution.py:105
  228.6 19.1 %all-to-all-done.2 = f32[128,1,2016]{2,1,0:T(1,128)S(1)} async-done(((f32[128,1,2016]{2,1,0:T(1,128)}), f32[128,1,2016]{2,1,0:T(1,128)S(1)}, u32[]{:S(2)}, u32[]{:S(2)}) %all-to-all-start.2) | async-done | bytes 1032224 | tf_op jit(solution)/shard_map/all_to_all | solution.py:105
  247.6 3.2 %reduce.9 = f32[128,2016]{1,0:T(8,128)S(1)} reduce(f32[128,1,2016]{2,1,0:T(1,128)S(1)} %all-to-all-done.2, f32[]{:T(128)} %broadcast.152), dimensions={1}, to_apply=%all_to_all.31.reduce_sub_computation | reduce | bytes 2064388 | tf_op jit(solution)/shard_map/all_to_all | solution.py:105
  250.9 2.8 %reshape.149 = f32[128,14,144]{2,1,0:T(8,128)} reshape(f32[128,2016]{1,0:T(8,128)S(1)} %reduce.9) | data formatting | bytes 2064384
  253.6 1.6 all_to_all.32
  255.3 3.5 %gather_fusion = f32[1024,144]{1,0:T(8,128)S(1)} fusion(f32[144,1792]{0,1:T(8,128)S(1)} %all_to_all.32, s32[1024]{0:T(1024)S(1)} %broadcast_clamp_fusion), kind=kCustom, calls=%fused_computation | custom fusion | bytes 1183744 | tf_op jit(solution)/shard_map/gather | solution.py:106
  (431 shorter events, 110.8 us)
Async XLA Ops:
  0.0 25.9 %copy-start = (f32[72,72]{1,0:T(8,128)S(1)}, f32[72,72]{1,0:T(8,128)}, u32[]{:S(2)}) copy-start(f32[72,72]{1,0:T(8,128)} %param.15) | copy-start | bytes 62212
  0.0 10.3 %copy-start.8 = (s32[8,128]{1,0:T(8,128)S(1)}, s32[8,128]{1,0:T(8,128)}, u32[]{:S(2)}) copy-start(s32[8,128]{1,0:T(8,128)} %param.13) | copy-start | bytes 12292
  1.4 21.2 %collective-permute-start.1 = (f32[144,1,128]{2,1,0:T(1,128)S(1)}, f32[144,1,128]{2,1,0:T(1,128)S(1)}, u32[]{:S(2)}, u32[]{:S(2)}) collective-permute-start(f32[144,1,128]{2,1,0:T(1,128)S(1)} %get-tuple-element.288), channel_id=1, source_target_pairs={{0,8},{8,16},{16,24},{24,32},{32,40},{40,48},{48,56},{56,64},{64,7... | collective-permute-start | bytes 221192 | tf_op jit(solution)/shard_map/ppermute | solution.py:24
  3.9 18.7 %collective-permute-start = (f32[144,1,128]{2,1,0:T(1,128)S(1)}, f32[144,1,128]{2,1,0:T(1,128)S(1)}, u32[]{:S(2)}, u32[]{:S(2)}) collective-permute-start(f32[144,1,128]{2,1,0:T(1,128)S(1)} %get-tuple-element.289), channel_id=1, source_target_pairs={{8,0},{16,8},{24,16},{32,24},{40,32},{48,40},{56,48},{64,56},{72,6... | collective-permute-start | bytes 221192 | tf_op jit(solution)/shard_map/ppermute | solution.py:26
  9.8 0.9 copy-start.11
  9.8 1.0 copy-start.10
  9.8 1.0 copy-start.9
  9.8 12.8 %copy-start.2 = (f32[144,8,128]{2,1,0:T(8,128)S(1)}, f32[144,8,128]{2,1,0:T(8,128)}, u32[]{:S(2)}) copy-start(f32[144,8,128]{2,1,0:T(8,128)} %param.12) | copy-start | bytes 1769476
  16.0 29.9 %all-to-all-start.1 = ((f32[1,128,14]{2,0,1:T(1,128)}), f32[1,128,14]{2,0,1:T(1,128)S(1)}, u32[]{:S(2)}, u32[]{:S(2)}) async-start(f32[1,128,14]{2,0,1:T(1,128)} %bitcast.23), calls=%async_computation.1 | async-start | bytes 131072 | tf_op jit(solution)/shard_map/all_to_all | solution.py:80
  24.2 5.7 %collective-permute-start.3 = (f32[144,10,1]{0,2,1:T(1,128)S(1)}, f32[144,10,1]{0,2,1:T(1,128)S(1)}, u32[]{:S(2)}, u32[]{:S(2)}) collective-permute-start(f32[144,10,1]{0,2,1:T(1,128)S(1)} %copy.27), channel_id=1, source_target_pairs={{0,1},{1,2},{2,3},{3,4},{4,5},{5,6},{6,7},{7,0},{8,9},{9,10},{10,1... | collective-permute-start | bytes 17288 | tf_op jit(solution)/shard_map/ppermute | solution.py:24
  25.9 3.4 %collective-permute-start.2 = (f32[144,10,1]{0,2,1:T(1,128)S(1)}, f32[144,10,1]{0,2,1:T(1,128)S(1)}, u32[]{:S(2)}, u32[]{:S(2)}) collective-permute-start(f32[144,10,1]{0,2,1:T(1,128)S(1)} %copy.25), channel_id=1, source_target_pairs={{1,0},{2,1},{3,2},{4,3},{5,4},{6,5},{7,6},{0,7},{9,8},{10,9},{11,1... | collective-permute-start | bytes 17288 | tf_op jit(solution)/shard_map/ppermute | solution.py:26
  33.5 0.8 copy-start.3
  45.9 28.0 %all-to-all-start = ((f32[128,1,2016]{2,1,0:T(1,128)}), f32[128,1,2016]{2,1,0:T(1,128)S(1)}, u32[]{:S(2)}, u32[]{:S(2)}) async-start(f32[128,1,2016]{2,1,0:T(1,128)} %reshape.146), calls=%async_computation | async-start | bytes 2097152 | tf_op jit(solution)/shard_map/all_to_all | solution.py:79
  80.6 4.0 %copy-start.5 = (f32[50,72]{1,0:T(8,128)S(1)}, f32[50,72]{1,0:T(8,128)}, u32[]{:S(2)}) copy-start(f32[50,72]{1,0:T(8,128)} %param.16) | copy-start | bytes 43204
  80.6 4.0 %copy-start.6 = (f32[72,50]{0,1:T(8,128)S(1)}, f32[72,50]{0,1:T(8,128)}, u32[]{:S(2)}) copy-start(f32[72,50]{0,1:T(8,128)} %param.17) | copy-start | bytes 43204
  80.6 4.0 %copy-start.7 = (f32[50]{0:T(128)S(1)}, f32[50]{0:T(128)}, u32[]{:S(2)}) copy-start(f32[50]{0:T(128)} %param.18) | copy-start | bytes 604
  223.8 23.8 %all-to-all-start.2 = ((f32[128,1,2016]{2,1,0:T(1,128)}), f32[128,1,2016]{2,1,0:T(1,128)S(1)}, u32[]{:S(2)}, u32[]{:S(2)}) async-start(f32[128,1,2016]{2,1,0:T(1,128)} %reshape.148), calls=%async_computation.2 | async-start | bytes 2097152 | tf_op jit(solution)/shard_map/all_to_all | solution.py:105
  258.8 1.1 copy-start.4
  258.8 1.9 copy-start.1
where the time goes:
time: 262 us; the launch traced here: 261 us
  local copies, waits for them, and re-layouts  95.3 us (36%)
  other arithmetic  86.8 us (33%)
  waiting for transfers between devices  39.1 us (15%)
  starting transfers between devices  28.8 us (11%)
  matrix products  7.07 us (3%)
  loops' own time  3.28 us (1%)
    select_n x56, other arithmetic, advance(): return jnp.where(active[None, None, None, :], result, fields)  25.7 us
    dynamic_slice x14, local copies, waits for them, and re-layouts, crm_block(): block_field = lax.dynamic_slice_in_dim(crm_field, start, block, 1)  21.6 us
    all_to_all x1, waiting for transfers between devices, body(): lax.all_to_all(tend_slots, ('gx', 'gy'), split_axis=1, concat_axis=1, til...  19.1 us
    sub x56, other arithmetic, advance(): moved = fields - courant[None, :, None, None] * (fields - shifted)  18.9 us
    unnamed x30, local copies, waits for them, and re-layouts  18.2 us
    all_to_all x1, waiting for transfers between devices, body(): lax.all_to_all(outgoing, ('gx', 'gy'), split_axis=1, concat_axis=1, tiled...  17.5 us
    add x56, other arithmetic, advance(): result = jnp.stack([temper + latent_heat * condensed, vapour - condensed])  16.2 us
    dynamic_slice x14, local copies, waits for them, and re-layouts, crm_block(): block_cols = lax.dynamic_slice_in_dim(arrived, start, block, 1)  12.5 us
  transfers between devices with their start and end apart: 7, of which 3 were waited for; matrix products, arithmetic and copies ran while one was open for 10% of the time, Pallas kernels for 0%

commit v1 on v0

v1 whole, which is shorter than its diff:
```python
import functools
import math

import jax
import jax.numpy as jnp
from jax import lax
from jax.experimental import pallas as pl
from jax.experimental.pallas import tpu as pltpu
from jax.sharding import PartitionSpec as P

S_MAX = 4
DIFFUSION = 0.1
CONDENSE = 0.5
SLOPE = 0.3
LANES = 128
BETA = SLOPE * math.log2(math.e)
SHIFT = math.log2(BETA)

NT = (((1,), (1,)), ((), ()))
NN = (((1,), (0,)), ((), ()))
TN = (((0,), (0,)), ((), ()))


def split(value):
    high = value.astype(jnp.bfloat16)
    low = (value - high.astype(jnp.float32)).astype(jnp.bfloat16)
    return high, low


def dot(a, b, dims=NN):
    return lax.dot_general(a, b, dims, preferred_element_type=jnp.float32)


def dot3(a, b):
    a_hi, a_lo = split(a)
    b_hi, b_lo = split(b)
    return dot(a_hi, b_hi) + (dot(a_hi, b_lo) + dot(a_lo, b_hi))


def edges_kernel(state_ref, top_ref, bottom_ref, side_ref):
    levels = top_ref.shape[0]
    top_ref[...] = state_ref[pl.ds(0, levels, stride=8), :]
    bottom_ref[...] = state_ref[pl.ds(7, levels, stride=8), :]
    row = lax.broadcasted_iota(jnp.int32, (8, LANES), 0)
    lane = lax.broadcasted_iota(jnp.int32, (8, LANES), 1)
    pick = ((row == 0) & (lane == 0)) | ((row == 1) & (lane == LANES - 1))
    pick = pick.astype(jnp.bfloat16)
    data = state_ref[...]
    hi = data.astype(jnp.bfloat16)
    rest = data - hi.astype(jnp.float32)
    mid = rest.astype(jnp.bfloat16)
    low = (rest - mid.astype(jnp.float32)).astype(jnp.bfloat16)
    side_ref[...] = (dot(pick, hi, NT) + dot(pick, mid, NT)) + dot(pick, low, NT)


def columns_kernel(
    cap, state_ref, above_ref, below_ref, left_ref, right_ref, owner_ref, counts_ref,
    vert_ref, down_ref, dyn_ref, slot_ref, out_ref,
):
    levels = above_ref.shape[0]
    half = levels // 2
    crm_z = down_ref.shape[0]
    pad_z = -(-crm_z // 8) * 8
    lane = lax.broadcasted_iota(jnp.int32, (8, LANES), 1)
    row = lax.broadcasted_iota(jnp.int32, (8, LANES), 0)
    sides = jnp.concatenate([left_ref[...], right_ref[...], jnp.zeros((6, 8 * levels), jnp.float32)], axis=0)
    place = ((row == 0) & (lane == 0)) | ((row == 1) & (lane == LANES - 1))
    place = place.astype(jnp.bfloat16)
    s_hi, s_lo = split(sides)
    dyn_ref[...] = dot(s_hi, place, TN) + dot(s_lo, place, TN)
    wide = lax.broadcasted_iota(jnp.int32, (levels, LANES), 1)
    rows = [state_ref[pl.ds(i, levels, stride=8), :] for i in range(8)]
    laps = []
    for i in range(8):
        mid = rows[i]
        up = rows[i - 1] if i > 0 else above_ref[...]
        dn = rows[i + 1] if i < 7 else below_ref[...]
        west = jnp.where(wide == 0, 0.0, pltpu.roll(mid, 1, 1))
        east = jnp.where(wide == LANES - 1, 0.0, pltpu.roll(mid, LANES - 1, 1))
        halo = dyn_ref[pl.ds(i, levels, stride=8), :]
        lap = (up + dn + (west + east + halo)) - 4.0 * mid
        laps.append(mid + DIFFUSION * lap)
    whole = jnp.concatenate(rows, axis=1)
    base = jnp.concatenate(laps, axis=1)
    vert = vert_ref[...]
    temper = base[:half] + dot3(vert, whole[:half])
    vapour = base[half:] + dot3(vert, whole[half:])
    down = jnp.concatenate([down_ref[...], jnp.zeros((pad_z - crm_z, half), jnp.float32)], axis=0)
    prof_t = dot3(down, temper)
    prof_q = dot3(down, vapour)
    for i in range(8):
        cols = slice(i * LANES, (i + 1) * LANES)
        dyn_ref[pl.ds(i, half, stride=8), :] = temper[:, cols]
        dyn_ref[pl.ds(8 * half + i, half, stride=8), :] = vapour[:, cols]

    owner = jnp.concatenate([owner_ref[i:i + 1, :] for i in range(8)], axis=1)
    counts = jnp.concatenate([counts_ref[i:i + 1, :] for i in range(8)], axis=1)
    width = owner.shape[1]
    devices = out_ref.shape[0] // cap
    which = lax.broadcasted_iota(jnp.int32, (devices, width), 0)
    mine = which == owner
    earlier = (
        lax.broadcasted_iota(jnp.int32, (width, width), 0)
        < lax.broadcasted_iota(jnp.int32, (width, width), 1)
    ).astype(jnp.bfloat16)
    before = dot(mine.astype(jnp.bfloat16), earlier)
    rank = jnp.sum(jnp.where(mine, before, 0.0), axis=0, keepdims=True).astype(jnp.int32)
    slot = owner * cap + rank
    slot_ref[...] = slot

    lead = (lax.broadcasted_iota(jnp.int32, (8, width), 0) == 0).astype(jnp.float32)
    steps = lead * counts.astype(jnp.float32)
    blank = jnp.zeros((LANES - 2 * pad_z - 8, width), jnp.float32)
    payload = jnp.concatenate([prof_t, prof_q, steps, blank], axis=0)
    p_hi, p_lo = split(payload)
    both = jnp.concatenate([p_hi, p_lo], axis=0)
    chunk = 256
    for start in range(0, out_ref.shape[0], chunk):
        ids = start + lax.broadcasted_iota(jnp.int32, (chunk, width), 0)
        pick = (ids == slot).astype(jnp.bfloat16)
        sent = dot(pick, both, NT)
        out_ref[start:start + chunk, :] = sent[:, :LANES] + sent[:, LANES:]


def crm_kernel(crm_z, crm_x, courant_ref, arrived_ref, field_ref, out_ref, prof_ref, part_ref, turn_ref):
    pad_z = -(-crm_z // 8) * 8
    quads = crm_x // 8
    cols = arrived_ref[...].T
    prof_t = cols[:pad_z]
    prof_q = cols[pad_z:2 * pad_z]
    counts = cols[2 * pad_z:2 * pad_z + 1]
    prof_ref[:pad_z, :] = BETA * (prof_t + prof_q) + SHIFT
    prof_ref[pad_z:2 * pad_z, :] = BETA * prof_q
    on = [jnp.broadcast_to(counts > float(k), (8, LANES)) for k in range(1, S_MAX)]

    def level(z, carry):
        c = courant_ref[z]
        keep = 1.0 - c
        base_s = jnp.broadcast_to(prof_ref[pl.ds(z, 1), :], (8, LANES))
        base_q = jnp.broadcast_to(prof_ref[pl.ds(pad_z + z, 1), :], (8, LANES))
        temper = [field_ref[pl.ds(z * crm_x + i, 8, stride=quads), :] for i in range(quads)]
        vapour = [field_ref[pl.ds((crm_z + z) * crm_x + i, 8, stride=quads), :] for i in range(quads)]
        sums = [t + v for t, v in zip(temper, vapour)]

        def advect(values, stay, come):
            moved = [come * v for v in values]
            last = pltpu.roll(moved[-1], 1, 0)
            return [stay * v + m for v, m in zip(values, [last] + moved[:-1])]

        def total(values):
            while len(values) > 1:
                values = [a + b for a, b in zip(values[::2], values[1::2])]
            return values[0]

        sums = [s + base_s for s in advect(sums, BETA * keep, BETA * c)]
        vapour = [v + base_q for v in advect(vapour, BETA * keep, BETA * c)]
        gone = None
        for k in range(S_MAX):
            if k > 0:
                sums = advect(sums, keep, c)
                vapour = advect(vapour, 0.5 * keep, 0.5 * c)
            excess = [jnp.maximum(v - jnp.exp2(s - v), 0.0) for s, v in zip(sums, vapour)]
            lost = total(excess)
            gone = lost if k == 0 else gone + jnp.where(on[k - 1], lost, 0.0)
            if k < S_MAX - 1:
                vapour = [(v + v) - e for v, e in zip(vapour, excess)]
        part_ref[pl.ds(8 * z, 8), :] = gone
        return carry

    lax.fori_loop(0, crm_z, level, 0, unroll=2)
    scale = CONDENSE / (BETA * crm_x)
    part_ref[8 * crm_z:, :] = jnp.zeros((8 * (64 - crm_z), LANES), jnp.float32)
    change = part_ref[pl.ds(0, 64, stride=8), :]
    for i in range(1, 8):
        change = change + part_ref[pl.ds(i, 64, stride=8), :]
    change = change * scale
    turn_ref[...] = jnp.concatenate([change, change], axis=0).T
    lane = lax.broadcasted_iota(jnp.int32, (LANES // 2, LANES), 1)
    even = turn_ref[pl.ds(0, LANES // 2, stride=2), :]
    odd = turn_ref[pl.ds(1, LANES // 2, stride=2), :]
    out_ref[...] = jnp.where(lane < LANES // 2, even, odd)


def final_kernel(dyn_ref, returned_ref, slot_ref, up_ref, out_ref):
    half, crm_z = up_ref.shape
    slot = slot_ref[...]
    width = slot.shape[1]
    pairs = returned_ref.shape[0]
    r_hi, r_lo = split(returned_ref[...])
    both = jnp.concatenate([r_hi, r_lo], axis=1)
    ids = lax.broadcasted_iota(jnp.int32, (pairs, width), 0)
    pick = (ids == slot // 2).astype(jnp.bfloat16)
    got = dot(both, pick, TN)
    got = got[:LANES] + got[LANES:]
    change = jnp.where(slot % 2 == 0, got[:LANES // 2], got[LANES // 2:])
    up = jnp.concatenate([up_ref[...], jnp.zeros((half, LANES // 2 - crm_z), jnp.float32)], axis=1)
    tend = dot3(up, change)
    for i in range(8):
        cols = slice(i * LANES, (i + 1) * LANES)
        top = pl.ds(i, half, stride=8)
        bottom = pl.ds(8 * half + i, half, stride=8)
        out_ref[top, :] = dyn_ref[top, :] + tend[:, cols]
        out_ref[bottom, :] = dyn_ref[bottom, :] - tend[:, cols]


VMEM = pl.BlockSpec(memory_space=pltpu.VMEM)


def params(limit_mib=40):
    return pltpu.CompilerParams(vmem_limit_bytes=limit_mib * 2**20)


def crm(courant, arrived, crm_field, crm_z, crm_x, interpret=False):
    slots = arrived.shape[0]
    rows = crm_field.shape[0]
    pad_z = -(-crm_z // 8) * 8
    return pl.pallas_call(
        functools.partial(crm_kernel, crm_z, crm_x),
        grid=(slots // LANES,),
        in_specs=[
            pl.BlockSpec(memory_space=pltpu.SMEM),
            pl.BlockSpec((LANES, LANES), lambda b: (b, 0)),
            pl.BlockSpec((rows, LANES), lambda b: (0, b)),
        ],
        out_specs=pl.BlockSpec((LANES // 2, LANES), lambda b: (b, 0)),
        out_shape=jax.ShapeDtypeStruct((slots // 2, LANES), jnp.float32),
        scratch_shapes=[
            pltpu.VMEM((2 * pad_z, LANES), jnp.float32),
            pltpu.VMEM((8 * 64, LANES), jnp.float32),
            pltpu.VMEM((LANES, LANES), jnp.float32),
        ],
        compiler_params=params(),
        name="crm",
    )(courant, arrived, crm_field)


def body(state, owner, counts, vert, down_map, up_map, courant, crm_field):
    rows, width_x, width_y = state.shape
    col_dev = width_x * width_y
    across = lax.axis_size("gx")
    along = lax.axis_size("gy")
    devices = across * along
    cap = max(2, 7 * col_dev // (4 * devices))
    slots = devices * cap
    crm_z = down_map.shape[0]
    crm_x = crm_field.shape[0] // (2 * crm_z)
    flat = state.reshape(rows * width_x, width_y)

    f32 = lambda *shape: jax.ShapeDtypeStruct(shape, jnp.float32)
    top, bottom, side = pl.pallas_call(
        edges_kernel,
        in_specs=[VMEM],
        out_specs=[VMEM] * 3,
        out_shape=[f32(rows, width_y), f32(rows, width_y), f32(8, rows * width_x)],
        compiler_params=params(),
        name="edges",
    )(flat)

    def shifted(value, axis, step):
        count = lax.axis_size(axis)
        return lax.ppermute(value, axis, [(i, (i + step) % count) for i in range(count)])

    above = shifted(bottom, "gx", 1)
    below = shifted(top, "gx", -1)
    left = shifted(side[1:2], "gy", 1)
    right = shifted(side[0:1], "gy", -1)

    dyn, slot, outgoing = pl.pallas_call(
        functools.partial(columns_kernel, cap),
        in_specs=[VMEM] * 9,
        out_specs=[VMEM] * 3,
        out_shape=[
            f32(rows * width_x, width_y),
            jax.ShapeDtypeStruct((1, col_dev), jnp.int32),
            f32(slots, LANES),
        ],
        compiler_params=params(),
        name="columns",
    )(flat, above, below, left, right, owner, counts, vert, down_map)

    arrived = lax.all_to_all(outgoing, ("gx", "gy"), split_axis=0, concat_axis=0, tiled=True)
    change = crm(courant, arrived, crm_field, crm_z, crm_x)
    returned = lax.all_to_all(change, ("gx", "gy"), split_axis=0, concat_axis=0, tiled=True)

    out = pl.pallas_call(
        final_kernel,
        in_specs=[VMEM] * 4,
        out_specs=VMEM,
        out_shape=f32(rows * width_x, width_y),
        compiler_params=params(),
        name="final",
    )(dyn, returned, slot, up_map)
    return out.reshape(state.shape)


def solution(mesh):
    in_specs = (
        P(None, "gx", "gy"),
        P("gx", "gy"),
        P("gx", "gy"),
        P(),
        P(),
        P(),
        P(),
        P(None, ("gx", "gy")),
    )
    out_specs = P(None, "gx", "gy")
    return jax.shard_map(body, mesh=mesh, in_specs=in_specs, out_specs=out_specs, check_vma=False)
```

time: 262 us -> 102 us (0.39)
  local copies, waits for them, and re-layouts: 95.3 us -> 6.98 us
  other arithmetic: 86.8 us -> 0 us
  Pallas kernels: 0 us -> 38.2 us
  blocking collectives: 0 us -> 25.9 us
  waiting for transfers between devices: 39.1 us -> 16.5 us
  starting transfers between devices: 28.8 us -> 13.7 us
  matrix products: 7.07 us -> 0 us
  loops' own time: 3.28 us -> 0 us
    pallas_call x0 -> x4, Pallas kernels: none -> 38.2 us  [the longest x1 33.3 us: crm(): pl.pallas_call(functools.partial(crm_kernel, crm_z, crm_x), grid=(slots /...]
    dynamic_slice x28 -> x0, local copies, waits for them, and re-layouts: 34.1 us -> none  [the longest x14 21.6 us: crm_block(): block_field = lax.dynamic_slice_in_dim(crm_field, start, block, 1)]
    all_to_all x0 -> x1, blocking collectives: none -> 25.9 us  [body(): lax.all_to_all(outgoing, ('gx', 'gy'), split_axis=0, concat_axis=0, tiled...]
    select_n x57 -> x0, other arithmetic: 25.7 us -> none  [the longest x56 25.7 us: advance(): return jnp.where(active[None, None, None, :], result, fields)]
    add x72 -> x0, other arithmetic: 23.1 us -> none  [the longest x56 16.2 us: advance(): result = jnp.stack([temper + latent_heat * condensed, vapour - condensed])]
    all_to_all x3 -> x1, waiting for transfers between devices: 36.6 us -> 13.5 us  [body(): lax.all_to_all(change, ('gx', 'gy'), split_axis=0, concat_axis=0, tiled=T...]
    sub x57 -> x0, other arithmetic: 18.9 us -> none  [the longest x56 18.9 us: advance(): moved = fields - courant[None, :, None, None] * (fields - shifted)]
    all_to_all x3 -> x1, starting transfers between devices: 20.2 us -> 4.69 us  [body(): lax.all_to_all(change, ('gx', 'gy'), split_axis=0, concat_axis=0, tiled=T...]
  transfers between devices with their start and end apart: 7 -> 5, of which waited for: 3 -> 3; matrix products, arithmetic and copies ran while one was open for 10% -> 0% of each run, Pallas kernels for 0% -> 0%
where the time goes in v1:
time: 102 us; the launch traced here: 101 us
  Pallas kernels  38.2 us (37%)
  blocking collectives  25.9 us (25%)
  waiting for transfers between devices  16.5 us (16%)
  starting transfers between devices  13.7 us (13%)
  local copies, waits for them, and re-layouts  6.98 us (7%)
    pallas_call x1, Pallas kernels, crm(): pl.pallas_call(functools.partial(crm_kernel, crm_z, crm_x), grid=(slots /...  33.3 us
    all_to_all x1, blocking collectives, body(): lax.all_to_all(outgoing, ('gx', 'gy'), split_axis=0, concat_axis=0, tiled...  25.9 us
    all_to_all x1, waiting for transfers between devices, body(): lax.all_to_all(change, ('gx', 'gy'), split_axis=0, concat_axis=0, tiled=T...  13.5 us
    ppermute x4, starting transfers between devices, shifted(): lax.ppermute(value, axis, [(i, (i + step) % count) for i in range(count)])  9.05 us
    unnamed x15, local copies, waits for them, and re-layouts  4.69 us
    all_to_all x1, starting transfers between devices, body(): lax.all_to_all(change, ('gx', 'gy'), split_axis=0, concat_axis=0, tiled=T...  4.69 us
    ppermute x4, waiting for transfers between devices, shifted(): lax.ppermute(value, axis, [(i, (i + step) % count) for i in range(count)])  3.04 us
    pallas_call x1, Pallas kernels, body(): pl.pallas_call(functools.partial(columns_kernel, cap), in_specs=[VMEM] *...  2.54 us
  transfers between devices with their start and end apart: 5, of which 3 were waited for; matrix products, arithmetic and copies ran while one was open for 0% of the time, Pallas kernels for 0%

profile of v1, /device:TPU:1, one launch (start us, length us, event | category | flops | bytes accessed | tf_op | source)
XLA Modules:
  0.0 101.4 jit_solution(15872369357340422931)
XLA Ops:
  0.0 0.0 copy-start
  0.0 1.1 %copy-done = f32[144,8,128]{2,1,0:T(8,128)S(1)} copy-done((f32[144,8,128]{2,1,0:T(8,128)S(1)}, f32[144,8,128]{2,1,0:T(8,128)}, u32[]{:S(2)}) %copy-start) | copy-done | bytes 589848
  1.1 0.0 copy-start.6
  1.1 0.4 edges.1
  1.5 2.5 %collective-permute-start = (f32[144,128]{1,0:T(8,128)S(1)}, f32[144,128]{1,0:T(8,128)S(1)}, u32[]{:S(2)}, u32[]{:S(2)}) collective-permute-start(f32[144,128]{1,0:T(8,128)S(1)} %get-tuple-element.11), channel_id=1, source_target_pairs={{0,8},{8,16},{16,24},{24,32},{32,40},{40,48},{48,56},{56,64},{64,7... | collective-permute-start | bytes 221192 | tf_op jit(solution)/shard_map/ppermute | solution.py:261
  4.0 4.4 %collective-permute-start.1 = (f32[144,128]{1,0:T(8,128)S(1)}, f32[144,128]{1,0:T(8,128)S(1)}, u32[]{:S(2)}, u32[]{:S(2)}) collective-permute-start(f32[144,128]{1,0:T(8,128)S(1)} %get-tuple-element.12), channel_id=1, source_target_pairs={{0,120},{8,0},{16,8},{24,16},{32,24},{40,32},{48,40},{56,48},{64,5... | collective-permute-start | bytes 221192 | tf_op jit(solution)/shard_map/ppermute | solution.py:261
  8.4 2.1 %collective-permute-start.2 = (f32[1,1152]{1,0:T(1,128)S(1)}, f32[1,1152]{1,0:T(1,128)S(1)}, u32[]{:S(2)}, u32[]{:S(2)}) collective-permute-start(f32[1,1152]{1,0:T(1,128)S(1)} %get-tuple-element.18), channel_id=1, source_target_pairs={{0,1},{1,2},{2,3},{3,4},{4,5},{5,6},{6,7},{7,0},{8,9},{9,10},{10,1... | collective-permute-start | bytes 13832 | tf_op jit(solution)/shard_map/ppermute | solution.py:261
  10.5 0.0 collective-permute-start.3
  10.5 0.8 collective-permute-done.2.left_ref
  11.3 2.3 %collective-permute-done.3.right_ref = f32[1,1152]{1,0:T(1,128)S(1)} collective-permute-done((f32[1,1152]{1,0:T(1,128)S(1)}, f32[1,1152]{1,0:T(1,128)S(1)}, u32[]{:S(2)}, u32[]{:S(2)}) %collective-permute-start.3) | collective-permute-done | bytes 4640 | tf_op jit(solution)/shard_map/ppermute | solution.py:261
  13.6 0.0 collective-permute-done.above_ref
  13.6 0.0 collective-permute-done.1.below_ref
  13.6 0.0 copy-start.1
  13.6 0.8 copy-done.1
  14.3 0.0 copy-start.2
  14.3 0.7 copy-done.2
  15.1 0.0 copy-start.3
  15.1 0.7 copy-done.3
  15.8 0.0 copy-start.4
  15.8 0.7 copy-done.4
  16.5 2.5 %columns.1 = (f32[1152,128]{1,0:T(8,128)S(1)}, s32[1,1024]{1,0:T(1,128)S(1)}, f32[1792,128]{1,0:T(8,128)S(1)}) custom-call(f32[1152,128]{1,0:T(8,128)S(1)} %bitcast.3, f32[144,128]{1,0:T(8,128)S(1)} %collective-permute-done.above_ref, f32[144,128]{1,0:T(8,128)S(1)} %collective-permute-done.1.below_ref, f32[1,1152]{1,0:T(1,128)S(1)} %collective-permute-done.2.left_ref, ...), custom_call_target="tpu_custom_call" | custom-call | tf_op jit(solution)/shard_map/columns/pallas_call | solution.py:268
  19.0 0.1 all_to_all.14
  19.1 25.9 %all_to_all.22 = f32[128,14,128]{2,1,0:T(8,128)} all-to-all(f32[128,14,128]{2,1,0:T(8,128)S(1)} %all_to_all.14), channel_id=1, replica_groups=mesh['gx'=16,'gy'=8] {'gx','gy'}, dimensions={0} | all-to-all | bytes 1835008 | tf_op jit(solution)/shard_map/all_to_all | solution.py:281
  45.0 1.3 %all_to_all.16.arrived_ref = f32[1792,128]{1,0:T(8,128)S(1)} reshape(f32[128,14,128]{2,1,0:T(8,128)} %all_to_all.22) | data formatting | bytes 1835008 | tf_op jit(solution)/shard_map/all_to_all | solution.py:281
  46.3 0.0 copy-start.5
  46.3 0.6 copy-done.5
  47.0 33.3 %crm.1 = f32[896,128]{1,0:T(8,128)S(1)} custom-call(f32[50]{0:T(128)S(1)} %copy-done.5, f32[1792,128]{1,0:T(8,128)S(1)} %all_to_all.16.arrived_ref, f32[3200,1792]{1,0:T(8,128)} %field_ref.1), custom_call_target="tpu_custom_call" | custom-call | tf_op jit(solution)/shard_map/crm/pallas_call | solution.py:217
  80.3 0.9 all_to_all.17
  81.2 4.7 %all-to-all-start.1 = ((f32[128,7,128]{2,1,0:T(8,128)}), f32[128,7,128]{2,1,0:T(8,128)S(1)}, u32[]{:S(2)}, u32[]{:S(2)}) async-start(f32[128,7,128]{2,1,0:T(8,128)} %all_to_all.17), calls=%async_computation.1 | async-start | bytes 1048576 | tf_op jit(solution)/shard_map/all_to_all | solution.py:283
  85.9 0.0 copy-done.6
  85.9 0.1 copy.10.up_ref
  86.0 13.5 %all-to-all-done.1 = f32[128,7,128]{2,1,0:T(8,128)S(1)} async-done(((f32[128,7,128]{2,1,0:T(8,128)}), f32[128,7,128]{2,1,0:T(8,128)S(1)}, u32[]{:S(2)}, u32[]{:S(2)}) %all-to-all-start.1) | async-done | bytes 458784 | tf_op jit(solution)/shard_map/all_to_all | solution.py:283
  99.5 2.0 %final.1 = f32[1152,128]{1,0:T(8,128)} custom-call(f32[1152,128]{1,0:T(8,128)S(1)} %get-tuple-element.14.dyn_ref, f32[896,128]{1,0:T(8,128)S(1)} %all_to_all.19.returned_ref, s32[1,1024]{1,0:T(1,128)S(1)} %get-tuple-element.16.slot_ref, f32[72,50]{1,0:T(8,128)S(1)} %copy.10.up_ref), custom_call_target="tpu_custom_call" | custom-call | tf_op jit(solution)/shard_map/final/pallas_call | solution.py:285
  (2 shorter events, 0.1 us)
Async XLA Ops:
  0.0 1.1 %copy-start = (f32[144,8,128]{2,1,0:T(8,128)S(1)}, f32[144,8,128]{2,1,0:T(8,128)}, u32[]{:S(2)}) copy-start(f32[144,8,128]{2,1,0:T(8,128)} %param.8) | copy-start | bytes 1769476
  1.1 84.8 %copy-start.6 = (f32[72,50]{0,1:T(8,128)S(1)}, f32[72,50]{0,1:T(8,128)}, u32[]{:S(2)}) copy-start(f32[72,50]{0,1:T(8,128)} %param.13) | copy-start | bytes 43204
  1.5 12.1 %collective-permute-start = (f32[144,128]{1,0:T(8,128)S(1)}, f32[144,128]{1,0:T(8,128)S(1)}, u32[]{:S(2)}, u32[]{:S(2)}) collective-permute-start(f32[144,128]{1,0:T(8,128)S(1)} %get-tuple-element.11), channel_id=1, source_target_pairs={{0,8},{8,16},{16,24},{24,32},{32,40},{40,48},{48,56},{56,64},{64,7... | collective-permute-start | bytes 221192 | tf_op jit(solution)/shard_map/ppermute | solution.py:261
  4.0 9.6 %collective-permute-start.1 = (f32[144,128]{1,0:T(8,128)S(1)}, f32[144,128]{1,0:T(8,128)S(1)}, u32[]{:S(2)}, u32[]{:S(2)}) collective-permute-start(f32[144,128]{1,0:T(8,128)S(1)} %get-tuple-element.12), channel_id=1, source_target_pairs={{0,120},{8,0},{16,8},{24,16},{32,24},{40,32},{48,40},{56,48},{64,5... | collective-permute-start | bytes 221192 | tf_op jit(solution)/shard_map/ppermute | solution.py:261
  8.4 2.9 %collective-permute-start.2 = (f32[1,1152]{1,0:T(1,128)S(1)}, f32[1,1152]{1,0:T(1,128)S(1)}, u32[]{:S(2)}, u32[]{:S(2)}) collective-permute-start(f32[1,1152]{1,0:T(1,128)S(1)} %get-tuple-element.18), channel_id=1, source_target_pairs={{0,1},{1,2},{2,3},{3,4},{4,5},{5,6},{6,7},{7,0},{8,9},{9,10},{10,1... | collective-permute-start | bytes 13832 | tf_op jit(solution)/shard_map/ppermute | solution.py:261
  10.5 3.0 %collective-permute-start.3 = (f32[1,1152]{1,0:T(1,128)S(1)}, f32[1,1152]{1,0:T(1,128)S(1)}, u32[]{:S(2)}, u32[]{:S(2)}) collective-permute-start(f32[1,1152]{1,0:T(1,128)S(1)} %get-tuple-element.17), channel_id=1, source_target_pairs={{0,7},{1,0},{2,1},{3,2},{4,3},{5,4},{6,5},{7,6},{8,15},{9,8},{10,9... | collective-permute-start | bytes 13832 | tf_op jit(solution)/shard_map/ppermute | solution.py:261
  13.6 0.8 copy-start.1
  14.3 0.7 copy-start.2
  15.1 0.7 copy-start.3
  15.8 0.7 copy-start.4
  46.3 0.7 copy-start.5
  81.2 18.2 %all-to-all-start.1 = ((f32[128,7,128]{2,1,0:T(8,128)}), f32[128,7,128]{2,1,0:T(8,128)S(1)}, u32[]{:S(2)}, u32[]{:S(2)}) async-start(f32[128,7,128]{2,1,0:T(8,128)} %all_to_all.17), calls=%async_computation.1 | async-start | bytes 1048576 | tf_op jit(solution)/shard_map/all_to_all | solution.py:283

commit v2 on v1

v2 whole, which is shorter than its diff:
```python
import functools
import math

import jax
import jax.numpy as jnp
from jax import lax
from jax.experimental import pallas as pl
from jax.experimental.pallas import tpu as pltpu
from jax.sharding import PartitionSpec as P

S_MAX = 4
DIFFUSION = 0.1
CONDENSE = 0.5
SLOPE = 0.3
LANES = 128
SUBL = 8
BETA = SLOPE * math.log2(math.e)
SHIFT = math.log2(BETA)

NT = (((1,), (1,)), ((), ()))
NN = (((1,), (0,)), ((), ()))
TN = (((0,), (0,)), ((), ()))


def split(value):
    high = value.astype(jnp.bfloat16)
    low = (value - high.astype(jnp.float32)).astype(jnp.bfloat16)
    return high, low


def dot(a, b, dims=NN):
    return lax.dot_general(a, b, dims, preferred_element_type=jnp.float32)


def dot3(a, b):
    a_hi, a_lo = split(a)
    b_hi, b_lo = split(b)
    return dot(a_hi, b_hi) + (dot(a_hi, b_lo) + dot(a_lo, b_hi))


def edges_kernel(state_ref, top_ref, bottom_ref, west_ref, east_ref):
    levels = top_ref.shape[0]
    rows = [state_ref[pl.ds(i, levels, stride=SUBL), :] for i in range(SUBL)]
    top_ref[...] = rows[0]
    bottom_ref[...] = rows[-1]
    row = lax.broadcasted_iota(jnp.int32, (SUBL, LANES), 0)
    lane = lax.broadcasted_iota(jnp.int32, (SUBL, LANES), 1)
    pick = ((row == 0) & (lane == 0)) | ((row == 1) & (lane == LANES - 1))
    pick = pick.astype(jnp.bfloat16)
    for i in range(SUBL):
        hi, lo = split(rows[i])
        side = dot(pick, hi, NT) + dot(pick, lo, NT)
        west_ref[i:i + 1, :] = side[0:1]
        east_ref[i:i + 1, :] = side[1:2]


def local_kernel(
    cap, state_ref, owner_hbm, counts_hbm, vert_hbm, courant_hbm, down_hbm,
    base_ref, slot_ref, steps_ref, const_ref, down_ref,
    owner_ref, counts_ref, vert_ref, courant_ref, sems,
):
    copies = [
        pltpu.make_async_copy(src, dst, sems.at[i])
        for i, (src, dst) in enumerate(
            [
                (owner_hbm, owner_ref),
                (counts_hbm, counts_ref),
                (vert_hbm, vert_ref),
                (courant_hbm, courant_ref),
                (down_hbm, down_ref),
            ]
        )
    ]
    for copy in copies:
        copy.start()
    levels = base_ref.shape[0]
    half = levels // 2
    crm_z = courant_ref.shape[0]
    wide = lax.broadcasted_iota(jnp.int32, (levels, LANES), 1)
    rows = [state_ref[pl.ds(i, levels, stride=SUBL), :] for i in range(SUBL)]
    laps = []
    for i in range(SUBL):
        mid = rows[i]
        lap = jnp.where(wide == 0, 0.0, pltpu.roll(mid, 1, 1))
        lap = lap + jnp.where(wide == LANES - 1, 0.0, pltpu.roll(mid, LANES - 1, 1))
        if i > 0:
            lap = lap + rows[i - 1]
        if i < SUBL - 1:
            lap = lap + rows[i + 1]
        laps.append(mid + DIFFUSION * (lap - 4.0 * mid))
    whole = jnp.concatenate(rows, axis=1)
    base = jnp.concatenate(laps, axis=1)
    copies[2].wait()
    vert = vert_ref[...]
    base_ref[:half, :] = base[:half] + dot3(vert, whole[:half])
    base_ref[half:, :] = base[half:] + dot3(vert, whole[half:])

    copies[0].wait()
    owner = jnp.concatenate([owner_ref[i:i + 1, :] for i in range(SUBL)], axis=1)
    width = owner.shape[1]
    devices = LANES * (-(-DEVICES // LANES))
    mine = lax.broadcasted_iota(jnp.int32, (devices, width), 0) == owner
    earlier = (
        lax.broadcasted_iota(jnp.int32, (width, width), 0)
        < lax.broadcasted_iota(jnp.int32, (width, width), 1)
    ).astype(jnp.bfloat16)
    before = dot(mine.astype(jnp.bfloat16), earlier)
    rank = jnp.sum(jnp.where(mine, before, 0.0), axis=0, keepdims=True).astype(jnp.int32)
    slot_ref[...] = owner * cap + rank
    copies[1].wait()
    counts = jnp.concatenate([counts_ref[i:i + 1, :] for i in range(SUBL)], axis=1)
    lead = (lax.broadcasted_iota(jnp.int32, (SUBL, width), 0) == 0).astype(jnp.float32)
    steps_ref[...] = lead * counts.astype(jnp.float32)
    copies[3].wait()
    row = lax.broadcasted_iota(jnp.int32, (SUBL, LANES), 0)
    for z in range(crm_z):
        c = courant_ref[z]
        keep = 1.0 - c
        part = jnp.where(row % 2 == 0, keep, c)
        const_ref[SUBL * z:SUBL * (z + 1), :] = part * jnp.where(row < 2, BETA, jnp.where(row < 4, 1.0, 0.5))
    copies[4].wait()


def send_kernel(
    base_ref, slot_ref, steps_ref, down_ref, above_ref, below_ref, left_ref, right_ref,
    dyn_ref, out_ref,
):
    levels, width = base_ref.shape
    half = levels // 2
    crm_z = down_ref.shape[0]
    pad_z = -(-crm_z // SUBL) * SUBL
    sides = jnp.concatenate([left_ref[...], right_ref[...]], axis=0)
    row = lax.broadcasted_iota(jnp.int32, (2 * SUBL, width), 0)
    lane = lax.broadcasted_iota(jnp.int32, (2 * SUBL, width), 1)
    target = jnp.where(row < SUBL, row * LANES, (row - SUBL) * LANES + (LANES - 1))
    place = (lane == target).astype(jnp.bfloat16)
    s_hi, s_lo = split(sides)
    halo = dot(s_hi, place, TN) + dot(s_lo, place, TN)
    first = halo[:, :LANES] + above_ref[...]
    last = halo[:, width - LANES:] + below_ref[...]
    halo = jnp.concatenate([first, halo[:, LANES:width - LANES], last], axis=1)
    dyn = base_ref[...] + DIFFUSION * halo
    dyn_ref[...] = dyn
    down = jnp.concatenate([down_ref[...], jnp.zeros((pad_z - crm_z, half), jnp.float32)], axis=0)
    prof_t = dot3(down, dyn[:half])
    prof_q = dot3(down, dyn[half:])
    blank = jnp.zeros((LANES - 2 * pad_z - SUBL, width), jnp.float32)
    payload = jnp.concatenate([prof_t, prof_q, steps_ref[...], blank], axis=0)
    p_hi, p_lo = split(payload)
    both = jnp.concatenate([p_hi, p_lo], axis=0)
    slot = slot_ref[...]
    chunk = 256
    for start in range(0, out_ref.shape[0], chunk):
        ids = start + lax.broadcasted_iota(jnp.int32, (chunk, width), 0)
        sent = dot((ids == slot).astype(jnp.bfloat16), both, NT)
        out_ref[start:start + chunk, :] = sent[:, :LANES] + sent[:, LANES:]


def total(values):
    while len(values) > 1:
        values = [a + b for a, b in zip(values[::2], values[1::2])]
    return values[0]


def advect(values, stay, come):
    moved = [come * v for v in values]
    last = pltpu.roll(moved[-1], 1, 0)
    return [stay * v + m for v, m in zip(values, [last] + moved[:-1])]


def crm_kernel(crm_z, crm_x, const_ref, arrived_ref, field_ref, out_ref, prof_ref, part_ref, turn_ref):
    pad_z = -(-crm_z // SUBL) * SUBL
    quads = crm_x // SUBL
    cols = arrived_ref[...].T
    prof_ref[:pad_z, :] = BETA * cols[:pad_z] + SHIFT
    prof_ref[pad_z:2 * pad_z, :] = BETA * cols[pad_z:2 * pad_z]
    counts = jnp.broadcast_to(cols[2 * pad_z:2 * pad_z + 1], (SUBL, LANES))
    part = jnp.where(counts > 3.0, 0.0625, jnp.where(counts > 2.0, 0.125, jnp.where(counts > 1.0, 0.25, 0.5)))
    scale = 2.0 * CONDENSE / (BETA * crm_x)
    w_first = (1.0 - part) * scale
    w_kept = [jnp.where(counts > float(k), part * (-scale * 2.0**k), 0.0) for k in range(S_MAX)]

    def spread(ref, row):
        return jnp.broadcast_to(ref[pl.ds(row, 1), :], (SUBL, LANES))

    for z in range(crm_z):
        beta_keep, beta_c, keep, c, half_keep, half_c = [spread(const_ref, SUBL * z + i) for i in range(6)]
        base_t = spread(prof_ref, z)
        base_q = spread(prof_ref, pad_z + z)
        temper = [field_ref[pl.ds(z * crm_x + i, SUBL, stride=quads), :] for i in range(quads)]
        vapour = [field_ref[pl.ds((crm_z + z) * crm_x + i, SUBL, stride=quads), :] for i in range(quads)]
        temper = [t + base_t for t in advect(temper, beta_keep, beta_c)]
        vapour = [v + base_q for v in advect(vapour, beta_keep, beta_c)]
        sums = [t + v for t, v in zip(temper, vapour)]
        gone = w_first * total(vapour)
        for k in range(S_MAX):
            if k > 0:
                sums = advect(sums, keep, c)
                vapour = advect(vapour, half_keep, half_c)
                temper = [s - v for s, v in zip(sums, vapour)]
            kept = [jnp.minimum(v, jnp.exp2(t)) for t, v in zip(temper, vapour)]
            gone = gone + w_kept[k] * total(kept)
            if k < S_MAX - 1:
                vapour = [v + e for v, e in zip(vapour, kept)]
        part_ref[SUBL * z:SUBL * (z + 1), :] = gone
    part_ref[SUBL * crm_z:, :] = jnp.zeros((SUBL * (LANES // 2 - crm_z), LANES), jnp.float32)
    change = part_ref[pl.ds(0, LANES // 2, stride=SUBL), :]
    for i in range(1, SUBL):
        change = change + part_ref[pl.ds(i, LANES // 2, stride=SUBL), :]
    turn_ref[...] = jnp.concatenate([change, change], axis=0).T
    lane = lax.broadcasted_iota(jnp.int32, (LANES // 2, LANES), 1)
    even = turn_ref[pl.ds(0, LANES // 2, stride=2), :]
    odd = turn_ref[pl.ds(1, LANES // 2, stride=2), :]
    out_ref[...] = jnp.where(lane < LANES // 2, even, odd)


def final_kernel(dyn_ref, returned_ref, slot_ref, up_ref, out_ref):
    half, crm_z = up_ref.shape
    slot = slot_ref[...]
    width = slot.shape[1]
    pairs = returned_ref.shape[0]
    r_hi, r_lo = split(returned_ref[...])
    both = jnp.concatenate([r_hi, r_lo], axis=1)
    ids = lax.broadcasted_iota(jnp.int32, (pairs, width), 0)
    pick = (ids == slot // 2).astype(jnp.bfloat16)
    got = dot(both, pick, TN)
    got = got[:LANES] + got[LANES:]
    change = jnp.where(slot % 2 == 0, got[:LANES // 2], got[LANES // 2:])
    up = jnp.concatenate([up_ref[...], jnp.zeros((half, LANES // 2 - crm_z), jnp.float32)], axis=1)
    tend = dot3(up, change)
    for i in range(SUBL):
        cols = slice(i * LANES, (i + 1) * LANES)
        out_ref[pl.ds(i, half, stride=SUBL), :] = dyn_ref[:half, cols] + tend[:, cols]
        out_ref[pl.ds(SUBL * half + i, half, stride=SUBL), :] = dyn_ref[half:, cols] - tend[:, cols]


VMEM = pl.BlockSpec(memory_space=pltpu.VMEM)
HBM = pl.BlockSpec(memory_space=pltpu.HBM)
DEVICES = 128


def params(limit_mib=16):
    return pltpu.CompilerParams(vmem_limit_bytes=limit_mib * 2**20)


def f32(*shape):
    return jax.ShapeDtypeStruct(shape, jnp.float32)


def i32(*shape):
    return jax.ShapeDtypeStruct(shape, jnp.int32)


def crm(const, arrived, crm_field, crm_z, crm_x):
    slots = arrived.shape[0]
    rows = crm_field.shape[0]
    pad_z = -(-crm_z // SUBL) * SUBL
    return pl.pallas_call(
        functools.partial(crm_kernel, crm_z, crm_x),
        grid=(slots // LANES,),
        in_specs=[
            VMEM,
            pl.BlockSpec((LANES, LANES), lambda b: (b, 0)),
            pl.BlockSpec((rows, LANES), lambda b: (0, b)),
        ],
        out_specs=pl.BlockSpec((LANES // 2, LANES), lambda b: (b, 0)),
        out_shape=f32(slots // 2, LANES),
        scratch_shapes=[
            pltpu.VMEM((2 * pad_z, LANES), jnp.float32),
            pltpu.VMEM((SUBL * LANES // 2, LANES), jnp.float32),
            pltpu.VMEM((LANES, LANES), jnp.float32),
        ],
        compiler_params=params(48),
        name="crm",
    )(const, arrived, crm_field)


def exchange(value, devices):
    sent = value.reshape(devices, 1, -1)
    got = lax.all_to_all(sent, ("gx", "gy"), split_axis=0, concat_axis=0, tiled=True)
    return got.reshape(value.shape)


def shifted(value, axis, step):
    count = lax.axis_size(axis)
    return lax.ppermute(value, axis, [(i, (i + step) % count) for i in range(count)])


def body(state, owner, counts, vert, down_map, up_map, courant, crm_field):
    rows, width_x, width_y = state.shape
    col_dev = width_x * width_y
    devices = lax.axis_size("gx") * lax.axis_size("gy")
    cap = max(2, 7 * col_dev // (4 * devices))
    slots = devices * cap
    crm_z = down_map.shape[0]
    crm_x = crm_field.shape[0] // (2 * crm_z)
    flat = state.reshape(rows * width_x, width_y)

    top, bottom, west, east = pl.pallas_call(
        edges_kernel,
        in_specs=[VMEM],
        out_specs=[VMEM] * 4,
        out_shape=[f32(rows, width_y), f32(rows, width_y), f32(width_x, rows), f32(width_x, rows)],
        compiler_params=params(),
        name="edges",
    )(flat)

    above = shifted(bottom, "gx", 1)
    below = shifted(top, "gx", -1)
    left = shifted(east, "gy", 1)
    right = shifted(west, "gy", -1)

    base, slot, steps, const, down = pl.pallas_call(
        functools.partial(local_kernel, cap),
        in_specs=[VMEM] + [HBM] * 5,
        out_specs=[VMEM] * 5,
        out_shape=[f32(rows, col_dev), i32(1, col_dev), f32(SUBL, col_dev), f32(SUBL * crm_z, LANES), f32(*down_map.shape)],
        scratch_shapes=[
            pltpu.VMEM(owner.shape, jnp.int32),
            pltpu.VMEM(counts.shape, jnp.int32),
            pltpu.VMEM(vert.shape, jnp.float32),
            pltpu.SMEM(courant.shape, jnp.float32),
            pltpu.SemaphoreType.DMA((5,)),
        ],
        compiler_params=params(),
        cost_estimate=pl.CostEstimate(flops=10**9, bytes_accessed=4 * 10**6, transcendentals=0),
        name="local",
    )(flat, owner, counts, vert, courant, down_map)

    dyn, outgoing = pl.pallas_call(
        send_kernel,
        in_specs=[VMEM] * 8,
        out_specs=[VMEM] * 2,
        out_shape=[f32(rows, col_dev), f32(slots, LANES)],
        compiler_params=params(),
        name="send",
    )(base, slot, steps, down, above, below, left, right)

    arrived = exchange(outgoing, devices)
    change = crm(const, arrived, crm_field, crm_z, crm_x)
    returned = exchange(change, devices)

    out = pl.pallas_call(
        final_kernel,
        in_specs=[VMEM] * 4,
        out_specs=VMEM,
        out_shape=f32(rows * width_x, width_y),
        compiler_params=params(),
        name="final",
    )(dyn, returned, slot, up_map)
    return out.reshape(state.shape)


def solution(mesh):
    in_specs = (
        P(None, "gx", "gy"),
        P("gx", "gy"),
        P("gx", "gy"),
        P(),
        P(),
        P(),
        P(),
        P(None, ("gx", "gy")),
    )
    out_specs = P(None, "gx", "gy")
    return jax.shard_map(body, mesh=mesh, in_specs=in_specs, out_specs=out_specs, check_vma=False)
```

time: 102 us -> 84.6 us (0.83)
  Pallas kernels: 38.2 us -> 29.1 us
  waiting for transfers between devices: 16.5 us -> 12.8 us
  local copies, waits for them, and re-layouts: 6.98 us -> 4.7 us
  blocking collectives: 25.9 us -> 23.8 us
    pallas_call x1, Pallas kernels: 33.3 us -> 23.6 us  [crm(): pl.pallas_call(functools.partial(crm_kernel, crm_z, crm_x), grid=(slots /...]
    ppermute x4, waiting for transfers between devices: 3.04 us -> 0.01 us  [shifted(): lax.ppermute(value, axis, [(i, (i + step) % count) for i in range(count)])]
    all_to_all x4 -> x0, local copies, waits for them, and re-layouts: 2.28 us -> none  [the longest x2 1.38 us: body(): lax.all_to_all(outgoing, ('gx', 'gy'), split_axis=0, concat_axis=0, tiled...]
    all_to_all x1, blocking collectives: 25.9 us -> 23.8 us  [exchange(): lax.all_to_all(sent, ('gx', 'gy'), split_axis=0, concat_axis=0, tiled=True)]
    pallas_call x2 -> x3, Pallas kernels: 2.92 us -> 3.64 us  [the longest x1 1.82 us: body(): pl.pallas_call(send_kernel, in_specs=[VMEM] * 8, out_specs=[VMEM] * 2, ou...]
  transfers between devices with their start and end apart: 5 -> 5, of which waited for: 3 -> 1; matrix products, arithmetic and copies ran while one was open for 0% -> 0% of each run, Pallas kernels for 0% -> 2%
where the time goes in v2:
time: 84.6 us; the launch traced here: 84.1 us
  Pallas kernels  29.1 us (34%)
  blocking collectives  23.8 us (28%)
  starting transfers between devices  13.7 us (16%)
  waiting for transfers between devices  12.8 us (15%)
  local copies, waits for them, and re-layouts  4.7 us (6%)
    all_to_all x1, blocking collectives, exchange(): lax.all_to_all(sent, ('gx', 'gy'), split_axis=0, concat_axis=0, tiled=True)  23.8 us
    pallas_call x1, Pallas kernels, crm(): pl.pallas_call(functools.partial(crm_kernel, crm_z, crm_x), grid=(slots /...  23.6 us
    all_to_all x1, waiting for transfers between devices, exchange(): lax.all_to_all(sent, ('gx', 'gy'), split_axis=0, concat_axis=0, tiled=True)  12.7 us
    ppermute x4, starting transfers between devices, shifted(): lax.ppermute(value, axis, [(i, (i + step) % count) for i in range(count)])  9.02 us
    unnamed x15, local copies, waits for them, and re-layouts  4.7 us
    all_to_all x1, starting transfers between devices, exchange(): lax.all_to_all(sent, ('gx', 'gy'), split_axis=0, concat_axis=0, tiled=True)  4.69 us
    pallas_call x1, Pallas kernels, body(): pl.pallas_call(final_kernel, in_specs=[VMEM] * 4, out_specs=VMEM, out_sha...  1.91 us
    pallas_call x1, Pallas kernels, body(): pl.pallas_call(send_kernel, in_specs=[VMEM] * 8, out_specs=[VMEM] * 2, ou...  1.82 us
  transfers between devices with their start and end apart: 5, of which 1 were waited for; matrix products, arithmetic and copies ran while one was open for 0% of the time, Pallas kernels for 2%

profile of v2, /device:TPU:1, one launch (start us, length us, event | category | flops | bytes accessed | tf_op | source)
XLA Modules:
  0.0 84.1 jit_solution(14883740929860613679)
XLA Ops:
  0.0 0.0 copy-start
  0.0 1.1 %copy-done = f32[144,8,128]{2,1,0:T(8,128)S(1)} copy-done((f32[144,8,128]{2,1,0:T(8,128)S(1)}, f32[144,8,128]{2,1,0:T(8,128)}, u32[]{:S(2)}) %copy-start) | copy-done | bytes 589848
  1.1 0.0 copy-start.6
  1.1 0.4 edges.1
  1.5 2.5 %collective-permute-start = (f32[144,128]{1,0:T(8,128)S(1)}, f32[144,128]{1,0:T(8,128)S(1)}, u32[]{:S(2)}, u32[]{:S(2)}) collective-permute-start(f32[144,128]{1,0:T(8,128)S(1)} %get-tuple-element.20), channel_id=1, source_target_pairs={{0,8},{8,16},{16,24},{24,32},{32,40},{40,48},{48,56},{56,64},{64,7... | collective-permute-start | bytes 221192 | tf_op jit(solution)/shard_map/ppermute | solution.py:286
  4.0 4.4 %collective-permute-start.1 = (f32[144,128]{1,0:T(8,128)S(1)}, f32[144,128]{1,0:T(8,128)S(1)}, u32[]{:S(2)}, u32[]{:S(2)}) collective-permute-start(f32[144,128]{1,0:T(8,128)S(1)} %get-tuple-element.21), channel_id=1, source_target_pairs={{0,120},{8,0},{16,8},{24,16},{32,24},{40,32},{48,40},{56,48},{64,5... | collective-permute-start | bytes 221192 | tf_op jit(solution)/shard_map/ppermute | solution.py:286
  8.4 2.1 %collective-permute-start.2 = (f32[8,144]{1,0:T(8,128)S(1)}, f32[8,144]{1,0:T(8,128)S(1)}, u32[]{:S(2)}, u32[]{:S(2)}) collective-permute-start(f32[8,144]{1,0:T(8,128)S(1)} %get-tuple-element.22), channel_id=1, source_target_pairs={{0,1},{1,2},{2,3},{3,4},{4,5},{5,6},{6,7},{7,0},{8,9},{9,10},{10,1... | collective-permute-start | bytes 13832 | tf_op jit(solution)/shard_map/ppermute | solution.py:286
  10.5 0.0 collective-permute-start.3
  10.5 0.0 copy-start.1
  10.5 0.8 copy-done.1
  11.3 0.0 copy-start.2
  11.3 0.7 copy-done.2
  12.0 0.0 copy-start.3
  12.0 0.7 copy-done.3
  12.7 0.0 copy-start.4
  12.7 0.7 copy-done.4
  13.4 0.0 copy-start.5
  13.4 0.7 copy-done.5
  14.1 1.4 %local.1 = (f32[144,1024]{1,0:T(8,128)S(1)}, s32[1,1024]{1,0:T(1,128)S(1)}, f32[8,1024]{1,0:T(8,128)S(1)}, f32[400,128]{1,0:T(8,128)S(1)}, f32[50,72]{1,0:T(8,128)S(1)}) custom-call(f32[1152,128]{1,0:T(8,128)S(1)} %bitcast.10, s32[8,128]{1,0:T(8,128)S(1)} %copy-done.3, s32[8,128]{1,0:T(8,128)S(1)} %copy-done.4, f32[72,72]{1,0:T(8,128)S(1)} %copy-done.1, ...), custom_call_target="tpu_custom_call" | custom-call | flops 1000000000 | bytes 4000000 | tf_op jit(solution)/shard_map/local/pallas_call | solution.py:313
  15.5 0.0 collective-permute-done.2.left_ref
  15.5 0.0 collective-permute-done.3.right_ref
  15.5 0.0 collective-permute-done.above_ref
  15.5 0.0 collective-permute-done.1.below_ref
  15.5 1.8 %send.1 = (f32[144,1024]{1,0:T(8,128)S(1)}, f32[1792,128]{1,0:T(8,128)S(1)}) custom-call(f32[144,1024]{1,0:T(8,128)S(1)} %get-tuple-element.16.base_ref, s32[1,1024]{1,0:T(1,128)S(1)} %get-tuple-element.17.slot_ref, f32[8,1024]{1,0:T(8,128)S(1)} %get-tuple-element.18.steps_ref, f32[50,72]{1,0:T(8,128)S(1)} %get-tuple-element.19.down_ref, ...), custom_call_target="tpu_custom_call" | custom-call | tf_op jit(solution)/shard_map/send/pallas_call | solution.py:330
  17.3 23.8 %all_to_all.10 = f32[128,1,1792]{2,1,0:T(1,128)S(1)} all-to-all(f32[128,1,1792]{2,1,0:T(1,128)S(1)} %bitcast.8), channel_id=1, replica_groups=mesh['gx'=16,'gy'=8] {'gx','gy'}, dimensions={0} | all-to-all | bytes 1835008 | tf_op jit(solution)/shard_map/all_to_all | solution.py:280
  41.1 23.6 %crm.1 = f32[896,128]{1,0:T(8,128)} custom-call(f32[400,128]{1,0:T(8,128)S(1)} %get-tuple-element.25.const_ref, f32[1792,128]{1,0:T(8,128)S(1)} %bitcast.6, f32[3200,1792]{1,0:T(8,128)} %field_ref.1), custom_call_target="tpu_custom_call" | custom-call | tf_op jit(solution)/shard_map/crm/pallas_call | solution.py:258
  64.7 4.7 %all-to-all-start.1 = ((f32[128,1,896]{2,1,0:T(1,128)}), f32[128,1,896]{2,1,0:T(1,128)S(1)}, u32[]{:S(2)}, u32[]{:S(2)}) async-start(f32[128,1,896]{2,1,0:T(1,128)} %bitcast.3), calls=%async_computation.1 | async-start | bytes 917504 | tf_op jit(solution)/shard_map/all_to_all | solution.py:280
  69.4 0.0 copy-done.6
  69.4 0.1 copy.12.up_ref
  69.5 12.7 %all-to-all-done.1 = f32[128,1,896]{2,1,0:T(1,128)S(1)} async-done(((f32[128,1,896]{2,1,0:T(1,128)}), f32[128,1,896]{2,1,0:T(1,128)S(1)}, u32[]{:S(2)}, u32[]{:S(2)}) %all-to-all-start.1) | async-done | bytes 458784 | tf_op jit(solution)/shard_map/all_to_all | solution.py:280
  82.2 1.9 %final.1 = f32[1152,128]{1,0:T(8,128)} custom-call(f32[144,1024]{1,0:T(8,128)S(1)} %get-tuple-element.24.dyn_ref, f32[896,128]{1,0:T(8,128)S(1)} %bitcast.7, s32[1,1024]{1,0:T(1,128)S(1)} %get-tuple-element.17.slot_ref, f32[72,50]{1,0:T(8,128)S(1)} %copy.12.up_ref), custom_call_target="tpu_custom_call" | custom-call | tf_op jit(solution)/shard_map/final/pallas_call | solution.py:343
Async XLA Ops:
  0.0 1.1 %copy-start = (f32[144,8,128]{2,1,0:T(8,128)S(1)}, f32[144,8,128]{2,1,0:T(8,128)}, u32[]{:S(2)}) copy-start(f32[144,8,128]{2,1,0:T(8,128)} %param.8) | copy-start | bytes 1769476
  1.1 68.3 %copy-start.6 = (f32[72,50]{0,1:T(8,128)S(1)}, f32[72,50]{0,1:T(8,128)}, u32[]{:S(2)}) copy-start(f32[72,50]{0,1:T(8,128)} %param.13) | copy-start | bytes 43204
  1.5 14.0 %collective-permute-start = (f32[144,128]{1,0:T(8,128)S(1)}, f32[144,128]{1,0:T(8,128)S(1)}, u32[]{:S(2)}, u32[]{:S(2)}) collective-permute-start(f32[144,128]{1,0:T(8,128)S(1)} %get-tuple-element.20), channel_id=1, source_target_pairs={{0,8},{8,16},{16,24},{24,32},{32,40},{40,48},{48,56},{56,64},{64,7... | collective-permute-start | bytes 221192 | tf_op jit(solution)/shard_map/ppermute | solution.py:286
  4.0 11.5 %collective-permute-start.1 = (f32[144,128]{1,0:T(8,128)S(1)}, f32[144,128]{1,0:T(8,128)S(1)}, u32[]{:S(2)}, u32[]{:S(2)}) collective-permute-start(f32[144,128]{1,0:T(8,128)S(1)} %get-tuple-element.21), channel_id=1, source_target_pairs={{0,120},{8,0},{16,8},{24,16},{32,24},{40,32},{48,40},{56,48},{64,5... | collective-permute-start | bytes 221192 | tf_op jit(solution)/shard_map/ppermute | solution.py:286
  8.4 7.1 %collective-permute-start.2 = (f32[8,144]{1,0:T(8,128)S(1)}, f32[8,144]{1,0:T(8,128)S(1)}, u32[]{:S(2)}, u32[]{:S(2)}) collective-permute-start(f32[8,144]{1,0:T(8,128)S(1)} %get-tuple-element.22), channel_id=1, source_target_pairs={{0,1},{1,2},{2,3},{3,4},{4,5},{5,6},{6,7},{7,0},{8,9},{9,10},{10,1... | collective-permute-start | bytes 13832 | tf_op jit(solution)/shard_map/ppermute | solution.py:286
  10.5 5.0 %collective-permute-start.3 = (f32[8,144]{1,0:T(8,128)S(1)}, f32[8,144]{1,0:T(8,128)S(1)}, u32[]{:S(2)}, u32[]{:S(2)}) collective-permute-start(f32[8,144]{1,0:T(8,128)S(1)} %get-tuple-element.23), channel_id=1, source_target_pairs={{0,7},{1,0},{2,1},{3,2},{4,3},{5,4},{6,5},{7,6},{8,15},{9,8},{10,9... | collective-permute-start | bytes 13832 | tf_op jit(solution)/shard_map/ppermute | solution.py:286
  10.5 0.8 copy-start.1
  11.3 0.7 copy-start.2
  12.0 0.7 copy-start.3
  12.7 0.7 copy-start.4
  13.4 0.7 copy-start.5
  64.7 17.5 %all-to-all-start.1 = ((f32[128,1,896]{2,1,0:T(1,128)}), f32[128,1,896]{2,1,0:T(1,128)S(1)}, u32[]{:S(2)}, u32[]{:S(2)}) async-start(f32[128,1,896]{2,1,0:T(1,128)} %bitcast.3), calls=%async_computation.1 | async-start | bytes 917504 | tf_op jit(solution)/shard_map/all_to_all | solution.py:280

commit v3 on v2

--- a/solution.py
+++ b/solution.py
@@ -54,28 +54,11 @@
         east_ref[i:i + 1, :] = side[1:2]
 
 
-def local_kernel(
-    cap, state_ref, owner_hbm, counts_hbm, vert_hbm, courant_hbm, down_hbm,
-    base_ref, slot_ref, steps_ref, const_ref, down_ref,
-    owner_ref, counts_ref, vert_ref, courant_ref, sems,
-):
-    copies = [
-        pltpu.make_async_copy(src, dst, sems.at[i])
-        for i, (src, dst) in enumerate(
-            [
-                (owner_hbm, owner_ref),
-                (counts_hbm, counts_ref),
-                (vert_hbm, vert_ref),
-                (courant_hbm, courant_ref),
-                (down_hbm, down_ref),
-            ]
-        )
-    ]
-    for copy in copies:
-        copy.start()
+def local_kernel(cap, crm_z, state_ref, maps_ref, columns_ref, base_ref, slot_ref, steps_ref, const_ref):
     levels = base_ref.shape[0]
     half = levels // 2
-    crm_z = courant_ref.shape[0]
+    vert = maps_ref[:half, :half]
+    columns = columns_ref[...]
     wide = lax.broadcasted_iota(jnp.int32, (levels, LANES), 1)
     rows = [state_ref[pl.ds(i, levels, stride=SUBL), :] for i in range(SUBL)]
     laps = []
@@ -90,13 +73,10 @@
         laps.append(mid + DIFFUSION * (lap - 4.0 * mid))
     whole = jnp.concatenate(rows, axis=1)
     base = jnp.concatenate(laps, axis=1)
-    copies[2].wait()
-    vert = vert_ref[...]
     base_ref[:half, :] = base[:half] + dot3(vert, whole[:half])
     base_ref[half:, :] = base[half:] + dot3(vert, whole[half:])
 
-    copies[0].wait()
-    owner = jnp.concatenate([owner_ref[i:i + 1, :] for i in range(SUBL)], axis=1)
+    owner = jnp.concatenate([columns[i:i + 1, :] for i in range(SUBL)], axis=1)
     width = owner.shape[1]
     devices = LANES * (-(-DEVICES // LANES))
     mine = lax.broadcasted_iota(jnp.int32, (devices, width), 0) == owner
@@ -107,28 +87,26 @@
     before = dot(mine.astype(jnp.bfloat16), earlier)
     rank = jnp.sum(jnp.where(mine, before, 0.0), axis=0, keepdims=True).astype(jnp.int32)
     slot_ref[...] = owner * cap + rank
-    copies[1].wait()
-    counts = jnp.concatenate([counts_ref[i:i + 1, :] for i in range(SUBL)], axis=1)
+    counts = jnp.concatenate([columns[i:i + 1, :] for i in range(SUBL, 2 * SUBL)], axis=1)
     lead = (lax.broadcasted_iota(jnp.int32, (SUBL, width), 0) == 0).astype(jnp.float32)
     steps_ref[...] = lead * counts.astype(jnp.float32)
-    copies[3].wait()
-    row = lax.broadcasted_iota(jnp.int32, (SUBL, LANES), 0)
-    for z in range(crm_z):
-        c = courant_ref[z]
-        keep = 1.0 - c
-        part = jnp.where(row % 2 == 0, keep, c)
-        const_ref[SUBL * z:SUBL * (z + 1), :] = part * jnp.where(row < 2, BETA, jnp.where(row < 4, 1.0, 0.5))
-    copies[4].wait()
+    last = maps_ref.shape[0] - SUBL
+    line = jnp.broadcast_to(maps_ref[last:last + 1, :], (LANES, LANES))
+    c = line.T[:crm_z]
+    keep = 1.0 - c
+    for i, value in enumerate((BETA * keep, BETA * c, keep, c, 0.5 * keep, 0.5 * c)):
+        const_ref[pl.ds(i, crm_z, stride=SUBL), :] = value
 
 
 def send_kernel(
-    base_ref, slot_ref, steps_ref, down_ref, above_ref, below_ref, left_ref, right_ref,
+    crm_z, base_ref, slot_ref, steps_ref, maps_ref, above_ref, below_ref, left_ref, right_ref,
     dyn_ref, out_ref,
 ):
     levels, width = base_ref.shape
     half = levels // 2
-    crm_z = down_ref.shape[0]
     pad_z = -(-crm_z // SUBL) * SUBL
+    start = maps_ref.shape[0] - SUBL - pad_z
+    down = maps_ref[start:start + pad_z, :half]
     sides = jnp.concatenate([left_ref[...], right_ref[...]], axis=0)
     row = lax.broadcasted_iota(jnp.int32, (2 * SUBL, width), 0)
     lane = lax.broadcasted_iota(jnp.int32, (2 * SUBL, width), 1)
@@ -141,7 +119,6 @@
     halo = jnp.concatenate([first, halo[:, LANES:width - LANES], last], axis=1)
     dyn = base_ref[...] + DIFFUSION * halo
     dyn_ref[...] = dyn
-    down = jnp.concatenate([down_ref[...], jnp.zeros((pad_z - crm_z, half), jnp.float32)], axis=0)
     prof_t = dot3(down, dyn[:half])
     prof_q = dot3(down, dyn[half:])
     blank = jnp.zeros((LANES - 2 * pad_z - SUBL, width), jnp.float32)
@@ -235,7 +212,6 @@
 
 
 VMEM = pl.BlockSpec(memory_space=pltpu.VMEM)
-HBM = pl.BlockSpec(memory_space=pltpu.HBM)
 DEVICES = 128
 
 
@@ -281,6 +257,16 @@
     return got.reshape(value.shape)
 
 
+def stacked(values):
+    tall = [-(-value.shape[0] // SUBL) * SUBL for value in values]
+    parts, above = [], 0
+    for value, height in zip(values, tall):
+        below = sum(tall) - above - value.shape[0]
+        parts.append(jnp.pad(value, ((above, below), (0, LANES - value.shape[1]))))
+        above += height
+    return sum(parts[1:], parts[0])
+
+
 def shifted(value, axis, step):
     count = lax.axis_size(axis)
     return lax.ppermute(value, axis, [(i, (i + step) % count) for i in range(count)])
@@ -310,31 +296,26 @@
     left = shifted(east, "gy", 1)
     right = shifted(west, "gy", -1)
 
-    base, slot, steps, const, down = pl.pallas_call(
-        functools.partial(local_kernel, cap),
-        in_specs=[VMEM] + [HBM] * 5,
-        out_specs=[VMEM] * 5,
-        out_shape=[f32(rows, col_dev), i32(1, col_dev), f32(SUBL, col_dev), f32(SUBL * crm_z, LANES), f32(*down_map.shape)],
-        scratch_shapes=[
-            pltpu.VMEM(owner.shape, jnp.int32),
-            pltpu.VMEM(counts.shape, jnp.int32),
-            pltpu.VMEM(vert.shape, jnp.float32),
-            pltpu.SMEM(courant.shape, jnp.float32),
-            pltpu.SemaphoreType.DMA((5,)),
-        ],
+    maps = stacked([vert, down_map, courant[None]])
+    columns = stacked([owner, counts])
+    base, slot, steps, const = pl.pallas_call(
+        functools.partial(local_kernel, cap, crm_z),
+        in_specs=[VMEM] * 3,
+        out_specs=[VMEM] * 4,
+        out_shape=[f32(rows, col_dev), i32(1, col_dev), f32(SUBL, col_dev), f32(SUBL * crm_z, LANES)],
         compiler_params=params(),
         cost_estimate=pl.CostEstimate(flops=10**9, bytes_accessed=4 * 10**6, transcendentals=0),
         name="local",
-    )(flat, owner, counts, vert, courant, down_map)
+    )(flat, maps, columns)
 
     dyn, outgoing = pl.pallas_call(
-        send_kernel,
+        functools.partial(send_kernel, crm_z),
         in_specs=[VMEM] * 8,
         out_specs=[VMEM] * 2,
         out_shape=[f32(rows, col_dev), f32(slots, LANES)],
         compiler_params=params(),
         name="send",
-    )(base, slot, steps, down, above, below, left, right)
+    )(base, slot, steps, maps, above, below, left, right)
 
     arrived = exchange(outgoing, devices)
     change = crm(const, arrived, crm_field, crm_z, crm_x)

time: 84.6 us -> 83.2 us (0.983)
  local copies, waits for them, and re-layouts: 4.7 us -> 1.15 us
  other arithmetic: 0 us -> 1.51 us
    unnamed x15 -> x5, local copies, waits for them, and re-layouts: 4.7 us -> 1.15 us
    add x0 -> x2, other arithmetic: none -> 1.51 us  [stacked(): return sum(parts[1:], parts[0])]
  transfers between devices with their start and end apart: 5 -> 5, of which waited for: 1 -> 2; matrix products, arithmetic and copies ran while one was open for 0% -> 2% of each run, Pallas kernels for 2% -> 1%
where the time goes in v3:
time: 83.2 us; the launch traced here: 82.8 us
  Pallas kernels  28.6 us (34%)
  blocking collectives  24.4 us (29%)
  starting transfers between devices  13.7 us (16%)
  waiting for transfers between devices  13.4 us (16%)
  other arithmetic  1.51 us (2%)
  local copies, waits for them, and re-layouts  1.15 us (1%)
    all_to_all x1, blocking collectives, exchange(): lax.all_to_all(sent, ('gx', 'gy'), split_axis=0, concat_axis=0, tiled=True)  24.4 us
    pallas_call x1, Pallas kernels, crm(): pl.pallas_call(functools.partial(crm_kernel, crm_z, crm_x), grid=(slots /...  23.6 us
    all_to_all x1, waiting for transfers between devices, exchange(): lax.all_to_all(sent, ('gx', 'gy'), split_axis=0, concat_axis=0, tiled=True)  12.7 us
    ppermute x4, starting transfers between devices, shifted(): lax.ppermute(value, axis, [(i, (i + step) % count) for i in range(count)])  9.02 us
    all_to_all x1, starting transfers between devices, exchange(): lax.all_to_all(sent, ('gx', 'gy'), split_axis=0, concat_axis=0, tiled=True)  4.69 us
    pallas_call x1, Pallas kernels, body(): pl.pallas_call(final_kernel, in_specs=[VMEM] * 4, out_specs=VMEM, out_sha...  1.91 us
    pallas_call x1, Pallas kernels, body(): pl.pallas_call(functools.partial(send_kernel, crm_z), in_specs=[VMEM] * 8...  1.8 us
  transfers between devices with their start and end apart: 5, of which 2 were waited for; matrix products, arithmetic and copies ran while one was open for 2% of the time, Pallas kernels for 1%

profile of v3, /device:TPU:1, one launch (start us, length us, event | category | flops | bytes accessed | tf_op | source)
XLA Modules:
  0.0 82.8 jit_solution(3816749603732710964)
XLA Ops:
  0.0 0.0 copy-start
  0.0 1.1 %copy-done = f32[144,8,128]{2,1,0:T(8,128)S(1)} copy-done((f32[144,8,128]{2,1,0:T(8,128)S(1)}, f32[144,8,128]{2,1,0:T(8,128)}, u32[]{:S(2)}) %copy-start) | copy-done | bytes 589848
  1.1 0.0 copy-start.1
  1.1 0.4 edges.1
  1.5 2.5 %collective-permute-start = (f32[144,128]{1,0:T(8,128)S(1)}, f32[144,128]{1,0:T(8,128)S(1)}, u32[]{:S(2)}, u32[]{:S(2)}) collective-permute-start(f32[144,128]{1,0:T(8,128)S(1)} %get-tuple-element.18), channel_id=1, source_target_pairs={{0,8},{8,16},{16,24},{24,32},{32,40},{40,48},{48,56},{56,64},{64,7... | collective-permute-start | bytes 221192 | tf_op jit(solution)/shard_map/ppermute | solution.py:272
  4.0 4.4 %collective-permute-start.1 = (f32[144,128]{1,0:T(8,128)S(1)}, f32[144,128]{1,0:T(8,128)S(1)}, u32[]{:S(2)}, u32[]{:S(2)}) collective-permute-start(f32[144,128]{1,0:T(8,128)S(1)} %get-tuple-element.19), channel_id=1, source_target_pairs={{0,120},{8,0},{16,8},{24,16},{32,24},{40,32},{48,40},{56,48},{64,5... | collective-permute-start | bytes 221192 | tf_op jit(solution)/shard_map/ppermute | solution.py:272
  8.4 2.1 %collective-permute-start.2 = (f32[8,144]{1,0:T(8,128)S(1)}, f32[8,144]{1,0:T(8,128)S(1)}, u32[]{:S(2)}, u32[]{:S(2)}) collective-permute-start(f32[8,144]{1,0:T(8,128)S(1)} %get-tuple-element.20), channel_id=1, source_target_pairs={{0,1},{1,2},{2,3},{3,4},{4,5},{5,6},{6,7},{7,0},{8,9},{9,10},{10,1... | collective-permute-start | bytes 13832 | tf_op jit(solution)/shard_map/ppermute | solution.py:272
  10.5 0.0 collective-permute-start.3
  10.5 0.7 pad_add_fusion.1.columns_ref
  11.2 0.8 pad_add_fusion.maps_ref
  12.0 0.9 %local.1 = (f32[144,1024]{1,0:T(8,128)S(1)}, s32[1,1024]{1,0:T(1,128)S(1)}, f32[8,1024]{1,0:T(8,128)S(1)}, f32[400,128]{1,0:T(8,128)S(1)}) custom-call(f32[1152,128]{1,0:T(8,128)S(1)} %bitcast.11, f32[136,128]{1,0:T(8,128)S(1)} %pad_add_fusion.maps_ref, s32[16,128]{1,0:T(8,128)S(1)} %pad_add_fusion.1.columns_ref), custom_call_target="tpu_custom_call" | custom-call | flops 1000000000 | bytes 4000000 | tf_op jit(solution)/shard_map/local/pallas_call | solution.py:301
  12.9 0.0 collective-permute-done.2.left_ref
  13.0 0.6 collective-permute-done.3.right_ref
  13.6 0.0 collective-permute-done.above_ref
  13.6 0.0 collective-permute-done.1.below_ref
  13.6 1.8 %send.1 = (f32[144,1024]{1,0:T(8,128)S(1)}, f32[1792,128]{1,0:T(8,128)S(1)}) custom-call(f32[144,1024]{1,0:T(8,128)S(1)} %get-tuple-element.15.base_ref, s32[1,1024]{1,0:T(1,128)S(1)} %get-tuple-element.16.slot_ref, f32[8,1024]{1,0:T(8,128)S(1)} %get-tuple-element.17.steps_ref, f32[136,128]{1,0:T(8,128)S(1)} %pad_add_fusion.maps_ref, ...), custom_call_target="tpu_custom_call" | custom-call | tf_op jit(solution)/shard_map/send/pallas_call | solution.py:311
  15.4 24.4 %all_to_all.10 = f32[128,1,1792]{2,1,0:T(1,128)S(1)} all-to-all(f32[128,1,1792]{2,1,0:T(1,128)S(1)} %bitcast.9), channel_id=1, replica_groups=mesh['gx'=16,'gy'=8] {'gx','gy'}, dimensions={0} | all-to-all | bytes 1835008 | tf_op jit(solution)/shard_map/all_to_all | solution.py:256
  39.8 23.6 %crm.1 = f32[896,128]{1,0:T(8,128)} custom-call(f32[400,128]{1,0:T(8,128)S(1)} %get-tuple-element.23.const_ref, f32[1792,128]{1,0:T(8,128)S(1)} %bitcast.7, f32[3200,1792]{1,0:T(8,128)} %field_ref.1), custom_call_target="tpu_custom_call" | custom-call | tf_op jit(solution)/shard_map/crm/pallas_call | solution.py:234
  63.4 4.7 %all-to-all-start.1 = ((f32[128,1,896]{2,1,0:T(1,128)}), f32[128,1,896]{2,1,0:T(1,128)S(1)}, u32[]{:S(2)}, u32[]{:S(2)}) async-start(f32[128,1,896]{2,1,0:T(1,128)} %bitcast.4), calls=%async_computation.1 | async-start | bytes 917504 | tf_op jit(solution)/shard_map/all_to_all | solution.py:256
  68.1 0.0 copy-done.1
  68.1 0.1 copy.12.up_ref
  68.2 12.7 %all-to-all-done.1 = f32[128,1,896]{2,1,0:T(1,128)S(1)} async-done(((f32[128,1,896]{2,1,0:T(1,128)}), f32[128,1,896]{2,1,0:T(1,128)S(1)}, u32[]{:S(2)}, u32[]{:S(2)}) %all-to-all-start.1) | async-done | bytes 458784 | tf_op jit(solution)/shard_map/all_to_all | solution.py:256
  80.9 1.9 %final.1 = f32[1152,128]{1,0:T(8,128)} custom-call(f32[144,1024]{1,0:T(8,128)S(1)} %get-tuple-element.22.dyn_ref, f32[896,128]{1,0:T(8,128)S(1)} %bitcast.8, s32[1,1024]{1,0:T(1,128)S(1)} %get-tuple-element.16.slot_ref, f32[72,50]{1,0:T(8,128)S(1)} %copy.12.up_ref), custom_call_target="tpu_custom_call" | custom-call | tf_op jit(solution)/shard_map/final/pallas_call | solution.py:324
Async XLA Ops:
  0.0 1.1 %copy-start = (f32[144,8,128]{2,1,0:T(8,128)S(1)}, f32[144,8,128]{2,1,0:T(8,128)}, u32[]{:S(2)}) copy-start(f32[144,8,128]{2,1,0:T(8,128)} %param.8) | copy-start | bytes 1769476
  1.1 67.0 %copy-start.1 = (f32[72,50]{0,1:T(8,128)S(1)}, f32[72,50]{0,1:T(8,128)}, u32[]{:S(2)}) copy-start(f32[72,50]{0,1:T(8,128)} %param.13) | copy-start | bytes 43204
  1.5 12.1 %collective-permute-start = (f32[144,128]{1,0:T(8,128)S(1)}, f32[144,128]{1,0:T(8,128)S(1)}, u32[]{:S(2)}, u32[]{:S(2)}) collective-permute-start(f32[144,128]{1,0:T(8,128)S(1)} %get-tuple-element.18), channel_id=1, source_target_pairs={{0,8},{8,16},{16,24},{24,32},{32,40},{40,48},{48,56},{56,64},{64,7... | collective-permute-start | bytes 221192 | tf_op jit(solution)/shard_map/ppermute | solution.py:272
  4.0 9.6 %collective-permute-start.1 = (f32[144,128]{1,0:T(8,128)S(1)}, f32[144,128]{1,0:T(8,128)S(1)}, u32[]{:S(2)}, u32[]{:S(2)}) collective-permute-start(f32[144,128]{1,0:T(8,128)S(1)} %get-tuple-element.19), channel_id=1, source_target_pairs={{0,120},{8,0},{16,8},{24,16},{32,24},{40,32},{48,40},{56,48},{64,5... | collective-permute-start | bytes 221192 | tf_op jit(solution)/shard_map/ppermute | solution.py:272
  8.4 4.6 %collective-permute-start.2 = (f32[8,144]{1,0:T(8,128)S(1)}, f32[8,144]{1,0:T(8,128)S(1)}, u32[]{:S(2)}, u32[]{:S(2)}) collective-permute-start(f32[8,144]{1,0:T(8,128)S(1)} %get-tuple-element.20), channel_id=1, source_target_pairs={{0,1},{1,2},{2,3},{3,4},{4,5},{5,6},{6,7},{7,0},{8,9},{9,10},{10,1... | collective-permute-start | bytes 13832 | tf_op jit(solution)/shard_map/ppermute | solution.py:272
  10.5 3.1 %collective-permute-start.3 = (f32[8,144]{1,0:T(8,128)S(1)}, f32[8,144]{1,0:T(8,128)S(1)}, u32[]{:S(2)}, u32[]{:S(2)}) collective-permute-start(f32[8,144]{1,0:T(8,128)S(1)} %get-tuple-element.21), channel_id=1, source_target_pairs={{0,7},{1,0},{2,1},{3,2},{4,3},{5,4},{6,5},{7,6},{8,15},{9,8},{10,9... | collective-permute-start | bytes 13832 | tf_op jit(solution)/shard_map/ppermute | solution.py:272
  63.4 17.5 %all-to-all-start.1 = ((f32[128,1,896]{2,1,0:T(1,128)}), f32[128,1,896]{2,1,0:T(1,128)S(1)}, u32[]{:S(2)}, u32[]{:S(2)}) async-start(f32[128,1,896]{2,1,0:T(1,128)} %bitcast.4), calls=%async_computation.1 | async-start | bytes 917504 | tf_op jit(solution)/shard_map/all_to_all | solution.py:256

commit v4 on v3

--- a/solution.py
+++ b/solution.py
@@ -54,11 +54,10 @@
         east_ref[i:i + 1, :] = side[1:2]
 
 
-def local_kernel(cap, crm_z, state_ref, maps_ref, columns_ref, base_ref, slot_ref, steps_ref, const_ref):
+def local_kernel(cap, crm_z, state_ref, small_ref, base_ref, slot_ref, steps_ref, const_ref):
     levels = base_ref.shape[0]
     half = levels // 2
-    vert = maps_ref[:half, :half]
-    columns = columns_ref[...]
+    vert = small_ref[2 * SUBL:2 * SUBL + half, :half]
     wide = lax.broadcasted_iota(jnp.int32, (levels, LANES), 1)
     rows = [state_ref[pl.ds(i, levels, stride=SUBL), :] for i in range(SUBL)]
     laps = []
@@ -76,7 +75,7 @@
     base_ref[:half, :] = base[:half] + dot3(vert, whole[:half])
     base_ref[half:, :] = base[half:] + dot3(vert, whole[half:])
 
-    owner = jnp.concatenate([columns[i:i + 1, :] for i in range(SUBL)], axis=1)
+    owner = jnp.concatenate([small_ref[i:i + 1, :] for i in range(SUBL)], axis=1).astype(jnp.int32)
     width = owner.shape[1]
     devices = LANES * (-(-DEVICES // LANES))
     mine = lax.broadcasted_iota(jnp.int32, (devices, width), 0) == owner
@@ -87,11 +86,11 @@
     before = dot(mine.astype(jnp.bfloat16), earlier)
     rank = jnp.sum(jnp.where(mine, before, 0.0), axis=0, keepdims=True).astype(jnp.int32)
     slot_ref[...] = owner * cap + rank
-    counts = jnp.concatenate([columns[i:i + 1, :] for i in range(SUBL, 2 * SUBL)], axis=1)
+    counts = jnp.concatenate([small_ref[i:i + 1, :] for i in range(SUBL, 2 * SUBL)], axis=1)
     lead = (lax.broadcasted_iota(jnp.int32, (SUBL, width), 0) == 0).astype(jnp.float32)
-    steps_ref[...] = lead * counts.astype(jnp.float32)
-    last = maps_ref.shape[0] - SUBL
-    line = jnp.broadcast_to(maps_ref[last:last + 1, :], (LANES, LANES))
+    steps_ref[...] = lead * counts
+    last = small_ref.shape[0] - SUBL
+    line = jnp.broadcast_to(small_ref[last:last + 1, :], (LANES, LANES))
     c = line.T[:crm_z]
     keep = 1.0 - c
     for i, value in enumerate((BETA * keep, BETA * c, keep, c, 0.5 * keep, 0.5 * c)):
@@ -99,14 +98,14 @@
 
 
 def send_kernel(
-    crm_z, base_ref, slot_ref, steps_ref, maps_ref, above_ref, below_ref, left_ref, right_ref,
+    crm_z, base_ref, slot_ref, steps_ref, small_ref, above_ref, below_ref, left_ref, right_ref,
     dyn_ref, out_ref,
 ):
     levels, width = base_ref.shape
     half = levels // 2
     pad_z = -(-crm_z // SUBL) * SUBL
-    start = maps_ref.shape[0] - SUBL - pad_z
-    down = maps_ref[start:start + pad_z, :half]
+    start = small_ref.shape[0] - SUBL - pad_z
+    down = small_ref[start:start + pad_z, :half]
     sides = jnp.concatenate([left_ref[...], right_ref[...]], axis=0)
     row = lax.broadcasted_iota(jnp.int32, (2 * SUBL, width), 0)
     lane = lax.broadcasted_iota(jnp.int32, (2 * SUBL, width), 1)
@@ -126,7 +125,7 @@
     p_hi, p_lo = split(payload)
     both = jnp.concatenate([p_hi, p_lo], axis=0)
     slot = slot_ref[...]
-    chunk = 256
+    chunk = out_ref.shape[0] // 2
     for start in range(0, out_ref.shape[0], chunk):
         ids = start + lax.broadcasted_iota(jnp.int32, (chunk, width), 0)
         sent = dot((ids == slot).astype(jnp.bfloat16), both, NT)
@@ -145,25 +144,57 @@
     return [stay * v + m for v, m in zip(values, [last] + moved[:-1])]
 
 
-def crm_kernel(crm_z, crm_x, const_ref, arrived_ref, field_ref, out_ref, prof_ref, part_ref, turn_ref):
+def spread(ref, row):
+    return jnp.broadcast_to(ref[pl.ds(row, 1), :], (SUBL, LANES))
+
+
+def crm_kernel(
+    crm_z, crm_x, blocks, const_ref, arrived_ref, field_hbm, out_ref,
+    prof_ref, weight_ref, part_ref, turn_ref, buffers, sems,
+):
     pad_z = -(-crm_z // SUBL) * SUBL
     quads = crm_x // SUBL
-    cols = arrived_ref[...].T
-    prof_ref[:pad_z, :] = BETA * cols[:pad_z] + SHIFT
-    prof_ref[pad_z:2 * pad_z, :] = BETA * cols[pad_z:2 * pad_z]
-    counts = jnp.broadcast_to(cols[2 * pad_z:2 * pad_z + 1], (SUBL, LANES))
-    part = jnp.where(counts > 3.0, 0.0625, jnp.where(counts > 2.0, 0.125, jnp.where(counts > 1.0, 0.25, 0.5)))
+    half = LANES // 2
+    block = pl.program_id(0)
     scale = 2.0 * CONDENSE / (BETA * crm_x)
-    w_first = (1.0 - part) * scale
-    w_kept = [jnp.where(counts > float(k), part * (-scale * 2.0**k), 0.0) for k in range(S_MAX)]
-
-    def spread(ref, row):
-        return jnp.broadcast_to(ref[pl.ds(row, 1), :], (SUBL, LANES))
-
+
+    def rows_of(index, size):
+        return pl.ds(pl.multiple_of(index * size, SUBL), size)
+
+    def fetch(i):
+        lanes = pl.ds(pl.multiple_of(i * LANES, LANES), LANES)
+        side = lax.rem(i, 2)
+        return pltpu.make_async_copy(field_hbm.at[:, lanes], buffers.at[side], sems.at[side])
+
+    @pl.when(block == 0)
+    def _():
+        fetch(block).start()
+
+        def unpack(i, carry):
+            cols = arrived_ref[rows_of(i, LANES), :].T
+            prof_ref[rows_of(2 * i, pad_z), :] = BETA * cols[:pad_z] + SHIFT
+            prof_ref[rows_of(2 * i + 1, pad_z), :] = BETA * cols[pad_z:2 * pad_z]
+            counts = cols[2 * pad_z:2 * pad_z + 1]
+            part = jnp.where(counts > 3.0, 0.0625, jnp.where(counts > 2.0, 0.125, jnp.where(counts > 1.0, 0.25, 0.5)))
+            weights = [(1.0 - part) * scale]
+            weights += [jnp.where(counts > float(k), part * (-scale * 2.0**k), 0.0) for k in range(S_MAX)]
+            weights += [jnp.zeros((SUBL - len(weights), LANES), jnp.float32)]
+            weight_ref[rows_of(i, SUBL), :] = jnp.concatenate(weights, axis=0)
+            return carry
+
+        lax.fori_loop(0, blocks, unpack, 0, unroll=True)
+
+    @pl.when(block + 1 < blocks)
+    def _():
+        fetch(block + 1).start()
+
+    fetch(block).wait()
+    field_ref = buffers.at[lax.rem(block, 2)]
+    w_first, *w_kept = [spread(weight_ref, SUBL * block + i) for i in range(S_MAX + 1)]
     for z in range(crm_z):
         beta_keep, beta_c, keep, c, half_keep, half_c = [spread(const_ref, SUBL * z + i) for i in range(6)]
-        base_t = spread(prof_ref, z)
-        base_q = spread(prof_ref, pad_z + z)
+        base_t = spread(prof_ref, 2 * pad_z * block + z)
+        base_q = spread(prof_ref, 2 * pad_z * block + pad_z + z)
         temper = [field_ref[pl.ds(z * crm_x + i, SUBL, stride=quads), :] for i in range(quads)]
         vapour = [field_ref[pl.ds((crm_z + z) * crm_x + i, SUBL, stride=quads), :] for i in range(quads)]
         temper = [t + base_t for t in advect(temper, beta_keep, beta_c)]
@@ -179,19 +210,30 @@
             gone = gone + w_kept[k] * total(kept)
             if k < S_MAX - 1:
                 vapour = [v + e for v, e in zip(vapour, kept)]
-        part_ref[SUBL * z:SUBL * (z + 1), :] = gone
-    part_ref[SUBL * crm_z:, :] = jnp.zeros((SUBL * (LANES // 2 - crm_z), LANES), jnp.float32)
-    change = part_ref[pl.ds(0, LANES // 2, stride=SUBL), :]
-    for i in range(1, SUBL):
-        change = change + part_ref[pl.ds(i, LANES // 2, stride=SUBL), :]
-    turn_ref[...] = jnp.concatenate([change, change], axis=0).T
-    lane = lax.broadcasted_iota(jnp.int32, (LANES // 2, LANES), 1)
-    even = turn_ref[pl.ds(0, LANES // 2, stride=2), :]
-    odd = turn_ref[pl.ds(1, LANES // 2, stride=2), :]
-    out_ref[...] = jnp.where(lane < LANES // 2, even, odd)
-
-
-def final_kernel(dyn_ref, returned_ref, slot_ref, up_ref, out_ref):
+        part_ref[pl.ds(pl.multiple_of(SUBL * (pad_z * block + z), SUBL), SUBL), :] = gone
+
+    @pl.when(block == blocks - 1)
+    def _():
+        lane = lax.broadcasted_iota(jnp.int32, (half, LANES), 1)
+        level = lax.broadcasted_iota(jnp.int32, (half, LANES), 0)
+
+        def pack(i, carry):
+            start = i * (SUBL * pad_z)
+            change = part_ref[pl.ds(start, pad_z, stride=SUBL), :]
+            for j in range(1, SUBL):
+                change = change + part_ref[pl.ds(start + j, pad_z, stride=SUBL), :]
+            change = jnp.concatenate([change, jnp.zeros((half - pad_z, LANES), jnp.float32)], axis=0)
+            change = jnp.where(level < crm_z, change, 0.0)
+            turn_ref[rows_of(i, LANES), :] = jnp.concatenate([change, change], axis=0).T
+            even = turn_ref[pl.ds(i * LANES, half, stride=2), :]
+            odd = turn_ref[pl.ds(i * LANES + 1, half, stride=2), :]
+            out_ref[rows_of(i, half), :] = jnp.where(lane < half, even, odd)
+            return carry
+
+        lax.fori_loop(0, blocks, pack, 0, unroll=True)
+
+
+def final_kernel(dyn_ref, returned_ref, slot_ref, up_ref, out_hbm, out_ref, sems):
     half, crm_z = up_ref.shape
     slot = slot_ref[...]
     width = slot.shape[1]
@@ -205,10 +247,15 @@
     change = jnp.where(slot % 2 == 0, got[:LANES // 2], got[LANES // 2:])
     up = jnp.concatenate([up_ref[...], jnp.zeros((half, LANES // 2 - crm_z), jnp.float32)], axis=1)
     tend = dot3(up, change)
-    for i in range(SUBL):
-        cols = slice(i * LANES, (i + 1) * LANES)
-        out_ref[pl.ds(i, half, stride=SUBL), :] = dyn_ref[:half, cols] + tend[:, cols]
-        out_ref[pl.ds(SUBL * half + i, half, stride=SUBL), :] = dyn_ref[half:, cols] - tend[:, cols]
+    copies = []
+    for v, new in enumerate((dyn_ref[:half, :] + tend, dyn_ref[half:, :] - tend)):
+        for i in range(SUBL):
+            out_ref[pl.ds(v * SUBL * half + i, half, stride=SUBL), :] = new[:, i * LANES:(i + 1) * LANES]
+        rows = pl.ds(v * SUBL * half, SUBL * half)
+        copies.append(pltpu.make_async_copy(out_ref.at[rows, :], out_hbm.at[rows, :], sems.at[v]))
+        copies[-1].start()
+    for copy in copies:
+        copy.wait()
 
 
 VMEM = pl.BlockSpec(memory_space=pltpu.VMEM)
@@ -230,21 +277,21 @@
 def crm(const, arrived, crm_field, crm_z, crm_x):
     slots = arrived.shape[0]
     rows = crm_field.shape[0]
+    blocks = slots // LANES
     pad_z = -(-crm_z // SUBL) * SUBL
     return pl.pallas_call(
-        functools.partial(crm_kernel, crm_z, crm_x),
-        grid=(slots // LANES,),
-        in_specs=[
-            VMEM,
-            pl.BlockSpec((LANES, LANES), lambda b: (b, 0)),
-            pl.BlockSpec((rows, LANES), lambda b: (0, b)),
-        ],
-        out_specs=pl.BlockSpec((LANES // 2, LANES), lambda b: (b, 0)),
+        functools.partial(crm_kernel, crm_z, crm_x, blocks),
+        grid=(blocks,),
+        in_specs=[VMEM, VMEM, pl.BlockSpec(memory_space=pl.ANY)],
+        out_specs=VMEM,
         out_shape=f32(slots // 2, LANES),
         scratch_shapes=[
-            pltpu.VMEM((2 * pad_z, LANES), jnp.float32),
-            pltpu.VMEM((SUBL * LANES // 2, LANES), jnp.float32),
-            pltpu.VMEM((LANES, LANES), jnp.float32),
+            pltpu.VMEM((blocks * 2 * pad_z, LANES), jnp.float32),
+            pltpu.VMEM((blocks * SUBL, LANES), jnp.float32),
+            pltpu.VMEM((blocks * SUBL * pad_z, LANES), jnp.float32),
+            pltpu.VMEM((slots, LANES), jnp.float32),
+            pltpu.VMEM((2, rows, LANES), jnp.float32),
+            pltpu.SemaphoreType.DMA((2,)),
         ],
         compiler_params=params(48),
         name="crm",
@@ -257,14 +304,16 @@
     return got.reshape(value.shape)
 
 
-def stacked(values):
+def stacked(whole, real):
+    values = [*whole, *real]
     tall = [-(-value.shape[0] // SUBL) * SUBL for value in values]
     parts, above = [], 0
     for value, height in zip(values, tall):
         below = sum(tall) - above - value.shape[0]
         parts.append(jnp.pad(value, ((above, below), (0, LANES - value.shape[1]))))
         above += height
-    return sum(parts[1:], parts[0])
+    count = len(whole)
+    return sum(parts[1:count], parts[0]).astype(jnp.float32) + sum(parts[count + 1:], parts[count])
 
 
 def shifted(value, axis, step):
@@ -296,17 +345,16 @@
     left = shifted(east, "gy", 1)
     right = shifted(west, "gy", -1)
 
-    maps = stacked([vert, down_map, courant[None]])
-    columns = stacked([owner, counts])
+    small = stacked([owner, counts], [vert, down_map, courant[None]])
     base, slot, steps, const = pl.pallas_call(
         functools.partial(local_kernel, cap, crm_z),
-        in_specs=[VMEM] * 3,
+        in_specs=[VMEM] * 2,
         out_specs=[VMEM] * 4,
         out_shape=[f32(rows, col_dev), i32(1, col_dev), f32(SUBL, col_dev), f32(SUBL * crm_z, LANES)],
         compiler_params=params(),
         cost_estimate=pl.CostEstimate(flops=10**9, bytes_accessed=4 * 10**6, transcendentals=0),
         name="local",
-    )(flat, maps, columns)
+    )(flat, small)
 
     dyn, outgoing = pl.pallas_call(
         functools.partial(send_kernel, crm_z),
@@ -315,7 +363,7 @@
         out_shape=[f32(rows, col_dev), f32(slots, LANES)],
         compiler_params=params(),
         name="send",
-    )(base, slot, steps, maps, above, below, left, right)
+    )(base, slot, steps, small, above, below, left, right)
 
     arrived = exchange(outgoing, devices)
     change = crm(const, arrived, crm_field, crm_z, crm_x)
@@ -324,8 +372,12 @@
     out = pl.pallas_call(
         final_kernel,
         in_specs=[VMEM] * 4,
-        out_specs=VMEM,
+        out_specs=pl.BlockSpec(memory_space=pl.ANY),
         out_shape=f32(rows * width_x, width_y),
+        scratch_shapes=[
+            pltpu.VMEM((rows * width_x, width_y), jnp.float32),
+            pltpu.SemaphoreType.DMA((2,)),
+        ],
         compiler_params=params(),
         name="final",
     )(dyn, returned, slot, up_map)

time: 83.2 us -> 82 us (0.986)
  Pallas kernels: 28.6 us -> 27.1 us
    pallas_call x2, Pallas kernels: 25.5 us -> 24 us  [the longest x1 22.1 us: crm(): pl.pallas_call(functools.partial(crm_kernel, crm_z, crm_x, blocks), grid=...]
  transfers between devices with their start and end apart: 5 -> 5, of which waited for: 2 -> 2; matrix products, arithmetic and copies ran while one was open for 2% -> 1% of each run, Pallas kernels for 1% -> 1%
where the time goes in v4:
time: 82 us; the launch traced here: 81.4 us
  Pallas kernels  27.1 us (33%)
  blocking collectives  24.4 us (30%)
  waiting for transfers between devices  14.1 us (17%)
  starting transfers between devices  13.7 us (17%)
  local copies, waits for them, and re-layouts  1.15 us (1%)
  other arithmetic  0.83 us (1%)
    all_to_all x1, blocking collectives, exchange(): lax.all_to_all(sent, ('gx', 'gy'), split_axis=0, concat_axis=0, tiled=True)  24.4 us
    pallas_call x1, Pallas kernels, crm(): pl.pallas_call(functools.partial(crm_kernel, crm_z, crm_x, blocks), grid=...  22.1 us
    all_to_all x1, waiting for transfers between devices, exchange(): lax.all_to_all(sent, ('gx', 'gy'), split_axis=0, concat_axis=0, tiled=True)  12.8 us
    ppermute x4, starting transfers between devices, shifted(): lax.ppermute(value, axis, [(i, (i + step) % count) for i in range(count)])  9.02 us
    all_to_all x1, starting transfers between devices, exchange(): lax.all_to_all(sent, ('gx', 'gy'), split_axis=0, concat_axis=0, tiled=True)  4.69 us
    pallas_call x1, Pallas kernels, body(): pl.pallas_call(final_kernel, in_specs=[VMEM] * 4, out_specs=pl.BlockSpec(...  1.9 us
    pallas_call x1, Pallas kernels, body(): pl.pallas_call(functools.partial(send_kernel, crm_z), in_specs=[VMEM] * 8...  1.8 us
  transfers between devices with their start and end apart: 5, of which 2 were waited for; matrix products, arithmetic and copies ran while one was open for 1% of the time, Pallas kernels for 1%

profile of v4, /device:TPU:1, one launch (start us, length us, event | category | flops | bytes accessed | tf_op | source)
XLA Modules:
  0.0 81.4 jit_solution(12271122267416365125)
XLA Ops:
  0.0 0.0 copy-start
  0.0 1.1 %copy-done = f32[144,8,128]{2,1,0:T(8,128)S(1)} copy-done((f32[144,8,128]{2,1,0:T(8,128)S(1)}, f32[144,8,128]{2,1,0:T(8,128)}, u32[]{:S(2)}) %copy-start) | copy-done | bytes 589848
  1.1 0.0 copy-start.1
  1.1 0.4 edges.1
  1.5 2.5 %collective-permute-start = (f32[144,128]{1,0:T(8,128)S(1)}, f32[144,128]{1,0:T(8,128)S(1)}, u32[]{:S(2)}, u32[]{:S(2)}) collective-permute-start(f32[144,128]{1,0:T(8,128)S(1)} %get-tuple-element.18), channel_id=1, source_target_pairs={{0,8},{8,16},{16,24},{24,32},{32,40},{40,48},{48,56},{56,64},{64,7... | collective-permute-start | bytes 221192 | tf_op jit(solution)/shard_map/ppermute | solution.py:321
  4.0 4.4 %collective-permute-start.1 = (f32[144,128]{1,0:T(8,128)S(1)}, f32[144,128]{1,0:T(8,128)S(1)}, u32[]{:S(2)}, u32[]{:S(2)}) collective-permute-start(f32[144,128]{1,0:T(8,128)S(1)} %get-tuple-element.19), channel_id=1, source_target_pairs={{0,120},{8,0},{16,8},{24,16},{32,24},{40,32},{48,40},{56,48},{64,5... | collective-permute-start | bytes 221192 | tf_op jit(solution)/shard_map/ppermute | solution.py:321
  8.4 2.1 %collective-permute-start.2 = (f32[8,144]{1,0:T(8,128)S(1)}, f32[8,144]{1,0:T(8,128)S(1)}, u32[]{:S(2)}, u32[]{:S(2)}) collective-permute-start(f32[8,144]{1,0:T(8,128)S(1)} %get-tuple-element.20), channel_id=1, source_target_pairs={{0,1},{1,2},{2,3},{3,4},{4,5},{5,6},{6,7},{7,0},{8,9},{9,10},{10,1... | collective-permute-start | bytes 13832 | tf_op jit(solution)/shard_map/ppermute | solution.py:321
  10.5 0.0 collective-permute-start.3
  10.5 0.8 %add_add_fusion.small_ref = f32[152,128]{1,0:T(8,128)S(1)} fusion(f32[1,50]{1,0:T(1,128)} %bitcast.12, f32[50,72]{1,0:T(8,128)} %param.12, f32[72,72]{1,0:T(8,128)} %param.11, s32[8,128]{1,0:T(8,128)} %param.10, s32[8,128]{1,0:T(8,128)} %param.9), kind=kLoop, calls=%fused_computation | loop fusion | flops 97280 | bytes 121352 | tf_op jit(solution)/shard_map/add | solution.py:316
  11.3 0.9 %local.1 = (f32[144,1024]{1,0:T(8,128)S(1)}, s32[1,1024]{1,0:T(1,128)S(1)}, f32[8,1024]{1,0:T(8,128)S(1)}, f32[400,128]{1,0:T(8,128)S(1)}) custom-call(f32[1152,128]{1,0:T(8,128)S(1)} %bitcast.11, f32[152,128]{1,0:T(8,128)S(1)} %add_add_fusion.small_ref), custom_call_target="tpu_custom_call" | custom-call | flops 1000000000 | bytes 4000000 | tf_op jit(solution)/shard_map/local/pallas_call | solution.py:349
  12.3 0.0 collective-permute-done.2.left_ref
  12.3 1.3 %collective-permute-done.3.right_ref = f32[8,144]{1,0:T(8,128)S(1)} collective-permute-done((f32[8,144]{1,0:T(8,128)S(1)}, f32[8,144]{1,0:T(8,128)S(1)}, u32[]{:S(2)}, u32[]{:S(2)}) %collective-permute-start.3) | collective-permute-done | bytes 4640 | tf_op jit(solution)/shard_map/ppermute | solution.py:321
  13.6 0.0 collective-permute-done.above_ref
  13.6 0.0 collective-permute-done.1.below_ref
  13.6 1.8 %send.1 = (f32[144,1024]{1,0:T(8,128)S(1)}, f32[1792,128]{1,0:T(8,128)S(1)}) custom-call(f32[144,1024]{1,0:T(8,128)S(1)} %get-tuple-element.15.base_ref, s32[1,1024]{1,0:T(1,128)S(1)} %get-tuple-element.16.slot_ref, f32[8,1024]{1,0:T(8,128)S(1)} %get-tuple-element.17.steps_ref, f32[152,128]{1,0:T(8,128)S(1)} %add_add_fusion.small_ref, ...), custom_call_target="tpu_custom_call" | custom-call | tf_op jit(solution)/shard_map/send/pallas_call | solution.py:359
  15.4 24.4 %all_to_all.10 = f32[128,1,1792]{2,1,0:T(1,128)S(1)} all-to-all(f32[128,1,1792]{2,1,0:T(1,128)S(1)} %bitcast.9), channel_id=1, replica_groups=mesh['gx'=16,'gy'=8] {'gx','gy'}, dimensions={0} | all-to-all | bytes 1835008 | tf_op jit(solution)/shard_map/all_to_all | solution.py:303
  39.8 22.1 %crm.1 = f32[896,128]{1,0:T(8,128)} custom-call(f32[400,128]{1,0:T(8,128)S(1)} %get-tuple-element.23.const_ref, f32[1792,128]{1,0:T(8,128)S(1)} %bitcast.7, f32[3200,1792]{1,0:T(8,128)} %field_hbm.1), custom_call_target="tpu_custom_call" | custom-call | tf_op jit(solution)/shard_map/crm/pallas_call | solution.py:282
  61.9 4.7 %all-to-all-start.1 = ((f32[128,1,896]{2,1,0:T(1,128)}), f32[128,1,896]{2,1,0:T(1,128)S(1)}, u32[]{:S(2)}, u32[]{:S(2)}) async-start(f32[128,1,896]{2,1,0:T(1,128)} %bitcast.4), calls=%async_computation.1 | async-start | bytes 917504 | tf_op jit(solution)/shard_map/all_to_all | solution.py:303
  66.6 0.0 copy-done.1
  66.6 0.1 copy.12.up_ref
  66.7 12.8 %all-to-all-done.1 = f32[128,1,896]{2,1,0:T(1,128)S(1)} async-done(((f32[128,1,896]{2,1,0:T(1,128)}), f32[128,1,896]{2,1,0:T(1,128)S(1)}, u32[]{:S(2)}, u32[]{:S(2)}) %all-to-all-start.1) | async-done | bytes 458784 | tf_op jit(solution)/shard_map/all_to_all | solution.py:303
  79.5 1.9 %final.1 = f32[1152,128]{1,0:T(8,128)} custom-call(f32[144,1024]{1,0:T(8,128)S(1)} %get-tuple-element.22.dyn_ref, f32[896,128]{1,0:T(8,128)S(1)} %bitcast.8, s32[1,1024]{1,0:T(1,128)S(1)} %get-tuple-element.16.slot_ref, f32[72,50]{1,0:T(8,128)S(1)} %copy.12.up_ref), custom_call_target="tpu_custom_call" | custom-call | tf_op jit(solution)/shard_map/final/pallas_call | solution.py:372
Async XLA Ops:
  0.0 1.1 %copy-start = (f32[144,8,128]{2,1,0:T(8,128)S(1)}, f32[144,8,128]{2,1,0:T(8,128)}, u32[]{:S(2)}) copy-start(f32[144,8,128]{2,1,0:T(8,128)} %param.8) | copy-start | bytes 1769476
  1.1 65.5 %copy-start.1 = (f32[72,50]{0,1:T(8,128)S(1)}, f32[72,50]{0,1:T(8,128)}, u32[]{:S(2)}) copy-start(f32[72,50]{0,1:T(8,128)} %param.13) | copy-start | bytes 43204
  1.5 12.1 %collective-permute-start = (f32[144,128]{1,0:T(8,128)S(1)}, f32[144,128]{1,0:T(8,128)S(1)}, u32[]{:S(2)}, u32[]{:S(2)}) collective-permute-start(f32[144,128]{1,0:T(8,128)S(1)} %get-tuple-element.18), channel_id=1, source_target_pairs={{0,8},{8,16},{16,24},{24,32},{32,40},{40,48},{48,56},{56,64},{64,7... | collective-permute-start | bytes 221192 | tf_op jit(solution)/shard_map/ppermute | solution.py:321
  4.0 9.6 %collective-permute-start.1 = (f32[144,128]{1,0:T(8,128)S(1)}, f32[144,128]{1,0:T(8,128)S(1)}, u32[]{:S(2)}, u32[]{:S(2)}) collective-permute-start(f32[144,128]{1,0:T(8,128)S(1)} %get-tuple-element.19), channel_id=1, source_target_pairs={{0,120},{8,0},{16,8},{24,16},{32,24},{40,32},{48,40},{56,48},{64,5... | collective-permute-start | bytes 221192 | tf_op jit(solution)/shard_map/ppermute | solution.py:321
  8.4 3.9 %collective-permute-start.2 = (f32[8,144]{1,0:T(8,128)S(1)}, f32[8,144]{1,0:T(8,128)S(1)}, u32[]{:S(2)}, u32[]{:S(2)}) collective-permute-start(f32[8,144]{1,0:T(8,128)S(1)} %get-tuple-element.20), channel_id=1, source_target_pairs={{0,1},{1,2},{2,3},{3,4},{4,5},{5,6},{6,7},{7,0},{8,9},{9,10},{10,1... | collective-permute-start | bytes 13832 | tf_op jit(solution)/shard_map/ppermute | solution.py:321
  10.5 3.1 %collective-permute-start.3 = (f32[8,144]{1,0:T(8,128)S(1)}, f32[8,144]{1,0:T(8,128)S(1)}, u32[]{:S(2)}, u32[]{:S(2)}) collective-permute-start(f32[8,144]{1,0:T(8,128)S(1)} %get-tuple-element.21), channel_id=1, source_target_pairs={{0,7},{1,0},{2,1},{3,2},{4,3},{5,4},{6,5},{7,6},{8,15},{9,8},{10,9... | collective-permute-start | bytes 13832 | tf_op jit(solution)/shard_map/ppermute | solution.py:321
  61.9 17.6 %all-to-all-start.1 = ((f32[128,1,896]{2,1,0:T(1,128)}), f32[128,1,896]{2,1,0:T(1,128)S(1)}, u32[]{:S(2)}, u32[]{:S(2)}) async-start(f32[128,1,896]{2,1,0:T(1,128)} %bitcast.4), calls=%async_computation.1 | async-start | bytes 917504 | tf_op jit(solution)/shard_map/all_to_all | solution.py:303

commit v5 on v4

--- a/solution.py
+++ b/solution.py
@@ -54,7 +54,7 @@
         east_ref[i:i + 1, :] = side[1:2]
 
 
-def local_kernel(cap, crm_z, state_ref, small_ref, base_ref, slot_ref, steps_ref, const_ref):
+def local_kernel(cap, crm_z, state_ref, small_ref, base_ref, slot_ref, sent_ref, edge_ref, const_ref):
     levels = base_ref.shape[0]
     half = levels // 2
     vert = small_ref[2 * SUBL:2 * SUBL + half, :half]
@@ -72,8 +72,10 @@
         laps.append(mid + DIFFUSION * (lap - 4.0 * mid))
     whole = jnp.concatenate(rows, axis=1)
     base = jnp.concatenate(laps, axis=1)
-    base_ref[:half, :] = base[:half] + dot3(vert, whole[:half])
-    base_ref[half:, :] = base[half:] + dot3(vert, whole[half:])
+    temper = base[:half] + dot3(vert, whole[:half])
+    vapour = base[half:] + dot3(vert, whole[half:])
+    base_ref[:half, :] = temper
+    base_ref[half:, :] = vapour
 
     owner = jnp.concatenate([small_ref[i:i + 1, :] for i in range(SUBL)], axis=1).astype(jnp.int32)
     width = owner.shape[1]
@@ -85,10 +87,24 @@
     ).astype(jnp.bfloat16)
     before = dot(mine.astype(jnp.bfloat16), earlier)
     rank = jnp.sum(jnp.where(mine, before, 0.0), axis=0, keepdims=True).astype(jnp.int32)
-    slot_ref[...] = owner * cap + rank
+    slot = owner * cap + rank
+    slot_ref[...] = slot
     counts = jnp.concatenate([small_ref[i:i + 1, :] for i in range(SUBL, 2 * SUBL)], axis=1)
     lead = (lax.broadcasted_iota(jnp.int32, (SUBL, width), 0) == 0).astype(jnp.float32)
-    steps_ref[...] = lead * counts
+    both = payload(down_of(small_ref, crm_z, half), temper, vapour, lead * counts)
+    chunk = sent_ref.shape[0] // 2
+    for start in range(0, sent_ref.shape[0], chunk):
+        ids = start + lax.broadcasted_iota(jnp.int32, (chunk, width), 0)
+        sent = dot((ids == slot).astype(jnp.bfloat16), both, NT)
+        sent_ref[start:start + chunk, :] = sent[:, :LANES] + sent[:, LANES:]
+    digits = jnp.concatenate([(slot // LANES).astype(jnp.float32), (slot % LANES).astype(jnp.float32)], axis=0)
+    ends = dot(digits.astype(jnp.bfloat16), ends_of(width), NT)
+    ends = (ends[0:1] * LANES + ends[1:2]).astype(jnp.int32)
+    ends = jnp.concatenate([ends, jnp.full((1, LANES - ends.shape[1]), -1, jnp.int32)], axis=1)
+    edges = jnp.concatenate([slot[:, :LANES], slot[:, width - LANES:], ends], axis=1)
+    ids = lax.broadcasted_iota(jnp.int32, edge_ref.shape, 0)
+    edge_ref[...] = (ids == edges).astype(jnp.bfloat16)
+
     last = small_ref.shape[0] - SUBL
     line = jnp.broadcast_to(small_ref[last:last + 1, :], (LANES, LANES))
     c = line.T[:crm_z]
@@ -97,39 +113,53 @@
         const_ref[pl.ds(i, crm_z, stride=SUBL), :] = value
 
 
-def send_kernel(
-    crm_z, base_ref, slot_ref, steps_ref, small_ref, above_ref, below_ref, left_ref, right_ref,
-    dyn_ref, out_ref,
-):
-    levels, width = base_ref.shape
-    half = levels // 2
-    pad_z = -(-crm_z // SUBL) * SUBL
-    start = small_ref.shape[0] - SUBL - pad_z
-    down = small_ref[start:start + pad_z, :half]
-    sides = jnp.concatenate([left_ref[...], right_ref[...]], axis=0)
+def ends_of(width):
     row = lax.broadcasted_iota(jnp.int32, (2 * SUBL, width), 0)
     lane = lax.broadcasted_iota(jnp.int32, (2 * SUBL, width), 1)
     target = jnp.where(row < SUBL, row * LANES, (row - SUBL) * LANES + (LANES - 1))
-    place = (lane == target).astype(jnp.bfloat16)
+    return (lane == target).astype(jnp.bfloat16)
+
+
+def down_of(small_ref, crm_z, half):
+    pad_z = -(-crm_z // SUBL) * SUBL
+    start = small_ref.shape[0] - SUBL - pad_z
+    return small_ref[start:start + pad_z, :half]
+
+
+def payload(down, temper, vapour, steps):
+    parts = [dot3(down, temper), dot3(down, vapour), steps]
+    blank = LANES - sum(part.shape[0] for part in parts)
+    parts.append(jnp.zeros((blank, temper.shape[1]), jnp.float32))
+    return jnp.concatenate(split(jnp.concatenate(parts, axis=0)), axis=0)
+
+
+def send_kernel(crm_z, small_ref, sent_ref, edge_ref, above_ref, below_ref, left_ref, right_ref, out_ref):
+    half = above_ref.shape[0] // 2
+    sides = jnp.concatenate([left_ref[...], right_ref[...]], axis=0)
+    row = lax.broadcasted_iota(jnp.int32, (2 * SUBL, LANES), 0)
+    lane = lax.broadcasted_iota(jnp.int32, (2 * SUBL, LANES), 1)
+    same = (row == lane).astype(jnp.bfloat16)
     s_hi, s_lo = split(sides)
+    ends = dot(s_hi, same, TN) + dot(s_lo, same, TN)
+    halo = DIFFUSION * jnp.concatenate([above_ref[...], below_ref[...], ends], axis=1)
+    both = payload(down_of(small_ref, crm_z, half), halo[:half], halo[half:], jnp.zeros((SUBL, halo.shape[1]), jnp.float32))
+    chunk = out_ref.shape[0] // 2
+    for start in range(0, out_ref.shape[0], chunk):
+        rows = slice(start, start + chunk)
+        sent = dot(edge_ref[rows, :], both, NT)
+        out_ref[rows, :] = sent_ref[rows, :] + (sent[:, :LANES] + sent[:, LANES:])
+
+
+def halo_kernel(base_ref, above_ref, below_ref, left_ref, right_ref, dyn_ref):
+    width = base_ref.shape[1]
+    sides = jnp.concatenate([left_ref[...], right_ref[...]], axis=0)
+    s_hi, s_lo = split(sides)
+    place = ends_of(width)
     halo = dot(s_hi, place, TN) + dot(s_lo, place, TN)
     first = halo[:, :LANES] + above_ref[...]
     last = halo[:, width - LANES:] + below_ref[...]
     halo = jnp.concatenate([first, halo[:, LANES:width - LANES], last], axis=1)
-    dyn = base_ref[...] + DIFFUSION * halo
-    dyn_ref[...] = dyn
-    prof_t = dot3(down, dyn[:half])
-    prof_q = dot3(down, dyn[half:])
-    blank = jnp.zeros((LANES - 2 * pad_z - SUBL, width), jnp.float32)
-    payload = jnp.concatenate([prof_t, prof_q, steps_ref[...], blank], axis=0)
-    p_hi, p_lo = split(payload)
-    both = jnp.concatenate([p_hi, p_lo], axis=0)
-    slot = slot_ref[...]
-    chunk = out_ref.shape[0] // 2
-    for start in range(0, out_ref.shape[0], chunk):
-        ids = start + lax.broadcasted_iota(jnp.int32, (chunk, width), 0)
-        sent = dot((ids == slot).astype(jnp.bfloat16), both, NT)
-        out_ref[start:start + chunk, :] = sent[:, :LANES] + sent[:, LANES:]
+    dyn_ref[...] = base_ref[...] + DIFFUSION * halo
 
 
 def total(values):
@@ -150,7 +180,7 @@
 
 def crm_kernel(
     crm_z, crm_x, blocks, const_ref, arrived_ref, field_hbm, out_ref,
-    prof_ref, weight_ref, part_ref, turn_ref, buffers, sems,
+    prof_ref, weight_ref, part_ref, pair_ref, turn_ref, buffers, sems,
 ):
     pad_z = -(-crm_z // SUBL) * SUBL
     quads = crm_x // SUBL
@@ -219,9 +249,10 @@
 
         def pack(i, carry):
             start = i * (SUBL * pad_z)
-            change = part_ref[pl.ds(start, pad_z, stride=SUBL), :]
-            for j in range(1, SUBL):
-                change = change + part_ref[pl.ds(start + j, pad_z, stride=SUBL), :]
+            pairs = [part_ref[pl.ds(start + j, 2 * pad_z, stride=4), :] for j in range(4)]
+            at = i * 2 * pad_z
+            pair_ref[pl.ds(at, 2 * pad_z), :] = (pairs[0] + pairs[1]) + (pairs[2] + pairs[3])
+            change = pair_ref[pl.ds(at, pad_z, stride=2), :] + pair_ref[pl.ds(at + 1, pad_z, stride=2), :]
             change = jnp.concatenate([change, jnp.zeros((half - pad_z, LANES), jnp.float32)], axis=0)
             change = jnp.where(level < crm_z, change, 0.0)
             turn_ref[rows_of(i, LANES), :] = jnp.concatenate([change, change], axis=0).T
@@ -289,6 +320,7 @@
             pltpu.VMEM((blocks * 2 * pad_z, LANES), jnp.float32),
             pltpu.VMEM((blocks * SUBL, LANES), jnp.float32),
             pltpu.VMEM((blocks * SUBL * pad_z, LANES), jnp.float32),
+            pltpu.VMEM((blocks * 2 * pad_z, LANES), jnp.float32),
             pltpu.VMEM((slots, LANES), jnp.float32),
             pltpu.VMEM((2, rows, LANES), jnp.float32),
             pltpu.SemaphoreType.DMA((2,)),
@@ -346,28 +378,43 @@
     right = shifted(west, "gy", -1)
 
     small = stacked([owner, counts], [vert, down_map, courant[None]])
-    base, slot, steps, const = pl.pallas_call(
+    base, slot, sent, edge, const = pl.pallas_call(
         functools.partial(local_kernel, cap, crm_z),
         in_specs=[VMEM] * 2,
-        out_specs=[VMEM] * 4,
-        out_shape=[f32(rows, col_dev), i32(1, col_dev), f32(SUBL, col_dev), f32(SUBL * crm_z, LANES)],
+        out_specs=[VMEM] * 5,
+        out_shape=[
+            f32(rows, col_dev),
+            i32(1, col_dev),
+            f32(slots, LANES),
+            jax.ShapeDtypeStruct((slots, 3 * LANES), jnp.bfloat16),
+            f32(SUBL * crm_z, LANES),
+        ],
         compiler_params=params(),
         cost_estimate=pl.CostEstimate(flops=10**9, bytes_accessed=4 * 10**6, transcendentals=0),
         name="local",
     )(flat, small)
 
-    dyn, outgoing = pl.pallas_call(
+    outgoing = pl.pallas_call(
         functools.partial(send_kernel, crm_z),
-        in_specs=[VMEM] * 8,
-        out_specs=[VMEM] * 2,
-        out_shape=[f32(rows, col_dev), f32(slots, LANES)],
+        in_specs=[VMEM] * 7,
+        out_specs=VMEM,
+        out_shape=f32(slots, LANES),
         compiler_params=params(),
         name="send",
-    )(base, slot, steps, small, above, below, left, right)
+    )(small, sent, edge, above, below, left, right)
 
     arrived = exchange(outgoing, devices)
     change = crm(const, arrived, crm_field, crm_z, crm_x)
     returned = exchange(change, devices)
+    dyn = pl.pallas_call(
+        halo_kernel,
+        in_specs=[VMEM] * 5,
+        out_specs=VMEM,
+        out_shape=f32(rows, col_dev),
+        compiler_params=params(),
+        cost_estimate=pl.CostEstimate(flops=10**8, bytes_accessed=2 * 10**6, transcendentals=0),
+        name="halo",
+    )(base, above, below, left, right)
 
     out = pl.pallas_call(
         final_kernel,

time: 82 us -> 81 us (0.988)
  waiting for transfers between devices: 14.1 us -> 12.4 us
  Pallas kernels: 27.1 us -> 28.2 us
    pallas_call x1, Pallas kernels: 0.94 us -> 2.61 us  [body(): pl.pallas_call(functools.partial(local_kernel, cap, crm_z), in_specs=[VME...]
    ppermute x4, waiting for transfers between devices: 1.3 us -> 0.01 us  [shifted(): lax.ppermute(value, axis, [(i, (i + step) % count) for i in range(count)])]
    pallas_call x1 -> x2, Pallas kernels: 1.8 us -> 1.4 us  [the longest x1 1.06 us: body(): pl.pallas_call(functools.partial(send_kernel, crm_z), in_specs=[VMEM] * 7...]
  transfers between devices with their start and end apart: 5 -> 5, of which waited for: 2 -> 1; matrix products, arithmetic and copies ran while one was open for 1% -> 1% of each run, Pallas kernels for 1% -> 4%
where the time goes in v5:
time: 81 us; the launch traced here: 80.4 us
  Pallas kernels  28.2 us (35%)
  blocking collectives  24 us (30%)
  starting transfers between devices  13.7 us (17%)
  waiting for transfers between devices  12.4 us (15%)
  local copies, waits for them, and re-layouts  1.15 us (1%)
  other arithmetic  0.83 us (1%)
    all_to_all x1, blocking collectives, exchange(): lax.all_to_all(sent, ('gx', 'gy'), split_axis=0, concat_axis=0, tiled=True)  24 us
    pallas_call x1, Pallas kernels, crm(): pl.pallas_call(functools.partial(crm_kernel, crm_z, crm_x, blocks), grid=...  21.9 us
    all_to_all x1, waiting for transfers between devices, exchange(): lax.all_to_all(sent, ('gx', 'gy'), split_axis=0, concat_axis=0, tiled=True)  12.4 us
    ppermute x4, starting transfers between devices, shifted(): lax.ppermute(value, axis, [(i, (i + step) % count) for i in range(count)])  9.02 us
    all_to_all x1, starting transfers between devices, exchange(): lax.all_to_all(sent, ('gx', 'gy'), split_axis=0, concat_axis=0, tiled=True)  4.69 us
    pallas_call x1, Pallas kernels, body(): pl.pallas_call(functools.partial(local_kernel, cap, crm_z), in_specs=[VME...  2.61 us
    pallas_call x1, Pallas kernels, body(): pl.pallas_call(final_kernel, in_specs=[VMEM] * 4, out_specs=pl.BlockSpec(...  1.89 us
  transfers between devices with their start and end apart: 5, of which 1 were waited for; matrix products, arithmetic and copies ran while one was open for 1% of the time, Pallas kernels for 4%

profile of v5, /device:TPU:1, one launch (start us, length us, event | category | flops | bytes accessed | tf_op | source)
XLA Modules:
  0.0 80.4 jit_solution(1945152444082710572)
XLA Ops:
  0.0 0.0 copy-start
  0.0 1.1 %copy-done = f32[144,8,128]{2,1,0:T(8,128)S(1)} copy-done((f32[144,8,128]{2,1,0:T(8,128)S(1)}, f32[144,8,128]{2,1,0:T(8,128)}, u32[]{:S(2)}) %copy-start) | copy-done | bytes 589848
  1.1 0.0 copy-start.1
  1.1 0.4 edges.1
  1.5 2.5 %collective-permute-start = (f32[144,128]{1,0:T(8,128)S(1)}, f32[144,128]{1,0:T(8,128)S(1)}, u32[]{:S(2)}, u32[]{:S(2)}) collective-permute-start(f32[144,128]{1,0:T(8,128)S(1)} %get-tuple-element.15), channel_id=1, source_target_pairs={{0,8},{8,16},{16,24},{24,32},{32,40},{40,48},{48,56},{56,64},{64,7... | collective-permute-start | bytes 221192 | tf_op jit(solution)/shard_map/ppermute | solution.py:353
  4.0 4.4 %collective-permute-start.1 = (f32[144,128]{1,0:T(8,128)S(1)}, f32[144,128]{1,0:T(8,128)S(1)}, u32[]{:S(2)}, u32[]{:S(2)}) collective-permute-start(f32[144,128]{1,0:T(8,128)S(1)} %get-tuple-element.16), channel_id=1, source_target_pairs={{0,120},{8,0},{16,8},{24,16},{32,24},{40,32},{48,40},{56,48},{64,5... | collective-permute-start | bytes 221192 | tf_op jit(solution)/shard_map/ppermute | solution.py:353
  8.4 2.1 %collective-permute-start.2 = (f32[8,144]{1,0:T(8,128)S(1)}, f32[8,144]{1,0:T(8,128)S(1)}, u32[]{:S(2)}, u32[]{:S(2)}) collective-permute-start(f32[8,144]{1,0:T(8,128)S(1)} %get-tuple-element.17), channel_id=1, source_target_pairs={{0,1},{1,2},{2,3},{3,4},{4,5},{5,6},{6,7},{7,0},{8,9},{9,10},{10,1... | collective-permute-start | bytes 13832 | tf_op jit(solution)/shard_map/ppermute | solution.py:353
  10.5 0.0 collective-permute-start.3
  10.5 0.8 %add_add_fusion.small_ref = f32[152,128]{1,0:T(8,128)S(1)} fusion(f32[1,50]{1,0:T(1,128)} %bitcast.12, f32[50,72]{1,0:T(8,128)} %param.12, f32[72,72]{1,0:T(8,128)} %param.11, s32[8,128]{1,0:T(8,128)} %param.10, s32[8,128]{1,0:T(8,128)} %param.9), kind=kLoop, calls=%fused_computation | loop fusion | flops 97280 | bytes 121352 | tf_op jit(solution)/shard_map/add | solution.py:348
  11.3 2.6 %local.1 = (f32[144,1024]{1,0:T(8,128)S(1)}, s32[1,1024]{1,0:T(1,128)S(1)}, f32[1792,128]{1,0:T(8,128)S(1)}, bf16[1792,384]{1,0:T(8,128)(2,1)S(1)}, f32[400,128]{1,0:T(8,128)S(1)}) custom-call(f32[1152,128]{1,0:T(8,128)S(1)} %bitcast.11, f32[152,128]{1,0:T(8,128)S(1)} %add_add_fusion.small_ref), custom_call_target="tpu_custom_call" | custom-call | flops 1000000000 | bytes 4000000 | tf_op jit(solution)/shard_map/local/pallas_call | solution.py:381
  13.9 0.0 collective-permute-done.2.left_ref
  14.0 0.0 collective-permute-done.3.right_ref
  14.0 0.0 collective-permute-done.above_ref
  14.0 0.0 collective-permute-done.1.below_ref
  14.0 1.1 %send.1 = f32[1792,128]{1,0:T(8,128)S(1)} custom-call(f32[152,128]{1,0:T(8,128)S(1)} %add_add_fusion.small_ref, f32[1792,128]{1,0:T(8,128)S(1)} %get-tuple-element.20.sent_ref, bf16[1792,384]{1,0:T(8,128)(2,1)S(1)} %get-tuple-element.21.edge_ref, f32[144,128]{1,0:T(8,128)S(1)} %collective-permute-done.above_ref, ...), custom_call_target="tpu_custom_call" | custom-call | tf_op jit(solution)/shard_map/send/pallas_call | solution.py:397
  15.0 24.0 %all_to_all.10 = f32[128,1,1792]{2,1,0:T(1,128)S(1)} all-to-all(f32[128,1,1792]{2,1,0:T(1,128)S(1)} %bitcast.7), channel_id=1, replica_groups=mesh['gx'=16,'gy'=8] {'gx','gy'}, dimensions={0} | all-to-all | bytes 1835008 | tf_op jit(solution)/shard_map/all_to_all | solution.py:335
  39.1 21.9 %crm.1 = f32[896,128]{1,0:T(8,128)} custom-call(f32[400,128]{1,0:T(8,128)S(1)} %get-tuple-element.19.const_ref, f32[1792,128]{1,0:T(8,128)S(1)} %bitcast.8, f32[3200,1792]{1,0:T(8,128)} %field_hbm.1), custom_call_target="tpu_custom_call" | custom-call | tf_op jit(solution)/shard_map/crm/pallas_call | solution.py:313
  61.0 4.7 %all-to-all-start.1 = ((f32[128,1,896]{2,1,0:T(1,128)}), f32[128,1,896]{2,1,0:T(1,128)S(1)}, u32[]{:S(2)}, u32[]{:S(2)}) async-start(f32[128,1,896]{2,1,0:T(1,128)} %bitcast.4), calls=%async_computation.1 | async-start | bytes 917504 | tf_op jit(solution)/shard_map/all_to_all | solution.py:335
  65.7 0.0 copy-done.1
  65.7 0.1 copy.12.up_ref
  65.8 0.3 halo.1.dyn_ref
  66.1 12.4 %all-to-all-done.1 = f32[128,1,896]{2,1,0:T(1,128)S(1)} async-done(((f32[128,1,896]{2,1,0:T(1,128)}), f32[128,1,896]{2,1,0:T(1,128)S(1)}, u32[]{:S(2)}, u32[]{:S(2)}) %all-to-all-start.1) | async-done | bytes 458784 | tf_op jit(solution)/shard_map/all_to_all | solution.py:335
  78.5 1.9 %final.1 = f32[1152,128]{1,0:T(8,128)} custom-call(f32[144,1024]{1,0:T(8,128)S(1)} %halo.1.dyn_ref, f32[896,128]{1,0:T(8,128)S(1)} %bitcast.9, s32[1,1024]{1,0:T(1,128)S(1)} %get-tuple-element.22.slot_ref, f32[72,50]{1,0:T(8,128)S(1)} %copy.12.up_ref), custom_call_target="tpu_custom_call" | custom-call | tf_op jit(solution)/shard_map/final/pallas_call | solution.py:419
Async XLA Ops:
  0.0 1.1 %copy-start = (f32[144,8,128]{2,1,0:T(8,128)S(1)}, f32[144,8,128]{2,1,0:T(8,128)}, u32[]{:S(2)}) copy-start(f32[144,8,128]{2,1,0:T(8,128)} %param.8) | copy-start | bytes 1769476
  1.1 64.6 %copy-start.1 = (f32[72,50]{0,1:T(8,128)S(1)}, f32[72,50]{0,1:T(8,128)}, u32[]{:S(2)}) copy-start(f32[72,50]{0,1:T(8,128)} %param.13) | copy-start | bytes 43204
  1.5 12.5 %collective-permute-start = (f32[144,128]{1,0:T(8,128)S(1)}, f32[144,128]{1,0:T(8,128)S(1)}, u32[]{:S(2)}, u32[]{:S(2)}) collective-permute-start(f32[144,128]{1,0:T(8,128)S(1)} %get-tuple-element.15), channel_id=1, source_target_pairs={{0,8},{8,16},{16,24},{24,32},{32,40},{40,48},{48,56},{56,64},{64,7... | collective-permute-start | bytes 221192 | tf_op jit(solution)/shard_map/ppermute | solution.py:353
  4.0 10.0 %collective-permute-start.1 = (f32[144,128]{1,0:T(8,128)S(1)}, f32[144,128]{1,0:T(8,128)S(1)}, u32[]{:S(2)}, u32[]{:S(2)}) collective-permute-start(f32[144,128]{1,0:T(8,128)S(1)} %get-tuple-element.16), channel_id=1, source_target_pairs={{0,120},{8,0},{16,8},{24,16},{32,24},{40,32},{48,40},{56,48},{64,5... | collective-permute-start | bytes 221192 | tf_op jit(solution)/shard_map/ppermute | solution.py:353
  8.4 5.6 %collective-permute-start.2 = (f32[8,144]{1,0:T(8,128)S(1)}, f32[8,144]{1,0:T(8,128)S(1)}, u32[]{:S(2)}, u32[]{:S(2)}) collective-permute-start(f32[8,144]{1,0:T(8,128)S(1)} %get-tuple-element.17), channel_id=1, source_target_pairs={{0,1},{1,2},{2,3},{3,4},{4,5},{5,6},{6,7},{7,0},{8,9},{9,10},{10,1... | collective-permute-start | bytes 13832 | tf_op jit(solution)/shard_map/ppermute | solution.py:353
  10.5 3.5 %collective-permute-start.3 = (f32[8,144]{1,0:T(8,128)S(1)}, f32[8,144]{1,0:T(8,128)S(1)}, u32[]{:S(2)}, u32[]{:S(2)}) collective-permute-start(f32[8,144]{1,0:T(8,128)S(1)} %get-tuple-element.18), channel_id=1, source_target_pairs={{0,7},{1,0},{2,1},{3,2},{4,3},{5,4},{6,5},{7,6},{8,15},{9,8},{10,9... | collective-permute-start | bytes 13832 | tf_op jit(solution)/shard_map/ppermute | solution.py:353
  61.0 17.6 %all-to-all-start.1 = ((f32[128,1,896]{2,1,0:T(1,128)}), f32[128,1,896]{2,1,0:T(1,128)S(1)}, u32[]{:S(2)}, u32[]{:S(2)}) async-start(f32[128,1,896]{2,1,0:T(1,128)} %bitcast.4), calls=%async_computation.1 | async-start | bytes 917504 | tf_op jit(solution)/shard_map/all_to_all | solution.py:335

commit v6 on v5

--- a/solution.py
+++ b/solution.py
@@ -33,9 +33,20 @@
 
 
 def dot3(a, b):
+    depth = b.shape[0]
+    pad = -depth % (2 * SUBL)
+    if pad:
+        a = jnp.concatenate([a, jnp.zeros((a.shape[0], pad), jnp.float32)], axis=1)
+        b = jnp.concatenate([b, jnp.zeros((pad, b.shape[1]), jnp.float32)], axis=0)
     a_hi, a_lo = split(a)
     b_hi, b_lo = split(b)
-    return dot(a_hi, b_hi) + (dot(a_hi, b_lo) + dot(a_lo, b_hi))
+    return dot(jnp.concatenate([a_hi, a_hi, a_lo], axis=1), jnp.concatenate([b_hi, b_lo, b_hi], axis=0))
+
+
+def chosen(start, count, index):
+    ids = start + lax.broadcasted_iota(jnp.int32, (count, index.shape[1]), 0)
+    hit = ids.astype(jnp.int16) == index.astype(jnp.int16)
+    return jnp.where(hit, jnp.bfloat16(1), jnp.bfloat16(0))
 
 
 def edges_kernel(state_ref, top_ref, bottom_ref, west_ref, east_ref):
@@ -81,12 +92,17 @@
     width = owner.shape[1]
     devices = LANES * (-(-DEVICES // LANES))
     mine = lax.broadcasted_iota(jnp.int32, (devices, width), 0) == owner
-    earlier = (
-        lax.broadcasted_iota(jnp.int32, (width, width), 0)
-        < lax.broadcasted_iota(jnp.int32, (width, width), 1)
-    ).astype(jnp.bfloat16)
-    before = dot(mine.astype(jnp.bfloat16), earlier)
-    rank = jnp.sum(jnp.where(mine, before, 0.0), axis=0, keepdims=True).astype(jnp.int32)
+    line = lax.broadcasted_iota(jnp.int32, (LANES, 2 * LANES), 0)
+    lane = lax.broadcasted_iota(jnp.int32, (LANES, 2 * LANES), 1)
+    counting = ((line < lane) | (lane >= LANES)).astype(jnp.bfloat16)
+    seen = jnp.zeros((devices, LANES), jnp.float32)
+    ranks = []
+    for i in range(SUBL):
+        here = mine[:, i * LANES:(i + 1) * LANES]
+        found = dot(here.astype(jnp.bfloat16), counting)
+        ranks.append(jnp.sum(jnp.where(here, found[:, :LANES] + seen, 0.0), axis=0, keepdims=True))
+        seen = seen + found[:, LANES:]
+    rank = jnp.concatenate(ranks, axis=1).astype(jnp.int32)
     slot = owner * cap + rank
     slot_ref[...] = slot
     counts = jnp.concatenate([small_ref[i:i + 1, :] for i in range(SUBL, 2 * SUBL)], axis=1)
@@ -94,16 +110,14 @@
     both = payload(down_of(small_ref, crm_z, half), temper, vapour, lead * counts)
     chunk = sent_ref.shape[0] // 2
     for start in range(0, sent_ref.shape[0], chunk):
-        ids = start + lax.broadcasted_iota(jnp.int32, (chunk, width), 0)
-        sent = dot((ids == slot).astype(jnp.bfloat16), both, NT)
+        sent = dot(chosen(start, chunk, slot), both, NT)
         sent_ref[start:start + chunk, :] = sent[:, :LANES] + sent[:, LANES:]
     digits = jnp.concatenate([(slot // LANES).astype(jnp.float32), (slot % LANES).astype(jnp.float32)], axis=0)
     ends = dot(digits.astype(jnp.bfloat16), ends_of(width), NT)
     ends = (ends[0:1] * LANES + ends[1:2]).astype(jnp.int32)
     ends = jnp.concatenate([ends, jnp.full((1, LANES - ends.shape[1]), -1, jnp.int32)], axis=1)
     edges = jnp.concatenate([slot[:, :LANES], slot[:, width - LANES:], ends], axis=1)
-    ids = lax.broadcasted_iota(jnp.int32, edge_ref.shape, 0)
-    edge_ref[...] = (ids == edges).astype(jnp.bfloat16)
+    edge_ref[...] = chosen(0, edge_ref.shape[0], edges)
 
     last = small_ref.shape[0] - SUBL
     line = jnp.broadcast_to(small_ref[last:last + 1, :], (LANES, LANES))
@@ -271,13 +285,14 @@
     pairs = returned_ref.shape[0]
     r_hi, r_lo = split(returned_ref[...])
     both = jnp.concatenate([r_hi, r_lo], axis=1)
-    ids = lax.broadcasted_iota(jnp.int32, (pairs, width), 0)
-    pick = (ids == slot // 2).astype(jnp.bfloat16)
-    got = dot(both, pick, TN)
-    got = got[:LANES] + got[LANES:]
-    change = jnp.where(slot % 2 == 0, got[:LANES // 2], got[LANES // 2:])
+    got = dot(both, chosen(0, pairs, slot // 2), TN)
+    even = jnp.broadcast_to(slot % 2 == 0, (LANES // 2, width))
+    c_hi, c_lo = [
+        jnp.where(even, part[:LANES // 2], part[LANES // 2:]).astype(jnp.bfloat16) for part in (got[:LANES], got[LANES:])
+    ]
     up = jnp.concatenate([up_ref[...], jnp.zeros((half, LANES // 2 - crm_z), jnp.float32)], axis=1)
-    tend = dot3(up, change)
+    u_hi, u_lo = split(up)
+    tend = dot(jnp.concatenate([u_hi, u_hi, u_lo], axis=1), jnp.concatenate([c_hi, c_lo, c_hi], axis=0))
     copies = []
     for v, new in enumerate((dyn_ref[:half, :] + tend, dyn_ref[half:, :] - tend)):
         for i in range(SUBL):

time: 81 us -> 80.8 us (level)
  transfers between devices with their start and end apart: 5 -> 5, of which waited for: 1 -> 2; matrix products, arithmetic and copies ran while one was open for 1% -> 1% of each run, Pallas kernels for 4% -> 3%
where the time goes in v6:
time: 80.8 us; the launch traced here: 80.2 us
  Pallas kernels  27.4 us (34%)
  blocking collectives  24.4 us (30%)
  starting transfers between devices  13.7 us (17%)
  waiting for transfers between devices  12.6 us (16%)
  local copies, waits for them, and re-layouts  1.15 us (1%)
  other arithmetic  0.83 us (1%)
    all_to_all x1, blocking collectives, exchange(): lax.all_to_all(sent, ('gx', 'gy'), split_axis=0, concat_axis=0, tiled=True)  24.4 us
    pallas_call x1, Pallas kernels, crm(): pl.pallas_call(functools.partial(crm_kernel, crm_z, crm_x, blocks), grid=...  21.9 us
    all_to_all x1, waiting for transfers between devices, exchange(): lax.all_to_all(sent, ('gx', 'gy'), split_axis=0, concat_axis=0, tiled=True)  12.4 us
    ppermute x4, starting transfers between devices, shifted(): lax.ppermute(value, axis, [(i, (i + step) % count) for i in range(count)])  9.02 us
    all_to_all x1, starting transfers between devices, exchange(): lax.all_to_all(sent, ('gx', 'gy'), split_axis=0, concat_axis=0, tiled=True)  4.69 us
    pallas_call x1, Pallas kernels, body(): pl.pallas_call(functools.partial(local_kernel, cap, crm_z), in_specs=[VME...  2.02 us
    pallas_call x1, Pallas kernels, body(): pl.pallas_call(final_kernel, in_specs=[VMEM] * 4, out_specs=pl.BlockSpec(...  1.73 us
  transfers between devices with their start and end apart: 5, of which 2 were waited for; matrix products, arithmetic and copies ran while one was open for 1% of the time, Pallas kernels for 3%

profile of v6, /device:TPU:1, one launch (start us, length us, event | category | flops | bytes accessed | tf_op | source)
XLA Modules:
  0.0 80.2 jit_solution(11497582976349657902)
XLA Ops:
  0.0 0.0 copy-start
  0.0 1.1 %copy-done = f32[144,8,128]{2,1,0:T(8,128)S(1)} copy-done((f32[144,8,128]{2,1,0:T(8,128)S(1)}, f32[144,8,128]{2,1,0:T(8,128)}, u32[]{:S(2)}) %copy-start) | copy-done | bytes 589848
  1.1 0.0 copy-start.1
  1.1 0.4 edges.1
  1.5 2.5 %collective-permute-start = (f32[144,128]{1,0:T(8,128)S(1)}, f32[144,128]{1,0:T(8,128)S(1)}, u32[]{:S(2)}, u32[]{:S(2)}) collective-permute-start(f32[144,128]{1,0:T(8,128)S(1)} %get-tuple-element.15), channel_id=1, source_target_pairs={{0,8},{8,16},{16,24},{24,32},{32,40},{40,48},{48,56},{56,64},{64,7... | collective-permute-start | bytes 221192 | tf_op jit(solution)/shard_map/ppermute | solution.py:368
  4.0 4.4 %collective-permute-start.1 = (f32[144,128]{1,0:T(8,128)S(1)}, f32[144,128]{1,0:T(8,128)S(1)}, u32[]{:S(2)}, u32[]{:S(2)}) collective-permute-start(f32[144,128]{1,0:T(8,128)S(1)} %get-tuple-element.16), channel_id=1, source_target_pairs={{0,120},{8,0},{16,8},{24,16},{32,24},{40,32},{48,40},{56,48},{64,5... | collective-permute-start | bytes 221192 | tf_op jit(solution)/shard_map/ppermute | solution.py:368
  8.4 2.1 %collective-permute-start.2 = (f32[8,144]{1,0:T(8,128)S(1)}, f32[8,144]{1,0:T(8,128)S(1)}, u32[]{:S(2)}, u32[]{:S(2)}) collective-permute-start(f32[8,144]{1,0:T(8,128)S(1)} %get-tuple-element.17), channel_id=1, source_target_pairs={{0,1},{1,2},{2,3},{3,4},{4,5},{5,6},{6,7},{7,0},{8,9},{9,10},{10,1... | collective-permute-start | bytes 13832 | tf_op jit(solution)/shard_map/ppermute | solution.py:368
  10.5 0.0 collective-permute-start.3
  10.5 0.8 %add_add_fusion.small_ref = f32[152,128]{1,0:T(8,128)S(1)} fusion(f32[1,50]{1,0:T(1,128)} %bitcast.12, f32[50,72]{1,0:T(8,128)} %param.12, f32[72,72]{1,0:T(8,128)} %param.11, s32[8,128]{1,0:T(8,128)} %param.10, s32[8,128]{1,0:T(8,128)} %param.9), kind=kLoop, calls=%fused_computation | loop fusion | flops 97280 | bytes 121352 | tf_op jit(solution)/shard_map/add | solution.py:363
  11.3 2.0 %local.1 = (f32[144,1024]{1,0:T(8,128)S(1)}, s32[1,1024]{1,0:T(1,128)S(1)}, f32[1792,128]{1,0:T(8,128)S(1)}, bf16[1792,384]{1,0:T(8,128)(2,1)S(1)}, f32[400,128]{1,0:T(8,128)S(1)}) custom-call(f32[1152,128]{1,0:T(8,128)S(1)} %bitcast.11, f32[152,128]{1,0:T(8,128)S(1)} %add_add_fusion.small_ref), custom_call_target="tpu_custom_call" | custom-call | flops 1000000000 | bytes 4000000 | tf_op jit(solution)/shard_map/local/pallas_call | solution.py:396
  13.4 0.0 collective-permute-done.2.left_ref
  13.4 0.2 collective-permute-done.3.right_ref
  13.6 0.0 collective-permute-done.above_ref
  13.6 0.0 collective-permute-done.1.below_ref
  13.6 1.0 %send.1 = f32[1792,128]{1,0:T(8,128)S(1)} custom-call(f32[152,128]{1,0:T(8,128)S(1)} %add_add_fusion.small_ref, f32[1792,128]{1,0:T(8,128)S(1)} %get-tuple-element.20.sent_ref, bf16[1792,384]{1,0:T(8,128)(2,1)S(1)} %get-tuple-element.21.edge_ref, f32[144,128]{1,0:T(8,128)S(1)} %collective-permute-done.above_ref, ...), custom_call_target="tpu_custom_call" | custom-call | tf_op jit(solution)/shard_map/send/pallas_call | solution.py:412
  14.5 24.4 %all_to_all.10 = f32[128,1,1792]{2,1,0:T(1,128)S(1)} all-to-all(f32[128,1,1792]{2,1,0:T(1,128)S(1)} %bitcast.7), channel_id=1, replica_groups=mesh['gx'=16,'gy'=8] {'gx','gy'}, dimensions={0} | all-to-all | bytes 1835008 | tf_op jit(solution)/shard_map/all_to_all | solution.py:350
  39.0 21.9 %crm.1 = f32[896,128]{1,0:T(8,128)} custom-call(f32[400,128]{1,0:T(8,128)S(1)} %get-tuple-element.19.const_ref, f32[1792,128]{1,0:T(8,128)S(1)} %bitcast.8, f32[3200,1792]{1,0:T(8,128)} %field_hbm.1), custom_call_target="tpu_custom_call" | custom-call | tf_op jit(solution)/shard_map/crm/pallas_call | solution.py:328
  60.9 4.7 %all-to-all-start.1 = ((f32[128,1,896]{2,1,0:T(1,128)}), f32[128,1,896]{2,1,0:T(1,128)S(1)}, u32[]{:S(2)}, u32[]{:S(2)}) async-start(f32[128,1,896]{2,1,0:T(1,128)} %bitcast.4), calls=%async_computation.1 | async-start | bytes 917504 | tf_op jit(solution)/shard_map/all_to_all | solution.py:350
  65.6 0.0 copy-done.1
  65.6 0.1 copy.12.up_ref
  65.7 0.3 halo.1.dyn_ref
  66.0 12.4 %all-to-all-done.1 = f32[128,1,896]{2,1,0:T(1,128)S(1)} async-done(((f32[128,1,896]{2,1,0:T(1,128)}), f32[128,1,896]{2,1,0:T(1,128)S(1)}, u32[]{:S(2)}, u32[]{:S(2)}) %all-to-all-start.1) | async-done | bytes 458784 | tf_op jit(solution)/shard_map/all_to_all | solution.py:350
  78.4 1.7 %final.1 = f32[1152,128]{1,0:T(8,128)} custom-call(f32[144,1024]{1,0:T(8,128)S(1)} %halo.1.dyn_ref, f32[896,128]{1,0:T(8,128)S(1)} %bitcast.9, s32[1,1024]{1,0:T(1,128)S(1)} %get-tuple-element.22.slot_ref, f32[72,50]{1,0:T(8,128)S(1)} %copy.12.up_ref), custom_call_target="tpu_custom_call" | custom-call | tf_op jit(solution)/shard_map/final/pallas_call | solution.py:434
Async XLA Ops:
  0.0 1.1 %copy-start = (f32[144,8,128]{2,1,0:T(8,128)S(1)}, f32[144,8,128]{2,1,0:T(8,128)}, u32[]{:S(2)}) copy-start(f32[144,8,128]{2,1,0:T(8,128)} %param.8) | copy-start | bytes 1769476
  1.1 64.5 %copy-start.1 = (f32[72,50]{0,1:T(8,128)S(1)}, f32[72,50]{0,1:T(8,128)}, u32[]{:S(2)}) copy-start(f32[72,50]{0,1:T(8,128)} %param.13) | copy-start | bytes 43204
  1.5 12.1 %collective-permute-start = (f32[144,128]{1,0:T(8,128)S(1)}, f32[144,128]{1,0:T(8,128)S(1)}, u32[]{:S(2)}, u32[]{:S(2)}) collective-permute-start(f32[144,128]{1,0:T(8,128)S(1)} %get-tuple-element.15), channel_id=1, source_target_pairs={{0,8},{8,16},{16,24},{24,32},{32,40},{40,48},{48,56},{56,64},{64,7... | collective-permute-start | bytes 221192 | tf_op jit(solution)/shard_map/ppermute | solution.py:368
  4.0 9.6 %collective-permute-start.1 = (f32[144,128]{1,0:T(8,128)S(1)}, f32[144,128]{1,0:T(8,128)S(1)}, u32[]{:S(2)}, u32[]{:S(2)}) collective-permute-start(f32[144,128]{1,0:T(8,128)S(1)} %get-tuple-element.16), channel_id=1, source_target_pairs={{0,120},{8,0},{16,8},{24,16},{32,24},{40,32},{48,40},{56,48},{64,5... | collective-permute-start | bytes 221192 | tf_op jit(solution)/shard_map/ppermute | solution.py:368
  8.4 5.0 %collective-permute-start.2 = (f32[8,144]{1,0:T(8,128)S(1)}, f32[8,144]{1,0:T(8,128)S(1)}, u32[]{:S(2)}, u32[]{:S(2)}) collective-permute-start(f32[8,144]{1,0:T(8,128)S(1)} %get-tuple-element.17), channel_id=1, source_target_pairs={{0,1},{1,2},{2,3},{3,4},{4,5},{5,6},{6,7},{7,0},{8,9},{9,10},{10,1... | collective-permute-start | bytes 13832 | tf_op jit(solution)/shard_map/ppermute | solution.py:368
  10.5 3.1 %collective-permute-start.3 = (f32[8,144]{1,0:T(8,128)S(1)}, f32[8,144]{1,0:T(8,128)S(1)}, u32[]{:S(2)}, u32[]{:S(2)}) collective-permute-start(f32[8,144]{1,0:T(8,128)S(1)} %get-tuple-element.18), channel_id=1, source_target_pairs={{0,7},{1,0},{2,1},{3,2},{4,3},{5,4},{6,5},{7,6},{8,15},{9,8},{10,9... | collective-permute-start | bytes 13832 | tf_op jit(solution)/shard_map/ppermute | solution.py:368
  60.9 17.6 %all-to-all-start.1 = ((f32[128,1,896]{2,1,0:T(1,128)}), f32[128,1,896]{2,1,0:T(1,128)S(1)}, u32[]{:S(2)}, u32[]{:S(2)}) async-start(f32[128,1,896]{2,1,0:T(1,128)} %bitcast.4), calls=%async_computation.1 | async-start | bytes 917504 | tf_op jit(solution)/shard_map/all_to_all | solution.py:350

commit v7 on v6

--- a/solution.py
+++ b/solution.py
@@ -121,10 +121,11 @@
 
     last = small_ref.shape[0] - SUBL
     line = jnp.broadcast_to(small_ref[last:last + 1, :], (LANES, LANES))
-    c = line.T[:crm_z]
+    pad_z = const_ref.shape[0] // 6
+    c = line.T[:pad_z]
     keep = 1.0 - c
     for i, value in enumerate((BETA * keep, BETA * c, keep, c, 0.5 * keep, 0.5 * c)):
-        const_ref[pl.ds(i, crm_z, stride=SUBL), :] = value
+        const_ref[i * pad_z:(i + 1) * pad_z, :] = value
 
 
 def ends_of(width):
@@ -176,28 +177,51 @@
     dyn_ref[...] = base_ref[...] + DIFFUSION * halo
 
 
-def total(values):
-    while len(values) > 1:
-        values = [a + b for a, b in zip(values[::2], values[1::2])]
-    return values[0]
-
-
-def advect(values, stay, come):
-    moved = [come * v for v in values]
-    last = pltpu.roll(moved[-1], 1, 0)
-    return [stay * v + m for v, m in zip(values, [last] + moved[:-1])]
-
-
-def spread(ref, row):
-    return jnp.broadcast_to(ref[pl.ds(row, 1), :], (SUBL, LANES))
+def substeps(count, load, wrap, coefs, base_t, base_q):
+    beta_keep, beta_c, keep, c, half_keep, half_c = coefs
+    raw = [load(p) for p in range(count)]
+    temper, raw_q = [t for t, _ in raw], [q for _, q in raw]
+    sums = [[None] * count for _ in range(S_MAX)]
+    vapour = [[None] * count for _ in range(S_MAX)]
+    first, kept_sums = None, [None] * S_MAX
+
+    def mixed(values, p, stay, come):
+        before = wrap(values[-1]) if p == 0 else values[p - 1]
+        return stay * values[p] + come * before
+
+    def plus(acc, value):
+        return value if acc is None else acc + value
+
+    for turn in range(count + S_MAX - 1):
+        for k in range(S_MAX):
+            if not k <= turn < count + k:
+                continue
+            p = turn % count
+            if k == 0:
+                t = mixed(temper, p, beta_keep, beta_c) + base_t
+                q = mixed(raw_q, p, beta_keep, beta_c) + base_q
+                s = t + q
+                first = plus(first, q)
+            else:
+                s = mixed(sums[k - 1], p, keep, c)
+                q = mixed(vapour[k - 1], p, half_keep, half_c)
+                t = s - q
+            kept = jnp.minimum(q, jnp.exp2(t))
+            kept_sums[k] = plus(kept_sums[k], kept)
+            if k < S_MAX - 1:
+                sums[k][p] = s
+                vapour[k][p] = q + kept
+    return first, kept_sums
 
 
 def crm_kernel(
     crm_z, crm_x, blocks, const_ref, arrived_ref, field_hbm, out_ref,
-    prof_ref, weight_ref, part_ref, pair_ref, turn_ref, buffers, sems,
+    prof_ref, weight_ref, part_ref, turn_ref, buffers, tails, sems,
 ):
     pad_z = -(-crm_z // SUBL) * SUBL
-    quads = crm_x // SUBL
+    groups, rest = crm_z // SUBL, crm_z % SUBL
+    runs = SUBL // rest if rest else 1
+    short = crm_x // runs
     half = LANES // 2
     block = pl.program_id(0)
     scale = 2.0 * CONDENSE / (BETA * crm_x)
@@ -205,14 +229,30 @@
     def rows_of(index, size):
         return pl.ds(pl.multiple_of(index * size, SUBL), size)
 
+    starts = [sum(FETCHED[:i]) for i in range(len(FETCHED))]
+
+    def refs_of(i):
+        lanes = pl.ds(starts[i] * LANES, FETCHED[i] * LANES)
+        own = pl.ds(starts[i], FETCHED[i])
+        return buffers.at[:, :, :, lanes], tails.at[own]
+
     def fetch(i):
-        lanes = pl.ds(pl.multiple_of(i * LANES, LANES), LANES)
-        side = lax.rem(i, 2)
-        return pltpu.make_async_copy(field_hbm.at[:, lanes], buffers.at[side], sems.at[side])
+        lanes = pl.ds(starts[i] * LANES, FETCHED[i] * LANES)
+        copies = []
+        for v in range(2):
+            full = field_hbm.at[v, pl.ds(0, groups * SUBL)].reshape(groups, SUBL, crm_x, field_hbm.shape[-1])
+            for sub in range(SUBL):
+                target = buffers.at[pl.ds(v * groups, groups), :, sub, lanes]
+                copies.append(pltpu.make_async_copy(full.at[:, sub, :, lanes], target, sems.at[i]))
+        for b in range(starts[i], starts[i] + FETCHED[i]):
+            source = field_hbm.at[:, pl.ds(groups * SUBL, rest), :, pl.ds(b * LANES, LANES)]
+            copies.append(pltpu.make_async_copy(source, tails.at[b], sems.at[i]))
+        for copy in copies:
+            copy.start()
 
     @pl.when(block == 0)
     def _():
-        fetch(block).start()
+        fetch(0)
 
         def unpack(i, carry):
             cols = arrived_ref[rows_of(i, LANES), :].T
@@ -228,47 +268,67 @@
 
         lax.fori_loop(0, blocks, unpack, 0, unroll=True)
 
-    @pl.when(block + 1 < blocks)
-    def _():
-        fetch(block + 1).start()
-
-    fetch(block).wait()
-    field_ref = buffers.at[lax.rem(block, 2)]
+    for i, start in enumerate(starts):
+        @pl.when(block == start)
+        def _(i=i):
+            if i + 1 < len(FETCHED):
+                fetch(i + 1)
+            for ref in refs_of(i):
+                pltpu.make_async_copy(ref, ref, sems.at[i]).wait()
+
+    own_lanes = pl.ds(pl.multiple_of(block * LANES, LANES), LANES)
+
+    def spread(ref, row):
+        return jnp.broadcast_to(ref[pl.ds(row, 1), :], (SUBL, LANES))
+
     w_first, *w_kept = [spread(weight_ref, SUBL * block + i) for i in range(S_MAX + 1)]
-    for z in range(crm_z):
-        beta_keep, beta_c, keep, c, half_keep, half_c = [spread(const_ref, SUBL * z + i) for i in range(6)]
-        base_t = spread(prof_ref, 2 * pad_z * block + z)
-        base_q = spread(prof_ref, 2 * pad_z * block + pad_z + z)
-        temper = [field_ref[pl.ds(z * crm_x + i, SUBL, stride=quads), :] for i in range(quads)]
-        vapour = [field_ref[pl.ds((crm_z + z) * crm_x + i, SUBL, stride=quads), :] for i in range(quads)]
-        temper = [t + base_t for t in advect(temper, beta_keep, beta_c)]
-        vapour = [v + base_q for v in advect(vapour, beta_keep, beta_c)]
-        sums = [t + v for t, v in zip(temper, vapour)]
-        gone = w_first * total(vapour)
-        for k in range(S_MAX):
-            if k > 0:
-                sums = advect(sums, keep, c)
-                vapour = advect(vapour, half_keep, half_c)
-                temper = [s - v for s, v in zip(sums, vapour)]
-            kept = [jnp.minimum(v, jnp.exp2(t)) for t, v in zip(temper, vapour)]
-            gone = gone + w_kept[k] * total(kept)
-            if k < S_MAX - 1:
-                vapour = [v + e for v, e in zip(vapour, kept)]
-        part_ref[pl.ds(pl.multiple_of(SUBL * (pad_z * block + z), SUBL), SUBL), :] = gone
+
+    def change_of(first, kept_sums):
+        gone = w_first * first
+        for w, kept in zip(w_kept, kept_sums):
+            gone = gone + w * kept
+        return gone
+
+    sub = lax.broadcasted_iota(jnp.int32, (SUBL, LANES), 0)
+    for g in range(groups):
+        coefs = [const_ref[i * pad_z + SUBL * g:i * pad_z + SUBL * (g + 1), :] for i in range(6)]
+        base_t = prof_ref[rows_of(2 * block * (pad_z // SUBL) + g, SUBL), :]
+        base_q = prof_ref[rows_of((2 * block + 1) * (pad_z // SUBL) + g, SUBL), :]
+        result = substeps(
+            crm_x,
+            lambda p: (buffers[g, p, :, own_lanes], buffers[groups + g, p, :, own_lanes]),
+            lambda v: v, coefs, base_t, base_q,
+        )
+        part_ref[rows_of(block * (pad_z // SUBL) + g, SUBL), :] = change_of(*result)
+    if rest:
+        def runs_of(ref, row):
+            value = spread(ref, row)
+            for z in range(1, rest):
+                value = jnp.where(sub >= z * runs, spread(ref, row + z), value)
+            return value
+
+        def wrap(value):
+            around = pltpu.roll(value, (1 - runs) % SUBL, 0)
+            return jnp.where(sub % runs == 0, around, pltpu.roll(value, 1, 0))
+
+        tail = tails.at[block].reshape(2, rest * crm_x, LANES)
+        z = SUBL * groups
+        coefs = [runs_of(const_ref, i * pad_z + z) for i in range(6)]
+        base_t = runs_of(prof_ref, 2 * block * pad_z + z)
+        base_q = runs_of(prof_ref, (2 * block + 1) * pad_z + z)
+        result = substeps(short, lambda p: tuple(tail[v, pl.ds(p, SUBL, stride=short), :] for v in range(2)), wrap, coefs, base_t, base_q)
+        gone = change_of(*result)
+        lines = [jnp.sum(gone[i * runs:(i + 1) * runs], axis=0, keepdims=True) for i in range(rest)]
+        lines.append(jnp.zeros((SUBL - rest, LANES), jnp.float32))
+        part_ref[rows_of(block * (pad_z // SUBL) + groups, SUBL), :] = jnp.concatenate(lines, axis=0)
 
     @pl.when(block == blocks - 1)
     def _():
         lane = lax.broadcasted_iota(jnp.int32, (half, LANES), 1)
-        level = lax.broadcasted_iota(jnp.int32, (half, LANES), 0)
 
         def pack(i, carry):
-            start = i * (SUBL * pad_z)
-            pairs = [part_ref[pl.ds(start + j, 2 * pad_z, stride=4), :] for j in range(4)]
-            at = i * 2 * pad_z
-            pair_ref[pl.ds(at, 2 * pad_z), :] = (pairs[0] + pairs[1]) + (pairs[2] + pairs[3])
-            change = pair_ref[pl.ds(at, pad_z, stride=2), :] + pair_ref[pl.ds(at + 1, pad_z, stride=2), :]
+            change = part_ref[rows_of(i, pad_z), :]
             change = jnp.concatenate([change, jnp.zeros((half - pad_z, LANES), jnp.float32)], axis=0)
-            change = jnp.where(level < crm_z, change, 0.0)
             turn_ref[rows_of(i, LANES), :] = jnp.concatenate([change, change], axis=0).T
             even = turn_ref[pl.ds(i * LANES, half, stride=2), :]
             odd = turn_ref[pl.ds(i * LANES + 1, half, stride=2), :]
@@ -306,6 +366,7 @@
 
 VMEM = pl.BlockSpec(memory_space=pltpu.VMEM)
 DEVICES = 128
+FETCHED = (1, 3, 5, 5)
 
 
 def params(limit_mib=16):
@@ -322,7 +383,6 @@
 
 def crm(const, arrived, crm_field, crm_z, crm_x):
     slots = arrived.shape[0]
-    rows = crm_field.shape[0]
     blocks = slots // LANES
     pad_z = -(-crm_z // SUBL) * SUBL
     return pl.pallas_call(
@@ -334,15 +394,15 @@
         scratch_shapes=[
             pltpu.VMEM((blocks * 2 * pad_z, LANES), jnp.float32),
             pltpu.VMEM((blocks * SUBL, LANES), jnp.float32),
-            pltpu.VMEM((blocks * SUBL * pad_z, LANES), jnp.float32),
-            pltpu.VMEM((blocks * 2 * pad_z, LANES), jnp.float32),
+            pltpu.VMEM((blocks * pad_z, LANES), jnp.float32),
             pltpu.VMEM((slots, LANES), jnp.float32),
-            pltpu.VMEM((2, rows, LANES), jnp.float32),
-            pltpu.SemaphoreType.DMA((2,)),
+            pltpu.VMEM((2 * (crm_z // SUBL), crm_x, SUBL, slots), jnp.float32),
+            pltpu.VMEM((blocks, 2, crm_z % SUBL, crm_x, LANES), jnp.float32),
+            pltpu.SemaphoreType.DMA((len(FETCHED),)),
         ],
         compiler_params=params(48),
         name="crm",
-    )(const, arrived, crm_field)
+    )(const, arrived, crm_field.reshape(2, crm_z, crm_x, slots))
 
 
 def exchange(value, devices):
@@ -402,7 +462,7 @@
             i32(1, col_dev),
             f32(slots, LANES),
             jax.ShapeDtypeStruct((slots, 3 * LANES), jnp.bfloat16),
-            f32(SUBL * crm_z, LANES),
+            f32(6 * (-(-crm_z // SUBL) * SUBL), LANES),
         ],
         compiler_params=params(),
         cost_estimate=pl.CostEstimate(flops=10**9, bytes_accessed=4 * 10**6, transcendentals=0),

time: 80.8 us -> 79.5 us (0.984)
  Pallas kernels: 27.4 us -> 26.4 us
    pallas_call x1, Pallas kernels: 21.9 us -> 20.9 us  [crm(): pl.pallas_call(functools.partial(crm_kernel, crm_z, crm_x, blocks), grid=...]
where the time goes in v7:
time: 79.5 us; the launch traced here: 79.2 us
  Pallas kernels  26.4 us (33%)
  blocking collectives  24.4 us (31%)
  starting transfers between devices  13.7 us (17%)
  waiting for transfers between devices  12.6 us (16%)
  local copies, waits for them, and re-layouts  1.15 us (1%)
  other arithmetic  0.83 us (1%)
    all_to_all x1, blocking collectives, exchange(): lax.all_to_all(sent, ('gx', 'gy'), split_axis=0, concat_axis=0, tiled=True)  24.4 us
    pallas_call x1, Pallas kernels, crm(): pl.pallas_call(functools.partial(crm_kernel, crm_z, crm_x, blocks), grid=...  20.9 us
    all_to_all x1, waiting for transfers between devices, exchange(): lax.all_to_all(sent, ('gx', 'gy'), split_axis=0, concat_axis=0, tiled=True)  12.4 us
    ppermute x4, starting transfers between devices, shifted(): lax.ppermute(value, axis, [(i, (i + step) % count) for i in range(count)])  9.02 us
    all_to_all x1, starting transfers between devices, exchange(): lax.all_to_all(sent, ('gx', 'gy'), split_axis=0, concat_axis=0, tiled=True)  4.69 us
    pallas_call x1, Pallas kernels, body(): pl.pallas_call(functools.partial(local_kernel, cap, crm_z), in_specs=[VME...  2.02 us
    pallas_call x1, Pallas kernels, body(): pl.pallas_call(final_kernel, in_specs=[VMEM] * 4, out_specs=pl.BlockSpec(...  1.73 us
  transfers between devices with their start and end apart: 5, of which 2 were waited for; matrix products, arithmetic and copies ran while one was open for 1% of the time, Pallas kernels for 3%

profile of v7, /device:TPU:1, one launch (start us, length us, event | category | flops | bytes accessed | tf_op | source)
XLA Modules:
  0.0 79.2 jit_solution(14394698273715544838)
XLA Ops:
  0.0 0.0 copy-start
  0.0 1.1 %copy-done = f32[144,8,128]{2,1,0:T(8,128)S(1)} copy-done((f32[144,8,128]{2,1,0:T(8,128)S(1)}, f32[144,8,128]{2,1,0:T(8,128)}, u32[]{:S(2)}) %copy-start) | copy-done | bytes 589848
  1.1 0.0 copy-start.1
  1.1 0.4 edges.1
  1.5 2.5 %collective-permute-start = (f32[144,128]{1,0:T(8,128)S(1)}, f32[144,128]{1,0:T(8,128)S(1)}, u32[]{:S(2)}, u32[]{:S(2)}) collective-permute-start(f32[144,128]{1,0:T(8,128)S(1)} %get-tuple-element.15), channel_id=1, source_target_pairs={{0,8},{8,16},{16,24},{24,32},{32,40},{40,48},{48,56},{56,64},{64,7... | collective-permute-start | bytes 221192 | tf_op jit(solution)/shard_map/ppermute | solution.py:428
  4.0 4.4 %collective-permute-start.1 = (f32[144,128]{1,0:T(8,128)S(1)}, f32[144,128]{1,0:T(8,128)S(1)}, u32[]{:S(2)}, u32[]{:S(2)}) collective-permute-start(f32[144,128]{1,0:T(8,128)S(1)} %get-tuple-element.16), channel_id=1, source_target_pairs={{0,120},{8,0},{16,8},{24,16},{32,24},{40,32},{48,40},{56,48},{64,5... | collective-permute-start | bytes 221192 | tf_op jit(solution)/shard_map/ppermute | solution.py:428
  8.4 2.1 %collective-permute-start.2 = (f32[8,144]{1,0:T(8,128)S(1)}, f32[8,144]{1,0:T(8,128)S(1)}, u32[]{:S(2)}, u32[]{:S(2)}) collective-permute-start(f32[8,144]{1,0:T(8,128)S(1)} %get-tuple-element.17), channel_id=1, source_target_pairs={{0,1},{1,2},{2,3},{3,4},{4,5},{5,6},{6,7},{7,0},{8,9},{9,10},{10,1... | collective-permute-start | bytes 13832 | tf_op jit(solution)/shard_map/ppermute | solution.py:428
  10.5 0.0 collective-permute-start.3
  10.5 0.8 %add_add_fusion.small_ref = f32[152,128]{1,0:T(8,128)S(1)} fusion(f32[1,50]{1,0:T(1,128)} %bitcast.14, f32[50,72]{1,0:T(8,128)} %param.12, f32[72,72]{1,0:T(8,128)} %param.11, s32[8,128]{1,0:T(8,128)} %param.10, s32[8,128]{1,0:T(8,128)} %param.9), kind=kLoop, calls=%fused_computation | loop fusion | flops 97280 | bytes 121352 | tf_op jit(solution)/shard_map/add | solution.py:423
  11.3 2.0 %local.1 = (f32[144,1024]{1,0:T(8,128)S(1)}, s32[1,1024]{1,0:T(1,128)S(1)}, f32[1792,128]{1,0:T(8,128)S(1)}, bf16[1792,384]{1,0:T(8,128)(2,1)S(1)}, f32[336,128]{1,0:T(8,128)S(1)}) custom-call(f32[1152,128]{1,0:T(8,128)S(1)} %bitcast.12, f32[152,128]{1,0:T(8,128)S(1)} %add_add_fusion.small_ref), custom_call_target="tpu_custom_call" | custom-call | flops 1000000000 | bytes 4000000 | tf_op jit(solution)/shard_map/local/pallas_call | solution.py:456
  13.4 0.0 collective-permute-done.2.left_ref
  13.4 0.2 collective-permute-done.3.right_ref
  13.6 0.0 collective-permute-done.above_ref
  13.6 0.0 collective-permute-done.1.below_ref
  13.6 1.0 %send.1 = f32[1792,128]{1,0:T(8,128)S(1)} custom-call(f32[152,128]{1,0:T(8,128)S(1)} %add_add_fusion.small_ref, f32[1792,128]{1,0:T(8,128)S(1)} %get-tuple-element.20.sent_ref, bf16[1792,384]{1,0:T(8,128)(2,1)S(1)} %get-tuple-element.21.edge_ref, f32[144,128]{1,0:T(8,128)S(1)} %collective-permute-done.above_ref, ...), custom_call_target="tpu_custom_call" | custom-call | tf_op jit(solution)/shard_map/send/pallas_call | solution.py:472
  14.5 24.4 %all_to_all.10 = f32[128,1,1792]{2,1,0:T(1,128)S(1)} all-to-all(f32[128,1,1792]{2,1,0:T(1,128)S(1)} %bitcast.8), channel_id=1, replica_groups=mesh['gx'=16,'gy'=8] {'gx','gy'}, dimensions={0} | all-to-all | bytes 1835008 | tf_op jit(solution)/shard_map/all_to_all | solution.py:410
  39.0 20.9 %crm.1 = f32[896,128]{1,0:T(8,128)} custom-call(f32[336,128]{1,0:T(8,128)S(1)} %get-tuple-element.19.const_ref, f32[1792,128]{1,0:T(8,128)S(1)} %bitcast.9, f32[2,50,32,1792]{3,2,1,0:T(8,128)} %bitcast.13), custom_call_target="tpu_custom_call" | custom-call | tf_op jit(solution)/shard_map/crm/pallas_call | solution.py:388
  59.9 4.7 %all-to-all-start.1 = ((f32[128,1,896]{2,1,0:T(1,128)}), f32[128,1,896]{2,1,0:T(1,128)S(1)}, u32[]{:S(2)}, u32[]{:S(2)}) async-start(f32[128,1,896]{2,1,0:T(1,128)} %bitcast.5), calls=%async_computation.1 | async-start | bytes 917504 | tf_op jit(solution)/shard_map/all_to_all | solution.py:410
  64.6 0.0 copy-done.1
  64.6 0.1 copy.12.up_ref
  64.7 0.3 halo.1.dyn_ref
  65.0 12.4 %all-to-all-done.1 = f32[128,1,896]{2,1,0:T(1,128)S(1)} async-done(((f32[128,1,896]{2,1,0:T(1,128)}), f32[128,1,896]{2,1,0:T(1,128)S(1)}, u32[]{:S(2)}, u32[]{:S(2)}) %all-to-all-start.1) | async-done | bytes 458784 | tf_op jit(solution)/shard_map/all_to_all | solution.py:410
  77.4 1.7 %final.1 = f32[1152,128]{1,0:T(8,128)} custom-call(f32[144,1024]{1,0:T(8,128)S(1)} %halo.1.dyn_ref, f32[896,128]{1,0:T(8,128)S(1)} %bitcast.10, s32[1,1024]{1,0:T(1,128)S(1)} %get-tuple-element.22.slot_ref, f32[72,50]{1,0:T(8,128)S(1)} %copy.12.up_ref), custom_call_target="tpu_custom_call" | custom-call | tf_op jit(solution)/shard_map/final/pallas_call | solution.py:494
Async XLA Ops:
  0.0 1.1 %copy-start = (f32[144,8,128]{2,1,0:T(8,128)S(1)}, f32[144,8,128]{2,1,0:T(8,128)}, u32[]{:S(2)}) copy-start(f32[144,8,128]{2,1,0:T(8,128)} %param.8) | copy-start | bytes 1769476
  1.1 63.5 %copy-start.1 = (f32[72,50]{0,1:T(8,128)S(1)}, f32[72,50]{0,1:T(8,128)}, u32[]{:S(2)}) copy-start(f32[72,50]{0,1:T(8,128)} %param.13) | copy-start | bytes 43204
  1.5 12.1 %collective-permute-start = (f32[144,128]{1,0:T(8,128)S(1)}, f32[144,128]{1,0:T(8,128)S(1)}, u32[]{:S(2)}, u32[]{:S(2)}) collective-permute-start(f32[144,128]{1,0:T(8,128)S(1)} %get-tuple-element.15), channel_id=1, source_target_pairs={{0,8},{8,16},{16,24},{24,32},{32,40},{40,48},{48,56},{56,64},{64,7... | collective-permute-start | bytes 221192 | tf_op jit(solution)/shard_map/ppermute | solution.py:428
  4.0 9.6 %collective-permute-start.1 = (f32[144,128]{1,0:T(8,128)S(1)}, f32[144,128]{1,0:T(8,128)S(1)}, u32[]{:S(2)}, u32[]{:S(2)}) collective-permute-start(f32[144,128]{1,0:T(8,128)S(1)} %get-tuple-element.16), channel_id=1, source_target_pairs={{0,120},{8,0},{16,8},{24,16},{32,24},{40,32},{48,40},{56,48},{64,5... | collective-permute-start | bytes 221192 | tf_op jit(solution)/shard_map/ppermute | solution.py:428
  8.4 5.0 %collective-permute-start.2 = (f32[8,144]{1,0:T(8,128)S(1)}, f32[8,144]{1,0:T(8,128)S(1)}, u32[]{:S(2)}, u32[]{:S(2)}) collective-permute-start(f32[8,144]{1,0:T(8,128)S(1)} %get-tuple-element.17), channel_id=1, source_target_pairs={{0,1},{1,2},{2,3},{3,4},{4,5},{5,6},{6,7},{7,0},{8,9},{9,10},{10,1... | collective-permute-start | bytes 13832 | tf_op jit(solution)/shard_map/ppermute | solution.py:428
  10.5 3.1 %collective-permute-start.3 = (f32[8,144]{1,0:T(8,128)S(1)}, f32[8,144]{1,0:T(8,128)S(1)}, u32[]{:S(2)}, u32[]{:S(2)}) collective-permute-start(f32[8,144]{1,0:T(8,128)S(1)} %get-tuple-element.18), channel_id=1, source_target_pairs={{0,7},{1,0},{2,1},{3,2},{4,3},{5,4},{6,5},{7,6},{8,15},{9,8},{10,9... | collective-permute-start | bytes 13832 | tf_op jit(solution)/shard_map/ppermute | solution.py:428
  59.9 17.6 %all-to-all-start.1 = ((f32[128,1,896]{2,1,0:T(1,128)}), f32[128,1,896]{2,1,0:T(1,128)S(1)}, u32[]{:S(2)}, u32[]{:S(2)}) async-start(f32[128,1,896]{2,1,0:T(1,128)} %bitcast.5), calls=%async_computation.1 | async-start | bytes 917504 | tf_op jit(solution)/shard_map/all_to_all | solution.py:410

commit v8 on v7

--- a/solution.py
+++ b/solution.py
@@ -156,12 +156,19 @@
     same = (row == lane).astype(jnp.bfloat16)
     s_hi, s_lo = split(sides)
     ends = dot(s_hi, same, TN) + dot(s_lo, same, TN)
-    halo = DIFFUSION * jnp.concatenate([above_ref[...], below_ref[...], ends], axis=1)
-    both = payload(down_of(small_ref, crm_z, half), halo[:half], halo[half:], jnp.zeros((SUBL, halo.shape[1]), jnp.float32))
+    down = down_of(small_ref, crm_z, half)
+
+    def packed(halo):
+        halo = DIFFUSION * halo
+        return payload(down, halo[:half], halo[half:], jnp.zeros((SUBL, halo.shape[1]), jnp.float32))
+
+    lines = packed(jnp.concatenate([above_ref[...], below_ref[...]], axis=1))
+    ends = packed(ends)
+    split_at = 2 * LANES
     chunk = out_ref.shape[0] // 2
     for start in range(0, out_ref.shape[0], chunk):
         rows = slice(start, start + chunk)
-        sent = dot(edge_ref[rows, :], both, NT)
+        sent = dot(edge_ref[rows, :split_at], lines, NT) + dot(edge_ref[rows, split_at:], ends, NT)
         out_ref[rows, :] = sent_ref[rows, :] + (sent[:, :LANES] + sent[:, LANES:])
 
 

time: 79.5 us -> 79.5 us (level)
  no operation moved by 1% of the time
where the time goes in v8:
time: 79.5 us; the launch traced here: 79.2 us
  Pallas kernels  26.5 us (33%)
  blocking collectives  24.4 us (31%)
  starting transfers between devices  13.7 us (17%)
  waiting for transfers between devices  12.6 us (16%)
  local copies, waits for them, and re-layouts  1.15 us (1%)
  other arithmetic  0.83 us (1%)
    all_to_all x1, blocking collectives, exchange(): lax.all_to_all(sent, ('gx', 'gy'), split_axis=0, concat_axis=0, tiled=True)  24.4 us
    pallas_call x1, Pallas kernels, crm(): pl.pallas_call(functools.partial(crm_kernel, crm_z, crm_x, blocks), grid=...  20.9 us
    all_to_all x1, waiting for transfers between devices, exchange(): lax.all_to_all(sent, ('gx', 'gy'), split_axis=0, concat_axis=0, tiled=True)  12.4 us
    ppermute x4, starting transfers between devices, shifted(): lax.ppermute(value, axis, [(i, (i + step) % count) for i in range(count)])  9.02 us
    all_to_all x1, starting transfers between devices, exchange(): lax.all_to_all(sent, ('gx', 'gy'), split_axis=0, concat_axis=0, tiled=True)  4.69 us
    pallas_call x1, Pallas kernels, body(): pl.pallas_call(functools.partial(local_kernel, cap, crm_z), in_specs=[VME...  2.02 us
    pallas_call x1, Pallas kernels, body(): pl.pallas_call(final_kernel, in_specs=[VMEM] * 4, out_specs=pl.BlockSpec(...  1.73 us
  transfers between devices with their start and end apart: 5, of which 2 were waited for; matrix products, arithmetic and copies ran while one was open for 1% of the time, Pallas kernels for 3%

profile of v8, /device:TPU:1, one launch (start us, length us, event | category | flops | bytes accessed | tf_op | source)
XLA Modules:
  0.0 79.2 jit_solution(6049401427137991957)
XLA Ops:
  0.0 0.0 copy-start
  0.0 1.1 %copy-done = f32[144,8,128]{2,1,0:T(8,128)S(1)} copy-done((f32[144,8,128]{2,1,0:T(8,128)S(1)}, f32[144,8,128]{2,1,0:T(8,128)}, u32[]{:S(2)}) %copy-start) | copy-done | bytes 589848
  1.1 0.0 copy-start.1
  1.1 0.4 edges.1
  1.5 2.5 %collective-permute-start = (f32[144,128]{1,0:T(8,128)S(1)}, f32[144,128]{1,0:T(8,128)S(1)}, u32[]{:S(2)}, u32[]{:S(2)}) collective-permute-start(f32[144,128]{1,0:T(8,128)S(1)} %get-tuple-element.15), channel_id=1, source_target_pairs={{0,8},{8,16},{16,24},{24,32},{32,40},{40,48},{48,56},{56,64},{64,7... | collective-permute-start | bytes 221192 | tf_op jit(solution)/shard_map/ppermute | solution.py:435
  4.0 4.4 %collective-permute-start.1 = (f32[144,128]{1,0:T(8,128)S(1)}, f32[144,128]{1,0:T(8,128)S(1)}, u32[]{:S(2)}, u32[]{:S(2)}) collective-permute-start(f32[144,128]{1,0:T(8,128)S(1)} %get-tuple-element.16), channel_id=1, source_target_pairs={{0,120},{8,0},{16,8},{24,16},{32,24},{40,32},{48,40},{56,48},{64,5... | collective-permute-start | bytes 221192 | tf_op jit(solution)/shard_map/ppermute | solution.py:435
  8.4 2.1 %collective-permute-start.2 = (f32[8,144]{1,0:T(8,128)S(1)}, f32[8,144]{1,0:T(8,128)S(1)}, u32[]{:S(2)}, u32[]{:S(2)}) collective-permute-start(f32[8,144]{1,0:T(8,128)S(1)} %get-tuple-element.17), channel_id=1, source_target_pairs={{0,1},{1,2},{2,3},{3,4},{4,5},{5,6},{6,7},{7,0},{8,9},{9,10},{10,1... | collective-permute-start | bytes 13832 | tf_op jit(solution)/shard_map/ppermute | solution.py:435
  10.5 0.0 collective-permute-start.3
  10.5 0.8 %add_add_fusion.small_ref = f32[152,128]{1,0:T(8,128)S(1)} fusion(f32[1,50]{1,0:T(1,128)} %bitcast.14, f32[50,72]{1,0:T(8,128)} %param.12, f32[72,72]{1,0:T(8,128)} %param.11, s32[8,128]{1,0:T(8,128)} %param.10, s32[8,128]{1,0:T(8,128)} %param.9), kind=kLoop, calls=%fused_computation | loop fusion | flops 97280 | bytes 121352 | tf_op jit(solution)/shard_map/add | solution.py:430
  11.3 2.0 %local.1 = (f32[144,1024]{1,0:T(8,128)S(1)}, s32[1,1024]{1,0:T(1,128)S(1)}, f32[1792,128]{1,0:T(8,128)S(1)}, bf16[1792,384]{1,0:T(8,128)(2,1)S(1)}, f32[336,128]{1,0:T(8,128)S(1)}) custom-call(f32[1152,128]{1,0:T(8,128)S(1)} %bitcast.12, f32[152,128]{1,0:T(8,128)S(1)} %add_add_fusion.small_ref), custom_call_target="tpu_custom_call" | custom-call | flops 1000000000 | bytes 4000000 | tf_op jit(solution)/shard_map/local/pallas_call | solution.py:463
  13.4 0.0 collective-permute-done.2.left_ref
  13.4 0.2 collective-permute-done.3.right_ref
  13.6 0.0 collective-permute-done.above_ref
  13.6 0.0 collective-permute-done.1.below_ref
  13.6 1.0 %send.1 = f32[1792,128]{1,0:T(8,128)S(1)} custom-call(f32[152,128]{1,0:T(8,128)S(1)} %add_add_fusion.small_ref, f32[1792,128]{1,0:T(8,128)S(1)} %get-tuple-element.20.sent_ref, bf16[1792,384]{1,0:T(8,128)(2,1)S(1)} %get-tuple-element.21.edge_ref, f32[144,128]{1,0:T(8,128)S(1)} %collective-permute-done.above_ref, ...), custom_call_target="tpu_custom_call" | custom-call | tf_op jit(solution)/shard_map/send/pallas_call | solution.py:479
  14.6 24.4 %all_to_all.10 = f32[128,1,1792]{2,1,0:T(1,128)S(1)} all-to-all(f32[128,1,1792]{2,1,0:T(1,128)S(1)} %bitcast.8), channel_id=1, replica_groups=mesh['gx'=16,'gy'=8] {'gx','gy'}, dimensions={0} | all-to-all | bytes 1835008 | tf_op jit(solution)/shard_map/all_to_all | solution.py:417
  39.0 20.9 %crm.1 = f32[896,128]{1,0:T(8,128)} custom-call(f32[336,128]{1,0:T(8,128)S(1)} %get-tuple-element.19.const_ref, f32[1792,128]{1,0:T(8,128)S(1)} %bitcast.9, f32[2,50,32,1792]{3,2,1,0:T(8,128)} %bitcast.13), custom_call_target="tpu_custom_call" | custom-call | tf_op jit(solution)/shard_map/crm/pallas_call | solution.py:395
  60.0 4.7 %all-to-all-start.1 = ((f32[128,1,896]{2,1,0:T(1,128)}), f32[128,1,896]{2,1,0:T(1,128)S(1)}, u32[]{:S(2)}, u32[]{:S(2)}) async-start(f32[128,1,896]{2,1,0:T(1,128)} %bitcast.5), calls=%async_computation.1 | async-start | bytes 917504 | tf_op jit(solution)/shard_map/all_to_all | solution.py:417
  64.7 0.0 copy-done.1
  64.7 0.1 copy.12.up_ref
  64.8 0.3 halo.1.dyn_ref
  65.1 12.4 %all-to-all-done.1 = f32[128,1,896]{2,1,0:T(1,128)S(1)} async-done(((f32[128,1,896]{2,1,0:T(1,128)}), f32[128,1,896]{2,1,0:T(1,128)S(1)}, u32[]{:S(2)}, u32[]{:S(2)}) %all-to-all-start.1) | async-done | bytes 458784 | tf_op jit(solution)/shard_map/all_to_all | solution.py:417
  77.5 1.7 %final.1 = f32[1152,128]{1,0:T(8,128)} custom-call(f32[144,1024]{1,0:T(8,128)S(1)} %halo.1.dyn_ref, f32[896,128]{1,0:T(8,128)S(1)} %bitcast.10, s32[1,1024]{1,0:T(1,128)S(1)} %get-tuple-element.22.slot_ref, f32[72,50]{1,0:T(8,128)S(1)} %copy.12.up_ref), custom_call_target="tpu_custom_call" | custom-call | tf_op jit(solution)/shard_map/final/pallas_call | solution.py:501
Async XLA Ops:
  0.0 1.1 %copy-start = (f32[144,8,128]{2,1,0:T(8,128)S(1)}, f32[144,8,128]{2,1,0:T(8,128)}, u32[]{:S(2)}) copy-start(f32[144,8,128]{2,1,0:T(8,128)} %param.8) | copy-start | bytes 1769476
  1.1 63.6 %copy-start.1 = (f32[72,50]{0,1:T(8,128)S(1)}, f32[72,50]{0,1:T(8,128)}, u32[]{:S(2)}) copy-start(f32[72,50]{0,1:T(8,128)} %param.13) | copy-start | bytes 43204
  1.5 12.1 %collective-permute-start = (f32[144,128]{1,0:T(8,128)S(1)}, f32[144,128]{1,0:T(8,128)S(1)}, u32[]{:S(2)}, u32[]{:S(2)}) collective-permute-start(f32[144,128]{1,0:T(8,128)S(1)} %get-tuple-element.15), channel_id=1, source_target_pairs={{0,8},{8,16},{16,24},{24,32},{32,40},{40,48},{48,56},{56,64},{64,7... | collective-permute-start | bytes 221192 | tf_op jit(solution)/shard_map/ppermute | solution.py:435
  4.0 9.6 %collective-permute-start.1 = (f32[144,128]{1,0:T(8,128)S(1)}, f32[144,128]{1,0:T(8,128)S(1)}, u32[]{:S(2)}, u32[]{:S(2)}) collective-permute-start(f32[144,128]{1,0:T(8,128)S(1)} %get-tuple-element.16), channel_id=1, source_target_pairs={{0,120},{8,0},{16,8},{24,16},{32,24},{40,32},{48,40},{56,48},{64,5... | collective-permute-start | bytes 221192 | tf_op jit(solution)/shard_map/ppermute | solution.py:435
  8.4 5.0 %collective-permute-start.2 = (f32[8,144]{1,0:T(8,128)S(1)}, f32[8,144]{1,0:T(8,128)S(1)}, u32[]{:S(2)}, u32[]{:S(2)}) collective-permute-start(f32[8,144]{1,0:T(8,128)S(1)} %get-tuple-element.17), channel_id=1, source_target_pairs={{0,1},{1,2},{2,3},{3,4},{4,5},{5,6},{6,7},{7,0},{8,9},{9,10},{10,1... | collective-permute-start | bytes 13832 | tf_op jit(solution)/shard_map/ppermute | solution.py:435
  10.5 3.1 %collective-permute-start.3 = (f32[8,144]{1,0:T(8,128)S(1)}, f32[8,144]{1,0:T(8,128)S(1)}, u32[]{:S(2)}, u32[]{:S(2)}) collective-permute-start(f32[8,144]{1,0:T(8,128)S(1)} %get-tuple-element.18), channel_id=1, source_target_pairs={{0,7},{1,0},{2,1},{3,2},{4,3},{5,4},{6,5},{7,6},{8,15},{9,8},{10,9... | collective-permute-start | bytes 13832 | tf_op jit(solution)/shard_map/ppermute | solution.py:435
  60.0 17.6 %all-to-all-start.1 = ((f32[128,1,896]{2,1,0:T(1,128)}), f32[128,1,896]{2,1,0:T(1,128)S(1)}, u32[]{:S(2)}, u32[]{:S(2)}) async-start(f32[128,1,896]{2,1,0:T(1,128)} %bitcast.5), calls=%async_computation.1 | async-start | bytes 917504 | tf_op jit(solution)/shard_map/all_to_all | solution.py:417
